TPU v7x, 256 devices: a whole 4x4x8 slice. The times are simulated.
256 devices in a mesh: gx: 4 (over x), gy: 4 (over z_hi, core), gz: 16 (over y, z_lo).
Axes of the slice: x: 4, y: 4, z: 8 (z_hi: 2, z_lo: 4; z = z_hi * 4 + z_lo), core: 2. Of those that a mesh axis runs over, the one named last changes fastest.
Arguments:
- adjoint: float32 [5, 16, 128, 4096], P(None, 'gx', 'gy', 'gz'), may hold values from -6 to 6
- viscosity: float32 [16, 128, 4096], P('gx', 'gy', 'gz'), may hold values from 0.5 to 2
- flux_jacobian: float32 [5, 5], replicated, may hold values from -4 to 4
- face_cell: int32 [262144], P(('gx', 'gy', 'gz')), may hold values from 0 to 32767
- face_patch: int32 [262144, 1], P(('gx', 'gy', 'gz')), may hold values from 0 to 15; in each aligned block of 1024 rows (0 to 1023, 1024 to 2047, ...) at most 128 rows name the same one
- wall_inverse: float32 [256, 128, 128], P(('gx', 'gy', 'gz')), may hold values from -1.2 to 1.2
- lift_matrix: float32 [128, 6], replicated, may hold values from -2.5 to 2.5
- readout: float32 [5, 128], replicated, may hold values from -0.5 to 0.5
Outputs:
- updated: float32 [5, 16, 128, 4096], P(None, 'gx', 'gy', 'gz')
- wall_shear: float32 [5, 262144], P(None, ('gx', 'gy', 'gz'))
Inputs may be any that keep to these rules, and one draw needn't show every extreme that they name: face_cell numbers a cell inside the block of the face's own device. `face_patch`: A patch number p of a face belongs to the device with gz index p // 1 in the face's own (gx, gy) column. Among the 1024 faces of one device at most 128 name one patch, and in every draw some patch is named by exactly 128 faces of some device.
All inputs are finite; a program needn't handle non-finite values.
Results may differ from a plain program's by a relative error of at most 0.0003.
Values sent between devices are 32-bit elements; how exact they have to be, the bound alone decides.
No kernel may reach another device: no remote copies, remote signals or barrier semaphores. Data moves between devices by JAX's collectives and lax.ppermute only.
A program may use at most 64 MiB of HBM per device.

v0:
```python
import jax
import jax.numpy as jnp
from jax import lax
from jax.sharding import PartitionSpec as P

CX = 4
CY = 32
CZ = 256
FACE_DEV = 1024
PATCH_DEV = 1
ITERS = 6


time_step = 0.08


def with_halo(array, sides, width, wrap):
    for axis, dim in sides:
        size, length = (lax.axis_size(axis), array.shape[dim])
        up = [(i, (i + 1) % size) for i in range(size if wrap else size - 1)]
        down = [(j, i) for i, j in up]
        last = lax.slice_in_dim(array, length - width, length, axis=dim)
        initial = lax.slice_in_dim(array, 0, width, axis=dim)
        before = lax.ppermute(last, axis, up)
        after = lax.ppermute(initial, axis, down)
        array = jnp.concatenate([before, array, after], axis=dim)
    return array


def solve_block(inverse, slot_rows, lift_matrix, readout):
    forcing = jnp.einsum("ic,bpcm->bpim", lift_matrix, slot_rows, precision=lax.Precision.HIGHEST)
    damping = 0.5 * slot_rows[:, :, 5:6, :]
    profile = jnp.zeros_like(forcing)
    for sweep in range(ITERS):
        profile = jnp.einsum(
            "pij,bpjm->bpim",
            inverse,
            forcing - damping * jnp.tanh(profile),
            precision=lax.Precision.HIGHEST,
        )
    return jnp.einsum("fi,bpim->bpfm", readout, profile, precision=lax.Precision.HIGHEST)


def slot_ranks(patches, patch_total):
    onehot = (patches[:, None] == jnp.arange(patch_total, dtype=jnp.int32)[None, :]).astype(
        jnp.int32
    )
    return jnp.sum(jnp.cumsum(onehot, axis=0) * onehot, axis=1) - 1


def combine_terms(fields, local_visc, neighbours, source, flux_jacobian):
    diffusion = jnp.zeros_like(fields)
    for beside in neighbours:
        diffusion = diffusion + 0.5 * (local_visc + beside[5]) * (beside[:5] - fields)
    coupling = jnp.einsum("fg,gxyz->fxyz", flux_jacobian, fields, precision=lax.Precision.HIGHEST)
    return fields + time_step * (diffusion + coupling + source)


def advance(padded, source, flux_jacobian):
    center = padded[:, 1:-1, 1:-1, 1:-1]
    neighbours = (
        padded[:, 2:, 1:-1, 1:-1],
        padded[:, :-2, 1:-1, 1:-1],
        padded[:, 1:-1, 2:, 1:-1],
        padded[:, 1:-1, :-2, 1:-1],
        padded[:, 1:-1, 1:-1, 2:],
        padded[:, 1:-1, 1:-1, :-2],
    )
    return combine_terms(center[:5], center[5], neighbours, source, flux_jacobian)


def body(
    adjoint, viscosity, flux_jacobian, face_cell, face_patch, wall_inverse, lift_matrix, readout
):
    span_devices = lax.axis_size("gz")
    patch_col = span_devices * PATCH_DEV
    capacity = 2 * FACE_DEV // patch_col
    stacked = jnp.concatenate([adjoint, viscosity[None]], axis=0)
    local = stacked.reshape(6, CX * CY * CZ)
    patches = face_patch[:, 0]
    row_data = jnp.take(local, face_cell, axis=1)
    ranks = slot_ranks(patches, patch_col)
    buffer = jnp.zeros((patch_col, 6, capacity), jnp.float32).at[patches, :, ranks].set(row_data.T)
    result = solve_block(
        lax.all_gather(wall_inverse, "gz", axis=0, tiled=True), buffer[None], lift_matrix, readout
    )[0]
    shear = result[patches, :, ranks].T
    source = (
        jnp.zeros((5, CX * CY * CZ), jnp.float32).at[:, face_cell].add(shear).reshape(5, CX, CY, CZ)
    )
    widened = with_halo(stacked, (("gx", 1), ("gy", 2)), 1, False)
    padded = with_halo(widened, (("gz", 3),), 1, True)
    updated = advance(padded, source, flux_jacobian)
    return (updated, shear)


def solution(mesh):
    in_specs = (
        P(None, "gx", "gy", "gz"),
        P("gx", "gy", "gz"),
        P(),
        P(("gx", "gy", "gz")),
        P(("gx", "gy", "gz"), None),
        P(("gx", "gy", "gz"), None, None),
        P(),
        P(),
    )
    out_specs = (P(None, "gx", "gy", "gz"), P(None, ("gx", "gy", "gz")))
    return jax.shard_map(body, mesh=mesh, in_specs=in_specs, out_specs=out_specs, check_vma=False)
```

profile of v0, /device:TPU:4, one launch (start us, length us, event | category | flops | bytes accessed | tf_op | source)
XLA Modules:
  0.0 159.4 jit_solution(15411407666337382090)
XLA Ops:
  8.0 1.1 pad_maximum_fusion.21
  9.0 2.4 %collective-permute-start = (f32[6,1,32,256]{3,2,1,0:T(8,128)S(1)}, f32[6,1,32,256]{3,2,1,0:T(8,128)S(1)}, u32[]{:S(2)}, u32[]{:S(2)}) collective-permute-start(f32[6,1,32,256]{3,2,1,0:T(8,128)S(1)} %get-tuple-element.20), channel_id=1, source_target_pairs={{64,0},{128,64},{192,128},{65,1},{129,65},{193,129},{66,2},{130,66... | collective-permute-start | bytes 589832 | tf_op jit(solution)/shard_map/ppermute | solution.py:25
  11.5 3.4 %collective-permute-start.1 = (f32[6,1,32,256]{3,2,1,0:T(8,128)S(1)}, f32[6,1,32,256]{3,2,1,0:T(8,128)S(1)}, u32[]{:S(2)}, u32[]{:S(2)}) collective-permute-start(f32[6,1,32,256]{3,2,1,0:T(8,128)S(1)} %get-tuple-element.19), channel_id=1, source_target_pairs={{0,64},{64,128},{128,192},{1,65},{65,129},{129,193},{2,66},{66,130... | collective-permute-start | bytes 589832 | tf_op jit(solution)/shard_map/ppermute | solution.py:24
  16.6 4.5 %reduce-window.6 = s32[16,8,128]{2,1,0:T(8,128)S(1)} reduce-window(s32[16,8,128]{2,1,0:T(8,128)S(1)} %fusion.69, s32[]{:T(128)} %constant.13.clone.1), window={size=1x1x128 pad=0_0x0_0x127_0}, to_apply=%region_0.1 | reduce-window | flops 2080768 | bytes 131076 | tf_op jit(solution)/shard_map/reduce-window
  22.5 9.0 %copy.51 = f32[6,32768]{0,1:T(8,128)} copy(f32[6,32768]{1,0:T(8,128)S(1)} %pad_maximum_fusion.2) | data formatting | bytes 1572864 | tf_op jit(solution)/shard_map/concatenate | solution.py:78
  31.5 9.7 %scatter_custom_fusion.1 = f32[6,2048]{0,1:T(8,128)S(1)} fusion(s32[1024]{0:T(1024)S(1)} %get-tuple-element.27, f32[]{:T(128)} %constant.12.clone.1, f32[]{:T(128)} %constant.38.clone.1, pred[1024]{0:T(1024)(128)(4,1)S(1)} %compare_and_fusion, f32[6,32768]{0,1:T(8,128)} %copy.51, s32[1024]{0:T(1024)S(1)} %get-tuple-element.22), kind=kCustom, calls=%fused_computation.84 | custom fusion | flops 6144 | bytes 840712
  41.7 1.3 collective-permute-start.2
  43.0 3.0 %collective-permute-start.3 = (f32[6,6,1,256]{3,2,1,0:T(1,128)S(1)}, f32[6,6,1,256]{3,2,1,0:T(1,128)S(1)}, u32[]{:S(2)}, u32[]{:S(2)}) collective-permute-start(f32[6,6,1,256]{3,2,1,0:T(1,128)S(1)} %get-tuple-element.15), channel_id=1, source_target_pairs={{0,16},{16,32},{32,48},{1,17},{17,33},{33,49},{2,18},{18,34},{34,5... | collective-permute-start | bytes 110600 | tf_op jit(solution)/shard_map/ppermute | solution.py:24
  46.1 1.8 %convolution_bitcast_fusion.1 = f32[1,16,128,128]{2,3,1,0:T(8,128)S(1)} fusion(f32[6,16,128]{2,0,1:T(8,128)S(1)} %copy.52, f32[128,6]{0,1:T(8,128)S(1)} %copy-done), kind=kOutput, calls=%fused_computation.18 | convolution fusion | flops 18874368 | bytes 1100800 | tf_op jit(solution)/shard_map/ic,bpcm->bpim/dot_general | solution.py:31
  47.9 1.1 pad_maximum_fusion
  49.1 1.1 copy-done.3
  50.2 1.3 fusion.74
  51.6 1.5 copy.43
  53.0 2.0 %collective-permute-start.5 = (f32[6,6,34,1]{2,3,1,0:T(1,128)S(1)}, f32[6,6,34,1]{2,3,1,0:T(1,128)}, u32[]{:S(2)}, u32[]{:S(2)}) collective-permute-start(f32[6,6,34,1]{2,3,1,0:T(1,128)S(1)} %copy.43), channel_id=1, source_target_pairs={{0,1},{1,2},{2,3},{3,4},{4,5},{5,6},{6,7},{7,8},{8,9},{9,10},{10,1... | collective-permute-start | bytes 14696 | tf_op jit(solution)/shard_map/ppermute | solution.py:24
  55.0 2.1 %copy.41 = f32[6,6,34,1]{2,3,1,0:T(1,128)} copy(f32[6,6,34,1]{3,2,1,0:T(8,128)} %get-tuple-element.10) | data formatting | bytes 9792 | tf_op jit(solution)/shard_map/slice | solution.py:23
  57.1 5.2 %collective-permute-start.4 = (f32[6,6,34,1]{2,3,1,0:T(1,128)}, f32[6,6,34,1]{2,3,1,0:T(1,128)}, u32[]{:S(2)}, u32[]{:S(2)}) collective-permute-start(f32[6,6,34,1]{2,3,1,0:T(1,128)} %copy.41), channel_id=1, source_target_pairs={{1,0},{2,1},{3,2},{4,3},{5,4},{6,5},{7,6},{8,7},{9,8},{10,9},{11,1... | collective-permute-start | bytes 14696 | tf_op jit(solution)/shard_map/ppermute | solution.py:25
  62.2 1.5 fusion.64
  64.5 2.1 %copy.44 = f32[6,6,34,1]{3,0,2,1:T(8,128)} copy(f32[6,6,34,1]{2,3,1,0:T(1,128)} %collective-permute-done.5) | data formatting | bytes 9792 | tf_op jit(solution)/shard_map/ppermute | solution.py:24
  66.6 2.0 %copy.42 = f32[6,6,34,1]{3,2,1,0:T(8,128)} copy(f32[6,6,34,1]{2,3,1,0:T(1,128)} %collective-permute-done.4) | data formatting | bytes 9792 | tf_op jit(solution)/shard_map/ppermute | solution.py:25
  68.6 1.5 pad_maximum_fusion.23
  71.1 1.4 fusion.37
  72.5 22.5 %all-gather.2.cloned.1.call-done = f32[16,128,128]{2,1,0:T(8,128)} async-done(((f32[1,128,128]{2,1,0:T(8,128)}), f32[16,128,128]{2,1,0:T(8,128)}) %all-gather.2.cloned.1.call-update) | async-done | bytes 1048592 | tf_op jit(solution)/shard_map/all_gather | solution.py:85
  95.1 3.6 %fusion.13 = f32[16,128,128]{1,2,0:T(8,128)S(1)} fusion(f32[1,16,128,128]{2,3,1,0:T(8,128)S(1)} %convolution_bitcast_fusion.1, f32[16,128,128]{2,1,0:T(8,128)} %all-gather.2.cloned.1.call-done, f32[16,128]{1,0:T(8,128)S(1)} %broadcast_multiply_fusion, f32[16,128]{1,0:T(8,128)S(1)} %bitcast.211), kind=kOutput, calls=%fused_computation.26 | convolution fusion | flops 403439616 | bytes 3162112 | tf_op jit(solution)/shard_map/pij,bpjm->bpim/dot_general | solution.py:35
  98.7 2.3 %fusion.17 = f32[16,128,128]{1,2,0:T(8,128)S(1)} fusion(f32[1,16,128,128]{2,3,1,0:T(8,128)S(1)} %convolution_bitcast_fusion.1, f32[16,128,128]{1,2,0:T(8,128)S(1)} %fusion.13, f32[16,128,128]{2,1,0:T(8,128)S(1)} %copy-done.2, f32[16,128]{1,0:T(8,128)S(1)} %bitcast.212), kind=kOutput, calls=%fused_computation.30 | convolution fusion | flops 403177472 | bytes 4202496 | tf_op jit(solution)/shard_map/pij,bpjm->bpim/dot_general | solution.py:35
  101.1 2.4 %fusion.21 = f32[16,128,128]{1,2,0:T(8,128)S(1)} fusion(f32[1,16,128,128]{2,3,1,0:T(8,128)S(1)} %convolution_bitcast_fusion.1, f32[16,128,128]{1,2,0:T(8,128)S(1)} %fusion.17, f32[16,128,128]{2,1,0:T(8,128)S(1)} %copy-done.2, f32[16,128]{1,0:T(8,128)S(1)} %bitcast.213), kind=kOutput, calls=%fused_computation.34 | convolution fusion | flops 403177472 | bytes 4202496 | tf_op jit(solution)/shard_map/pij,bpjm->bpim/dot_general | solution.py:35
  103.4 2.4 %fusion.25 = f32[16,128,128]{1,2,0:T(8,128)S(1)} fusion(f32[1,16,128,128]{2,3,1,0:T(8,128)S(1)} %convolution_bitcast_fusion.1, f32[16,128,128]{1,2,0:T(8,128)S(1)} %fusion.21, f32[16,128,128]{2,1,0:T(8,128)S(1)} %copy-done.2, f32[16,128]{1,0:T(8,128)S(1)} %bitcast.214), kind=kOutput, calls=%fused_computation.38 | convolution fusion | flops 403177472 | bytes 4202496 | tf_op jit(solution)/shard_map/pij,bpjm->bpim/dot_general | solution.py:35
  105.8 2.4 %fusion.29 = f32[16,128,128]{1,2,0:T(8,128)S(1)} fusion(f32[1,16,128,128]{2,3,1,0:T(8,128)S(1)} %convolution_bitcast_fusion.1, f32[16,128,128]{1,2,0:T(8,128)S(1)} %fusion.25, f32[16,128,128]{2,1,0:T(8,128)S(1)} %copy-done.2, f32[16,128]{1,0:T(8,128)S(1)} %bitcast.215), kind=kOutput, calls=%fused_computation.42 | convolution fusion | flops 403177472 | bytes 4202496 | tf_op jit(solution)/shard_map/pij,bpjm->bpim/dot_general | solution.py:35
  108.2 2.3 %convolution_bitcast_fusion = f32[16,128,128]{1,2,0:T(8,128)S(1)} fusion(f32[16,128,128]{1,2,0:T(8,128)S(1)} %fusion.29, f32[16,128,128]{2,1,0:T(8,128)S(1)} %copy-done.2), kind=kOutput, calls=%fused_computation.7 | convolution fusion | flops 402653184 | bytes 3145728 | tf_op jit(solution)/shard_map/pij,bpjm->bpim/dot_general | solution.py:35
  111.9 11.6 %gather_fusion = f32[1024,5]{1,0:T(8,128)} fusion(f32[16,5,128]{1,2,0:T(8,128)S(1)} %copy.54, s32[1024]{0:T(1024)S(1)} %bitcast.198), kind=kCustom, calls=%fused_computation.1 | custom fusion | bytes 49152 | tf_op jit(solution)/shard_map/gather | solution.py:87
  123.4 13.4 %scatter_custom_fusion = f32[5,32768]{0,1:T(8,128)} fusion(s32[1024]{0:T(1024)S(1)} %get-tuple-element.23, f32[1024,5]{1,0:T(8,128)} %gather_fusion, f32[]{:T(128)} %constant.12.clone.1), kind=kCustom, calls=%fused_computation.4 | custom fusion | flops 5120 | bytes 655872 | tf_op jit(solution)/shard_map/scatter-add | solution.py:89
  136.8 10.1 %copy.56 = f32[5,4,32,256]{3,0,2,1:T(8,128)} copy(f32[5,4,32,256]{0,3,2,1:T(8,128)} %bitcast.199) | data formatting | bytes 1310720 | tf_op jit(solution)/shard_map/reshape | solution.py:89
  146.9 3.8 %fusion.9 = f32[5,4,32,256]{3,0,2,1:T(8,128)S(1)} fusion(f32[5,4,32,256]{3,0,2,1:T(8,128)} %copy.56, f32[5,4,32,256]{3,2,1,0:T(8,128)S(1)} %copy-done.1, f32[6,6,34,256]{3,0,2,1:T(8,128)S(1)} %copy.45, f32[6,6,34,1]{3,0,2,1:T(8,128)S(1)} %copy-done.6, f32[5,4,32,256]{3,2,1,0:T(8,128)} %fusion.37, f32[4,32,256]{2,1,0:T(8,128)S(1)} %copy-done.15, ...), kind=kOutput, calls=%fused_computation.22 | convolution fusion | flops 11141120 | bytes 4010884 | tf_op jit(solution)/shard_map/fg,gxyz->fxyz/dot_general | solution.py:55
  (86 shorter events, 9.2 us)
Async XLA Ops:
  7.2 38.9 %copy-start = (f32[128,6]{0,1:T(8,128)S(1)}, f32[128,6]{0,1:T(8,128)}, u32[]{:S(2)}) copy-start(f32[128,6]{0,1:T(8,128)} %param.14) | copy-start | bytes 9220
  7.2 14.5 %copy-start.25 = (s32[2]{0:T(128)S(1)}, s32[2]{0:T(128)}, u32[]{:S(2)}) copy-start(s32[2]{0:T(128)} %constant.44) | copy-start | bytes 28
  7.2 14.6 %copy-start.24 = (s32[2]{0:T(128)S(1)}, s32[2]{0:T(128)}, u32[]{:S(2)}) copy-start(s32[2]{0:T(128)} %constant.41) | copy-start | bytes 28
  7.2 14.7 %copy-start.1 = (f32[5,4,32,256]{3,2,1,0:T(8,128)S(1)}, f32[5,4,32,256]{3,2,1,0:T(8,128)}, u32[]{:S(2)}) copy-start(f32[5,4,32,256]{3,2,1,0:T(8,128)} %param.8) | copy-start | bytes 1966084
  7.2 14.3 %copy-start.20 = (s32[1024,1]{0,1:T(1,128)S(1)}, s32[1024,1]{0,1:T(1,128)}, u32[]{:S(2)}) copy-start(s32[1024,1]{0,1:T(1,128)} %param.12) | copy-start | bytes 12292
  7.2 14.6 %copy-start.21 = (s32[1024]{0:T(1024)S(1)}, s32[1024]{0:T(1024)}, u32[]{:S(2)}) copy-start(s32[1024]{0:T(1024)} %param.11) | copy-start | bytes 12292
  7.2 87.8 %all-gather.2.cloned.1.call-start = ((), (), s32[]{:S(2)}) async-start(), calls=%async_computation | async-start | bytes 1114112 | tf_op jit(solution)/shard_map/all_gather | solution.py:85
  9.0 32.6 %collective-permute-start = (f32[6,1,32,256]{3,2,1,0:T(8,128)S(1)}, f32[6,1,32,256]{3,2,1,0:T(8,128)S(1)}, u32[]{:S(2)}, u32[]{:S(2)}) collective-permute-start(f32[6,1,32,256]{3,2,1,0:T(8,128)S(1)} %get-tuple-element.20), channel_id=1, source_target_pairs={{64,0},{128,64},{192,128},{65,1},{129,65},{193,129},{66,2},{130,66... | collective-permute-start | bytes 589832 | tf_op jit(solution)/shard_map/ppermute | solution.py:25
  11.5 30.1 %collective-permute-start.1 = (f32[6,1,32,256]{3,2,1,0:T(8,128)S(1)}, f32[6,1,32,256]{3,2,1,0:T(8,128)S(1)}, u32[]{:S(2)}, u32[]{:S(2)}) collective-permute-start(f32[6,1,32,256]{3,2,1,0:T(8,128)S(1)} %get-tuple-element.19), channel_id=1, source_target_pairs={{0,64},{64,128},{128,192},{1,65},{65,129},{129,193},{2,66},{66,130... | collective-permute-start | bytes 589832 | tf_op jit(solution)/shard_map/ppermute | solution.py:24
  31.5 10.1 %copy-start.5 = (f32[4,32,256]{2,1,0:T(8,128)S(1)}, f32[4,32,256]{2,1,0:T(8,128)}, u32[]{:S(2)}) copy-start(f32[4,32,256]{2,1,0:T(8,128)} %param.9) | copy-start | bytes 393220
  41.6 20.6 %copy-start.8 = (f32[6,1,32,256]{3,2,1,0:T(8,128)}, f32[6,1,32,256]{3,2,1,0:T(8,128)S(1)}, u32[]{:S(2)}) copy-start(f32[6,1,32,256]{3,2,1,0:T(8,128)S(1)} %collective-permute-done) | copy-start | bytes 589828
  41.7 1.4 copy-start.10
  41.7 6.2 %collective-permute-start.2 = (f32[6,6,1,256]{3,2,1,0:T(1,128)S(1)}, f32[6,6,1,256]{3,2,1,0:T(1,128)S(1)}, u32[]{:S(2)}, u32[]{:S(2)}) collective-permute-start(f32[6,6,1,256]{3,2,1,0:T(1,128)S(1)} %get-tuple-element.16), channel_id=1, source_target_pairs={{16,0},{32,16},{48,32},{17,1},{33,17},{49,33},{18,2},{34,18},{50,3... | collective-permute-start | bytes 110600 | tf_op jit(solution)/shard_map/ppermute | solution.py:25
  43.0 4.9 %collective-permute-start.3 = (f32[6,6,1,256]{3,2,1,0:T(1,128)S(1)}, f32[6,6,1,256]{3,2,1,0:T(1,128)S(1)}, u32[]{:S(2)}, u32[]{:S(2)}) collective-permute-start(f32[6,6,1,256]{3,2,1,0:T(1,128)S(1)} %get-tuple-element.15), channel_id=1, source_target_pairs={{0,16},{16,32},{32,48},{1,17},{17,33},{33,49},{2,18},{18,34},{34,5... | collective-permute-start | bytes 110600 | tf_op jit(solution)/shard_map/ppermute | solution.py:24
  47.9 3.7 %copy-start.16 = (f32[6,6,1,256]{3,2,1,0:T(1,128)}, f32[6,6,1,256]{3,2,1,0:T(1,128)S(1)}, u32[]{:S(2)}) copy-start(f32[6,6,1,256]{3,2,1,0:T(1,128)S(1)} %collective-permute-done.2) | copy-start | bytes 110596
  47.9 3.6 %copy-start.18 = (f32[6,6,1,256]{3,2,1,0:T(1,128)}, f32[6,6,1,256]{3,2,1,0:T(1,128)S(1)}, u32[]{:S(2)}) copy-start(f32[6,6,1,256]{3,2,1,0:T(1,128)S(1)} %collective-permute-done.3) | copy-start | bytes 110596
  49.1 1.1 copy-start.3
  53.0 11.5 %collective-permute-start.5 = (f32[6,6,34,1]{2,3,1,0:T(1,128)S(1)}, f32[6,6,34,1]{2,3,1,0:T(1,128)}, u32[]{:S(2)}, u32[]{:S(2)}) collective-permute-start(f32[6,6,34,1]{2,3,1,0:T(1,128)S(1)} %copy.43), channel_id=1, source_target_pairs={{0,1},{1,2},{2,3},{3,4},{4,5},{5,6},{6,7},{7,8},{8,9},{9,10},{10,1... | collective-permute-start | bytes 14696 | tf_op jit(solution)/shard_map/ppermute | solution.py:24
  57.1 6.7 %copy-start.4 = (f32[6,6,34,256]{3,2,1,0:T(8,128)S(1)}, f32[6,6,34,256]{3,2,1,0:T(8,128)}, u32[]{:S(2)}) copy-start(f32[6,6,34,256]{3,2,1,0:T(8,128)} %copy-done.3) | copy-start | bytes 3760132
  57.1 9.5 %collective-permute-start.4 = (f32[6,6,34,1]{2,3,1,0:T(1,128)}, f32[6,6,34,1]{2,3,1,0:T(1,128)}, u32[]{:S(2)}, u32[]{:S(2)}) collective-permute-start(f32[6,6,34,1]{2,3,1,0:T(1,128)} %copy.41), channel_id=1, source_target_pairs={{1,0},{2,1},{3,2},{4,3},{5,4},{6,5},{7,6},{8,7},{9,8},{10,9},{11,1... | collective-permute-start | bytes 14696 | tf_op jit(solution)/shard_map/ppermute | solution.py:25
  68.5 1.5 copy-start.7
  68.5 1.5 copy-start.9
  68.5 1.5 copy-start.11
  68.5 1.6 copy-start.17
  68.6 1.6 copy-start.19
  70.1 1.0 copy-start.14
  95.0 3.7 %copy-start.2 = (f32[16,128,128]{2,1,0:T(8,128)S(1)}, f32[16,128,128]{2,1,0:T(8,128)}, u32[]{:S(2)}) copy-start(f32[16,128,128]{2,1,0:T(8,128)} %all-gather.2.cloned.1.call-done) | copy-start | bytes 3145732
  108.1 2.3 %copy-start.22 = (f32[5,128]{1,0:T(8,128)S(1)}, f32[5,128]{1,0:T(8,128)}, u32[]{:S(2)}) copy-start(f32[5,128]{1,0:T(8,128)} %param.15) | copy-start | bytes 7684
  136.8 10.1 %copy-start.6 = (f32[6,6,34,1]{3,0,2,1:T(8,128)S(1)}, f32[6,6,34,1]{3,0,2,1:T(8,128)}, u32[]{:S(2)}) copy-start(f32[6,6,34,1]{3,0,2,1:T(8,128)} %copy.44) | copy-start | bytes 14692
  136.8 10.1 %copy-start.15 = (f32[4,32,256]{2,1,0:T(8,128)S(1)}, f32[4,32,256]{2,1,0:T(8,128)}, u32[]{:S(2)}) copy-start(f32[4,32,256]{2,1,0:T(8,128)} %get-tuple-element.21) | copy-start | bytes 393220
  136.8 10.1 %copy-start.23 = (f32[5,5]{1,0:T(8,128)S(1)}, f32[5,5]{1,0:T(8,128)}, u32[]{:S(2)}) copy-start(f32[5,5]{1,0:T(8,128)} %param.10) | copy-start | bytes 304
  150.7 1.1 copy-start.12
  (1 other events, 0.9 us)
Sparse Core Ops, SparseCore 0:
  9.9 85.1 all-gather.1
where the time goes:
time: 160 us; the launch traced here: 159 us
  local copies, waits for them, and re-layouts  46 us (29%)
  other arithmetic  36.3 us (23%)
  waiting for transfers between devices  23.2 us (14%)
  matrix products  21.9 us (14%)
  starting transfers between devices  17.4 us (11%)
  between operations  14.5 us (9%)
    all_gather x1, waiting for transfers between devices, body(): lax.all_gather(wall_inverse, 'gz', axis=0, tiled=True)  22.5 us
    dot_general x6, matrix products, solve_block(): jnp.einsum('pij,bpjm->bpim', inverse, forcing - damping * jnp.tanh(profil...  15.4 us
    scatter-add x1, other arithmetic, body(): jnp.zeros((5, CX * CY * CZ), jnp.float32).at[:, face_cell].add(shear)  13.4 us
    gather x1, local copies, waits for them, and re-layouts, body(): shear = result[patches, :, ranks].T  11.6 us
    reshape x1, local copies, waits for them, and re-layouts, body(): jnp.zeros((5, CX * CY * CZ), jnp.float32).at[:, face_cell].add(shear)  10.1 us
    concatenate x2, local copies, waits for them, and re-layouts, body(): stacked = jnp.concatenate([adjoint, viscosity[None]], axis=0)  10 us
    unnamed x3, other arithmetic  9.89 us
    ppermute x3, starting transfers between devices, with_halo(): after = lax.ppermute(initial, axis, down)  8.9 us
  transfers between devices with their start and end apart: 7, of which 1 were waited for; matrix products, arithmetic and copies ran while one was open for 28% of the time, Pallas kernels for 0%

commit v1 on v0

v1 whole, which is shorter than its diff:
```python
import functools

import jax
import jax.numpy as jnp
from jax import lax
from jax.experimental import pallas as pl
from jax.experimental.pallas import tpu as pltpu
from jax.sharding import PartitionSpec as P

CX = 4
CY = 32
CZ = 256
FACES = 1024
ROWS = CX * CY
PATCHES = 16
CAP = 128
PROF = 128
ITERS = 6
GROUP = 4

time_step = 0.08

F32 = jnp.float32
BF16 = jnp.bfloat16
VMEM = pl.BlockSpec(memory_space=pltpu.VMEM)
SMEM = pl.BlockSpec(memory_space=pltpu.SMEM)
PARAMS = pltpu.CompilerParams(vmem_limit_bytes=48 * 1024 * 1024)


def split(x):
    high = x.astype(BF16)
    low = (x - high.astype(F32)).astype(BF16)
    return high, low


def dot(a, b):
    return jnp.dot(a, b, preferred_element_type=F32)


def dot_t(a, b):
    return lax.dot_general(a, b, (((1,), (1,)), ((), ())), preferred_element_type=F32)


def one_hot(count, index, dtype):
    numbers = lax.broadcasted_iota(jnp.int32, (count, index.shape[-1]), 0)
    return jnp.where(numbers == index, 1.0, 0.0).astype(dtype)


def gather_kernel(
    adjoint, viscosity, cell, patch, x_low, x_high, y_low, y_high, z_low, z_high, slots, ranks
):
    for f in range(6):
        field = viscosity if f == 5 else adjoint.at[f]
        x_low[f] = field[0]
        x_high[f] = field[CX - 1]
        for x in range(CX):
            y_low[f * CX + x : f * CX + x + 1, :] = field[x, 0:1, :]
            y_high[f * CX + x : f * CX + x + 1, :] = field[x, CY - 1 : CY, :]
    cells = cell[...]
    patches = patch[...]
    row = cells >> 8
    span = cells & (CZ - 1)
    span_hot = one_hot(CZ, span, BF16)
    row_hot = lax.broadcasted_iota(jnp.int32, (ROWS, FACES), 0) == row
    ends = lax.broadcasted_iota(jnp.int32, (8, CZ), 0)
    lanes = lax.broadcasted_iota(jnp.int32, (8, CZ), 1)
    edge = jnp.where(
        ((ends == 0) & (lanes == 0)) | ((ends == 1) & (lanes == CZ - 1)), 1.0, 0.0
    ).astype(BF16)
    values = []
    for f in range(6):
        field = (viscosity[...] if f == 5 else adjoint[f]).reshape(ROWS, CZ)
        high, low = split(field)
        found = dot(high, span_hot) + dot(low, span_hot)
        values.append(jnp.sum(jnp.where(row_hot, found, 0.0), axis=0, keepdims=True))
        rest = (field - high.astype(F32) - low.astype(F32)).astype(BF16)
        outer = dot_t(edge, high) + dot_t(edge, low) + dot_t(edge, rest)
        z_low[f : f + 1, :] = outer[0:1]
        z_high[f : f + 1, :] = outer[1:2]
    z_low[6:8, :] = jnp.zeros((2, ROWS), F32)
    z_high[6:8, :] = jnp.zeros((2, ROWS), F32)

    hot = one_hot(PATCHES, patches, F32)
    pieces = FACES // 128
    stacked = jnp.concatenate([hot[:, b * 128 : (b + 1) * 128] for b in range(pieces)], axis=0)
    stacked = stacked.astype(BF16)
    upto = (
        lax.broadcasted_iota(jnp.int32, (128, 256), 0)
        <= lax.broadcasted_iota(jnp.int32, (128, 256), 1)
    )
    counts = dot(stacked, jnp.where(upto, 1.0, 0.0).astype(BF16))
    before = jnp.zeros((PATCHES, 128), F32)
    found_ranks = []
    for b in range(pieces):
        mine = slice(b * PATCHES, (b + 1) * PATCHES)
        piece = hot[:, b * 128 : (b + 1) * 128]
        found_ranks.append(
            jnp.sum(piece * (counts[mine, :128] + before), axis=0, keepdims=True) - 1.0
        )
        before = before + counts[mine, 128:]
    rank = jnp.concatenate(found_ranks, axis=1).astype(jnp.int32)
    ranks[...] = rank

    rank_hot = one_hot(CAP, rank, BF16)
    table = jnp.concatenate(values + [jnp.zeros((2, FACES), F32)], axis=0)
    high, low = split(table)
    both = jnp.concatenate([high.astype(F32), low.astype(F32)], axis=0)
    spread = jnp.concatenate(
        [jnp.where(patches == p, both, 0.0).astype(BF16) for p in range(PATCHES)], axis=0
    )
    placed = dot_t(spread, rank_hot).reshape(PATCHES, 16, CAP)
    slots[...] = placed[:, :8] + placed[:, 8:]


def stencil_kernel(
    adjoint, viscosity, jacobian, x_before, x_after, y_before, y_after, z_before, z_after, out
):
    gx, gy = lax.axis_index("gx"), lax.axis_index("gy")
    has_before_x = jnp.where(gx > 0, 1.0, 0.0)
    has_after_x = jnp.where(gx < lax.axis_size("gx") - 1, 1.0, 0.0)
    has_before_y = jnp.where(gy > 0, 1.0, 0.0)
    has_after_y = jnp.where(gy < lax.axis_size("gy") - 1, 1.0, 0.0)
    rows = lax.broadcasted_iota(jnp.int32, (CY, CZ), 0)
    lanes = lax.broadcasted_iota(jnp.int32, (CY, CZ), 1)
    z_low = jnp.transpose(z_before[...])
    z_high = jnp.transpose(z_after[...])

    def field_at(f, x):
        return viscosity[x] if f == 5 else adjoint[f, x]

    def neighbours(f, x):
        center = field_at(f, x)
        yield field_at(f, x - 1) if x > 0 else x_before[f] * has_before_x
        yield field_at(f, x + 1) if x < CX - 1 else x_after[f] * has_after_x
        at = slice(f * CX + x, f * CX + x + 1)
        yield jnp.where(rows == 0, y_before[at, :] * has_before_y, pltpu.roll(center, 1, 0))
        yield jnp.where(
            rows == CY - 1, y_after[at, :] * has_after_y, pltpu.roll(center, CY - 1, 0)
        )
        part = slice(x * CY, (x + 1) * CY)
        yield jnp.where(lanes == 0, z_low[part, f : f + 1], pltpu.roll(center, 1, 1))
        yield jnp.where(lanes == CZ - 1, z_high[part, f : f + 1], pltpu.roll(center, CZ - 1, 1))

    for x in range(CX):
        visc = viscosity[x]
        weights = [0.5 * (visc + other) for other in neighbours(5, x)]
        for f in range(5):
            center = adjoint[f, x]
            total = jnp.zeros((CY, CZ), F32)
            for weight, other in zip(weights, neighbours(f, x)):
                total = total + weight * (other - center)
            for g in range(5):
                total = total + jacobian[f, g] * adjoint[g, x]
            out[f, x] = center + time_step * total


def solve_kernel(inverse, slots, lift, readout, cell, patch, ranks, partial, updated, shear):
    lift_all = lift[...]
    read = jnp.concatenate([readout[...], jnp.zeros((3, PROF), F32)], axis=0)

    def stack_matrix(matrix):
        high, low = split(matrix)
        return jnp.concatenate(
            [
                jnp.concatenate([high, high], axis=1),
                jnp.concatenate([low, jnp.zeros_like(low)], axis=1),
            ],
            axis=0,
        )

    def product(stacked, right):
        count = stacked.shape[0] // 2
        both = dot(stacked, jnp.concatenate(split(right), axis=0))
        return both[:count] + both[count:]

    read_stack = stack_matrix(read)
    results = []
    for start in range(0, PATCHES, GROUP):
        group = range(start, start + GROUP)
        stacks = [stack_matrix(inverse[p]) for p in group]
        rows = [slots[p] for p in group]
        forcing = [
            jnp.dot(
                lift_all, r[:6], precision=lax.Precision.HIGHEST, preferred_element_type=F32
            )
            for r in rows
        ]
        damping = [0.5 * r[5:6] for r in rows]
        right = forcing
        for sweep in range(ITERS):
            profile = [product(s, r) for s, r in zip(stacks, right)]
            if sweep < ITERS - 1:
                right = [g - d * jnp.tanh(q) for g, d, q in zip(forcing, damping, profile)]
        results += [product(read_stack, q) for q in profile]

    result = jnp.concatenate(results, axis=0)
    rank_hot = one_hot(CAP, ranks[...], BF16)
    back = dot(
        jnp.concatenate(split(result), axis=1), jnp.concatenate([rank_hot, rank_hot], axis=0)
    )
    patches = patch[...]
    wall = jnp.zeros((8, FACES), F32)
    for p in range(PATCHES):
        wall = wall + jnp.where(patches == p, back[p * 8 : (p + 1) * 8], 0.0)
    shear[...] = wall[:5]

    cells = cell[...]
    span_hot = one_hot(CZ, cells & (CZ - 1), BF16)
    row_hot = lax.broadcasted_iota(jnp.int32, (ROWS, FACES), 0) == (cells >> 8)
    high = wall.astype(BF16).astype(F32)
    low = wall - high
    for f in range(5):
        spread = [jnp.where(row_hot, part[f : f + 1], 0.0).astype(BF16) for part in (high, low)]
        source = dot_t(spread[0], span_hot) + dot_t(spread[1], span_hot)
        updated[f] = partial[f] + time_step * source.reshape(CX, CY, CZ)


def shifted(array, axis, step):
    size = lax.axis_size(axis)
    return lax.ppermute(array, axis, [(i, (i + step) % size) for i in range(size)])


def shape(*dims, dtype=F32):
    return jax.ShapeDtypeStruct(dims, dtype)


def body(
    adjoint, viscosity, flux_jacobian, face_cell, face_patch, wall_inverse, lift_matrix, readout
):
    inverses = lax.all_to_all(
        jnp.broadcast_to(wall_inverse, (PATCHES, PROF, PROF)), "gz", 0, 0, tiled=True
    )
    cell = face_cell.reshape(1, FACES)
    patch = face_patch.reshape(1, FACES)
    face_x, face_y, face_z = shape(6, CY, CZ), shape(6 * CX, CZ), shape(8, ROWS)
    x_low, x_high, y_low, y_high, z_low, z_high, slots, ranks = pl.pallas_call(
        gather_kernel,
        out_shape=(
            face_x,
            face_x,
            face_y,
            face_y,
            face_z,
            face_z,
            shape(PATCHES, 8, CAP),
            shape(1, FACES, dtype=jnp.int32),
        ),
        in_specs=[VMEM] * 4,
        out_specs=[VMEM] * 8,
        compiler_params=PARAMS,
        name="gather",
    )(adjoint, viscosity, cell, patch)
    partial = pl.pallas_call(
        stencil_kernel,
        out_shape=shape(5, CX, CY, CZ),
        in_specs=[VMEM, VMEM, SMEM] + [VMEM] * 6,
        out_specs=VMEM,
        compiler_params=PARAMS,
        name="stencil",
    )(
        adjoint,
        viscosity,
        flux_jacobian,
        shifted(x_high, "gx", 1),
        shifted(x_low, "gx", -1),
        shifted(y_high, "gy", 1),
        shifted(y_low, "gy", -1),
        shifted(z_high, "gz", 1),
        shifted(z_low, "gz", -1),
    )
    return pl.pallas_call(
        solve_kernel,
        out_shape=(shape(5, CX, CY, CZ), shape(5, FACES)),
        in_specs=[VMEM] * 8,
        out_specs=[VMEM] * 2,
        compiler_params=PARAMS,
        name="solve",
    )(inverses, slots, lift_matrix, readout, cell, patch, ranks, partial)


def solution(mesh):
    in_specs = (
        P(None, "gx", "gy", "gz"),
        P("gx", "gy", "gz"),
        P(),
        P(("gx", "gy", "gz")),
        P(("gx", "gy", "gz"), None),
        P(("gx", "gy", "gz"), None, None),
        P(),
        P(),
    )
    out_specs = (P(None, "gx", "gy", "gz"), P(None, ("gx", "gy", "gz")))
    return jax.shard_map(body, mesh=mesh, in_specs=in_specs, out_specs=out_specs, check_vma=False)
```

time: 160 us -> 51 us (0.32)
  local copies, waits for them, and re-layouts: 46 us -> 2.06 us
  other arithmetic: 36.3 us -> 0 us
  matrix products: 21.9 us -> 0 us
  between operations: 14.5 us -> 0.74 us
  Pallas kernels: 0 us -> 13.3 us
  waiting for transfers between devices: 23.2 us -> 16.2 us
    all_gather x1 -> x0, waiting for transfers between devices: 22.5 us -> none  [body(): lax.all_gather(wall_inverse, 'gz', axis=0, tiled=True)]
    dot_general x9 -> x0, matrix products: 21.9 us -> none  [the longest x6 15.4 us: solve_block(): jnp.einsum('pij,bpjm->bpim', inverse, forcing - damping * jnp.tanh(profil...]
    ppermute x6, waiting for transfers between devices: 0.02 us -> 16.2 us  [shifted(): lax.ppermute(array, axis, [(i, (i + step) % size) for i in range(size)])]
    scatter-add x1 -> x0, other arithmetic: 13.4 us -> none  [body(): jnp.zeros((5, CX * CY * CZ), jnp.float32).at[:, face_cell].add(shear)]
    pallas_call x0 -> x3, Pallas kernels: none -> 13.3 us  [the longest x1 9.39 us: body(): pl.pallas_call(solve_kernel, out_shape=(shape(5, CX, CY, CZ), shape(5, FA...]
    gather x1 -> x0, local copies, waits for them, and re-layouts: 11.6 us -> none  [body(): shear = result[patches, :, ranks].T]
    concatenate x3 -> x0, local copies, waits for them, and re-layouts: 10.8 us -> none  [the longest x2 10 us: body(): stacked = jnp.concatenate([adjoint, viscosity[None]], axis=0)]
    reshape x1 -> x0, local copies, waits for them, and re-layouts: 10.1 us -> none  [body(): jnp.zeros((5, CX * CY * CZ), jnp.float32).at[:, face_cell].add(shear)]
  transfers between devices with their start and end apart: 7 -> 7, of which waited for: 1 -> 2; matrix products, arithmetic and copies ran while one was open for 28% -> 0% of each run, Pallas kernels for 0% -> 8%
where the time goes in v1:
time: 51 us; the launch traced here: 50.7 us
  starting transfers between devices  18.5 us (36%)
  waiting for transfers between devices  16.2 us (32%)
  Pallas kernels  13.3 us (26%)
  local copies, waits for them, and re-layouts  2.06 us (4%)
  between operations  0.74 us (1%)
    ppermute x6, waiting for transfers between devices, shifted(): lax.ppermute(array, axis, [(i, (i + step) % size) for i in range(size)])  16.2 us
    ppermute x6, starting transfers between devices, shifted(): lax.ppermute(array, axis, [(i, (i + step) % size) for i in range(size)])  9.67 us
    pallas_call x1, Pallas kernels, body(): pl.pallas_call(solve_kernel, out_shape=(shape(5, CX, CY, CZ), shape(5, FA...  9.39 us
    all_to_all x1, starting transfers between devices, body(): lax.all_to_all(jnp.broadcast_to(wall_inverse, (PATCHES, PROF, PROF)), 'gz...  8.78 us
    pallas_call x1, Pallas kernels, body(): pl.pallas_call(stencil_kernel, out_shape=shape(5, CX, CY, CZ), in_specs=[...  2.05 us
    broadcast_in_dim x1, local copies, waits for them, and re-layouts, body(): jnp.broadcast_to(wall_inverse, (PATCHES, PROF, PROF))  1.92 us
    pallas_call x1, Pallas kernels, body(): pl.pallas_call(gather_kernel, out_shape=(face_x, face_x, face_y, face_y,...  1.87 us
  transfers between devices with their start and end apart: 7, of which 2 were waited for; matrix products, arithmetic and copies ran while one was open for 0% of the time, Pallas kernels for 8%

profile of v1, /device:TPU:4, one launch (start us, length us, event | category | flops | bytes accessed | tf_op | source)
XLA Modules:
  0.0 50.7 jit_solution(1858536978232586773)
XLA Ops:
  0.6 1.9 %broadcast_in_dim.8 = f32[16,128,128]{2,1,0:T(8,128)} broadcast(f32[128,128]{1,0:T(8,128)} %bitcast.7), dimensions={1,2} | broadcast | bytes 1114112 | tf_op jit(solution)/shard_map/broadcast_in_dim | solution.py:231
  2.6 0.0 copy-start
  2.6 0.0 copy-start.1
  2.6 0.0 copy-start.2
  2.6 0.0 copy-start.3
  2.6 8.8 %all-to-all-start = ((f32[16,128,128]{2,1,0:T(8,128)}), f32[16,128,128]{2,1,0:T(8,128)S(1)}, u32[]{:S(2)}, u32[]{:S(2)}) async-start(f32[16,128,128]{2,1,0:T(8,128)} %broadcast_in_dim.8), calls=%async_computation | async-start | bytes 2097152 | tf_op jit(solution)/shard_map/all_to_all | solution.py:230
  11.3 0.0 copy-done
  11.4 0.0 copy-done.1
  11.4 0.0 copy-done.2
  11.4 0.0 copy-done.3
  11.4 1.9 %gather.1 = (f32[6,32,256]{2,1,0:T(8,128)S(1)}, f32[6,32,256]{2,1,0:T(8,128)S(1)}, f32[24,256]{1,0:T(8,128)S(1)}, f32[24,256]{1,0:T(8,128)S(1)}, f32[8,128]{1,0:...) custom-call(f32[5,4,32,256]{3,2,1,0:T(8,128)S(1)} %copy-done, ...), custom_call_target="tpu_custom_call" | custom-call | tf_op jit(solution)/shard_map/gather/pallas_call | solution.py:236
  13.3 1.3 %collective-permute-start = (f32[6,32,256]{2,1,0:T(8,128)S(1)}, f32[6,32,256]{2,1,0:T(8,128)S(1)}, u32[]{:S(2)}, u32[]{:S(2)}) collective-permute-start(f32[6,32,256]{2,1,0:T(8,128)S(1)} %get-tuple-element.12), channel_id=1, source_target_pairs={{0,64},{64,128},{128,192},{192,0},{1,65},{65,129},{129,193},{193,1... | collective-permute-start | bytes 589832 | tf_op jit(solution)/shard_map/ppermute | solution.py:220
  14.5 0.0 copy-start.6
  14.5 0.8 %collective-permute-start.1 = (f32[6,32,256]{2,1,0:T(8,128)S(1)}, f32[6,32,256]{2,1,0:T(8,128)S(1)}, u32[]{:S(2)}, u32[]{:S(2)}) collective-permute-start(f32[6,32,256]{2,1,0:T(8,128)S(1)} %get-tuple-element.13), channel_id=1, source_target_pairs={{0,192},{64,0},{128,64},{192,128},{1,193},{65,1},{129,65},{193,129... | collective-permute-start | bytes 589832 | tf_op jit(solution)/shard_map/ppermute | solution.py:220
  15.4 0.0 collective-permute-start.2
  15.4 5.7 %collective-permute-start.3 = (f32[24,256]{1,0:T(8,128)S(1)}, f32[24,256]{1,0:T(8,128)S(1)}, u32[]{:S(2)}, u32[]{:S(2)}) collective-permute-start(f32[24,256]{1,0:T(8,128)S(1)} %get-tuple-element.15), channel_id=1, source_target_pairs={{0,48},{16,0},{32,16},{48,32},{1,49},{17,1},{33,17},{49,33},{2,50}... | collective-permute-start | bytes 73736 | tf_op jit(solution)/shard_map/ppermute | solution.py:220
  21.0 1.9 %collective-permute-start.4 = (f32[8,128]{1,0:T(8,128)S(1)}, f32[8,128]{1,0:T(8,128)S(1)}, u32[]{:S(2)}, u32[]{:S(2)}) collective-permute-start(f32[8,128]{1,0:T(8,128)S(1)} %get-tuple-element.16), channel_id=1, source_target_pairs={{0,1},{1,2},{2,3},{3,4},{4,5},{5,6},{6,7},{7,8},{8,9},{9,10},{10,1... | collective-permute-start | bytes 12296 | tf_op jit(solution)/shard_map/ppermute | solution.py:220
  22.9 12.7 %collective-permute-done.4.z_before = f32[8,128]{1,0:T(8,128)S(1)} collective-permute-done((f32[8,128]{1,0:T(8,128)S(1)}, f32[8,128]{1,0:T(8,128)S(1)}, u32[]{:S(2)}, u32[]{:S(2)}) %collective-permute-start.4) | collective-permute-done | bytes 4128 | tf_op jit(solution)/shard_map/ppermute | solution.py:220
  35.6 0.0 collective-permute-start.5
  35.6 0.0 copy-done.6
  35.6 0.1 copy.10.lift
  35.7 3.5 %collective-permute-done.5.z_after = f32[8,128]{1,0:T(8,128)S(1)} collective-permute-done((f32[8,128]{1,0:T(8,128)S(1)}, f32[8,128]{1,0:T(8,128)S(1)}, u32[]{:S(2)}, u32[]{:S(2)}) %collective-permute-start.5) | collective-permute-done | bytes 4128 | tf_op jit(solution)/shard_map/ppermute | solution.py:220
  39.2 0.0 collective-permute-done.2.y_before
  39.2 0.0 collective-permute-done.3.y_after
  39.2 0.0 collective-permute-done.x_before
  39.2 0.0 collective-permute-done.1.x_after
  39.2 0.0 copy-done.4
  39.2 0.0 copy-start.5
  39.3 2.0 %stencil.1.partial = f32[5,4,32,256]{3,2,1,0:T(8,128)S(1)} custom-call(f32[5,4,32,256]{3,2,1,0:T(8,128)S(1)} %copy-done, f32[4,32,256]{2,1,0:T(8,128)S(1)} %copy-done.1, f32[5,5]{1,0:T(8,128)S(1)} %copy-done.4, f32[6,32,256]{2,1,0:T(8,128)S(1)} %collective-permute-done.x_before, f32[6,32,256]{2,1,0:T(8,128)S(1)} %collective-permute-done.1.x_after, ...), custom_call_target="tpu_custom_call" | custom-call | tf_op jit(solution)/shard_map/stencil/pallas_call | solution.py:253
  41.3 0.0 all-to-all-done.inverse
  41.3 0.0 copy-done.5
  41.3 9.4 %solve.1 = (f32[5,4,32,256]{3,2,1,0:T(8,128)}, f32[5,1024]{1,0:T(8,128)}) custom-call(f32[16,128,128]{2,1,0:T(8,128)S(1)} %all-to-all-done.inverse, f32[16,8,128]{2,1,0:T(8,128)S(1)} %get-tuple-element.10.slots, f32[128,6]{1,0:T(8,128)S(1)} %copy.10.lift, f32[5,128]{1,0:T(8,128)S(1)} %copy-done.5, s32[1,1024]{1,0:T(1,128)S(1)} %bitcast.4, ...), custom_call_target="tpu_custom_call" | custom-call | tf_op jit(solution)/shard_map/solve/pallas_call | solution.py:271
  (1 shorter events, 0.0 us)
Async XLA Ops:
  2.6 8.8 %copy-start = (f32[5,4,32,256]{3,2,1,0:T(8,128)S(1)}, f32[5,4,32,256]{3,2,1,0:T(8,128)}, u32[]{:S(2)}) copy-start(f32[5,4,32,256]{3,2,1,0:T(8,128)} %adjoint.3) | copy-start | bytes 1966084
  2.6 8.8 %copy-start.1 = (f32[4,32,256]{2,1,0:T(8,128)S(1)}, f32[4,32,256]{2,1,0:T(8,128)}, u32[]{:S(2)}) copy-start(f32[4,32,256]{2,1,0:T(8,128)} %viscosity.3) | copy-start | bytes 393220
  2.6 8.8 %copy-start.2 = (s32[1024]{0:T(1024)S(1)}, s32[1024]{0:T(1024)}, u32[]{:S(2)}) copy-start(s32[1024]{0:T(1024)} %param.11) | copy-start | bytes 12292
  2.6 8.8 %copy-start.3 = (s32[1024,1]{0,1:T(1,128)S(1)}, s32[1024,1]{0,1:T(1,128)}, u32[]{:S(2)}) copy-start(s32[1024,1]{0,1:T(1,128)} %param.12) | copy-start | bytes 12292
  2.6 38.7 %all-to-all-start = ((f32[16,128,128]{2,1,0:T(8,128)}), f32[16,128,128]{2,1,0:T(8,128)S(1)}, u32[]{:S(2)}, u32[]{:S(2)}) async-start(f32[16,128,128]{2,1,0:T(8,128)} %broadcast_in_dim.8), calls=%async_computation | async-start | bytes 2097152 | tf_op jit(solution)/shard_map/all_to_all | solution.py:230
  13.3 26.0 %collective-permute-start = (f32[6,32,256]{2,1,0:T(8,128)S(1)}, f32[6,32,256]{2,1,0:T(8,128)S(1)}, u32[]{:S(2)}, u32[]{:S(2)}) collective-permute-start(f32[6,32,256]{2,1,0:T(8,128)S(1)} %get-tuple-element.12), channel_id=1, source_target_pairs={{0,64},{64,128},{128,192},{192,0},{1,65},{65,129},{129,193},{193,1... | collective-permute-start | bytes 589832 | tf_op jit(solution)/shard_map/ppermute | solution.py:220
  14.5 21.1 %copy-start.6 = (f32[128,6]{0,1:T(8,128)S(1)}, f32[128,6]{0,1:T(8,128)}, u32[]{:S(2)}) copy-start(f32[128,6]{0,1:T(8,128)} %param.14) | copy-start | bytes 9220
  14.5 24.7 %collective-permute-start.1 = (f32[6,32,256]{2,1,0:T(8,128)S(1)}, f32[6,32,256]{2,1,0:T(8,128)S(1)}, u32[]{:S(2)}, u32[]{:S(2)}) collective-permute-start(f32[6,32,256]{2,1,0:T(8,128)S(1)} %get-tuple-element.13), channel_id=1, source_target_pairs={{0,192},{64,0},{128,64},{192,128},{1,193},{65,1},{129,65},{193,129... | collective-permute-start | bytes 589832 | tf_op jit(solution)/shard_map/ppermute | solution.py:220
  15.4 23.8 %collective-permute-start.2 = (f32[24,256]{1,0:T(8,128)S(1)}, f32[24,256]{1,0:T(8,128)S(1)}, u32[]{:S(2)}, u32[]{:S(2)}) collective-permute-start(f32[24,256]{1,0:T(8,128)S(1)} %get-tuple-element.14), channel_id=1, source_target_pairs={{0,16},{16,32},{32,48},{48,0},{1,17},{17,33},{33,49},{49,1},{2,18}... | collective-permute-start | bytes 73736 | tf_op jit(solution)/shard_map/ppermute | solution.py:220
  15.4 23.8 %collective-permute-start.3 = (f32[24,256]{1,0:T(8,128)S(1)}, f32[24,256]{1,0:T(8,128)S(1)}, u32[]{:S(2)}, u32[]{:S(2)}) collective-permute-start(f32[24,256]{1,0:T(8,128)S(1)} %get-tuple-element.15), channel_id=1, source_target_pairs={{0,48},{16,0},{32,16},{48,32},{1,49},{17,1},{33,17},{49,33},{2,50}... | collective-permute-start | bytes 73736 | tf_op jit(solution)/shard_map/ppermute | solution.py:220
  21.0 14.6 %collective-permute-start.4 = (f32[8,128]{1,0:T(8,128)S(1)}, f32[8,128]{1,0:T(8,128)S(1)}, u32[]{:S(2)}, u32[]{:S(2)}) collective-permute-start(f32[8,128]{1,0:T(8,128)S(1)} %get-tuple-element.16), channel_id=1, source_target_pairs={{0,1},{1,2},{2,3},{3,4},{4,5},{5,6},{6,7},{7,8},{8,9},{9,10},{10,1... | collective-permute-start | bytes 12296 | tf_op jit(solution)/shard_map/ppermute | solution.py:220
  35.6 3.6 %copy-start.4 = (f32[5,5]{1,0:T(8,128)S(1)}, f32[5,5]{1,0:T(8,128)}, u32[]{:S(2)}) copy-start(f32[5,5]{1,0:T(8,128)} %jacobian.1) | copy-start | bytes 304
  35.6 3.6 %collective-permute-start.5 = (f32[8,128]{1,0:T(8,128)S(1)}, f32[8,128]{1,0:T(8,128)S(1)}, u32[]{:S(2)}, u32[]{:S(2)}) collective-permute-start(f32[8,128]{1,0:T(8,128)S(1)} %get-tuple-element.17), channel_id=1, source_target_pairs={{0,15},{1,0},{2,1},{3,2},{4,3},{5,4},{6,5},{7,6},{8,7},{9,8},{10,9... | collective-permute-start | bytes 12296 | tf_op jit(solution)/shard_map/ppermute | solution.py:220
  39.2 2.1 %copy-start.5 = (f32[5,128]{1,0:T(8,128)S(1)}, f32[5,128]{1,0:T(8,128)}, u32[]{:S(2)}) copy-start(f32[5,128]{1,0:T(8,128)} %readout.1) | copy-start | bytes 7684

commit v2 on v1

v2 whole, which is shorter than its diff:
```python
import functools

import jax
import jax.numpy as jnp
from jax import lax
from jax.experimental import pallas as pl
from jax.experimental.pallas import tpu as pltpu
from jax.sharding import PartitionSpec as P

CX = 4
CY = 32
CZ = 256
FACES = 1024
ROWS = CX * CY
PATCHES = 16
HALF = 8
CAP = 128
PROF = 128
ITERS = 6

time_step = 0.08

F32 = jnp.float32
BF16 = jnp.bfloat16
VMEM = pl.BlockSpec(memory_space=pltpu.VMEM)
HBM = pl.BlockSpec(memory_space=pltpu.HBM)
ANY = pl.BlockSpec(memory_space=pl.ANY)
SMEM = pl.BlockSpec(memory_space=pltpu.SMEM)
LONG = pl.CostEstimate(flops=20_000_000_000, bytes_accessed=60_000_000, transcendentals=0)
PARAMS = pltpu.CompilerParams(vmem_limit_bytes=48 * 1024 * 1024)


def split(x):
    high = x.astype(BF16)
    low = (x - high.astype(F32)).astype(BF16)
    return high, low


def dot(a, b):
    return jnp.dot(a, b, preferred_element_type=F32)


def dot_t(a, b):
    return lax.dot_general(a, b, (((1,), (1,)), ((), ())), preferred_element_type=F32)


def one_hot(count, index, dtype):
    numbers = lax.broadcasted_iota(jnp.int32, (count, index.shape[-1]), 0)
    return jnp.where(numbers == index, 1.0, 0.0).astype(dtype)


def parity(axis):
    return lax.axis_index(axis) & 1


def slot_group(patches):
    apart = patches ^ lax.axis_index("gz")
    return ((apart >> 1) & 1) * HALF + (apart & 1) * (HALF // 2) + (apart >> 2)


def load_kernel(
    adjoint_hbm,
    viscosity_hbm,
    cell_hbm,
    patch_hbm,
    inverse_hbm,
    adjoint,
    viscosity,
    cell,
    patch,
    inverse,
    x_one,
    x_two,
    y_one,
    y_two,
    arrivals,
):
    pairs = (
        (viscosity_hbm, viscosity),
        (adjoint_hbm, adjoint),
        (cell_hbm, cell),
        (patch_hbm, patch),
        (inverse_hbm, inverse),
    )
    copies = [
        pltpu.make_async_copy(source, target, arrivals.at[at])
        for at, (source, target) in enumerate(pairs)
    ]
    for copy in copies:
        copy.start()
    odd_x, odd_y = parity("gx"), parity("gy")
    x_first, x_second = (1 - odd_x) * (CX - 1), odd_x * (CX - 1)
    copies[0].wait()
    copies[1].wait()
    for f in range(6):
        field = viscosity if f == 5 else adjoint.at[f]
        x_one[f] = field[x_first]
        x_two[f] = field[x_second]
        for x in range(CX):
            low, high = field[x, 0:1, :], field[x, CY - 1 : CY, :]
            at = slice(f * CX + x, f * CX + x + 1)
            y_one[at, :] = jnp.where(odd_y == 1, low, high)
            y_two[at, :] = jnp.where(odd_y == 1, high, low)
    for copy in copies[2:]:
        copy.wait()


def gather_kernel(
    adjoint, viscosity, cell, patch, z_one, z_two, own, other, ranks
):
    odd_z = parity("gz")
    cells = cell[...]
    patches = slot_group(patch[...])
    row = cells >> 8
    span = cells & (CZ - 1)
    span_hot = one_hot(CZ, span, BF16)
    row_hot = lax.broadcasted_iota(jnp.int32, (ROWS, FACES), 0) == row
    columns = lax.broadcasted_iota(jnp.int32, (ROWS, 128), 1)
    z_low = z_high = jnp.zeros((ROWS, 128), F32)
    values = []
    for f in range(6):
        field = (viscosity[...] if f == 5 else adjoint[f]).reshape(ROWS, CZ)
        both = dot(jnp.concatenate(split(field), axis=0), span_hot)
        found = both[:ROWS] + both[ROWS:]
        values.append(jnp.sum(jnp.where(row_hot, found, 0.0), axis=0, keepdims=True))
        z_low = jnp.where(columns == f, field[:, 0:1], z_low)
        z_high = jnp.where(columns == f, field[:, CZ - 1 : CZ], z_high)
    z_low, z_high = jnp.transpose(z_low)[:8], jnp.transpose(z_high)[:8]
    z_one[...] = jnp.where(odd_z == 1, z_low, z_high)
    z_two[...] = jnp.where(odd_z == 1, z_high, z_low)

    hot = one_hot(PATCHES, patches, F32)
    pieces = FACES // 128
    stacked = jnp.concatenate([hot[:, b * 128 : (b + 1) * 128] for b in range(pieces)], axis=0)
    stacked = stacked.astype(BF16)
    upto = (
        lax.broadcasted_iota(jnp.int32, (128, 256), 0)
        <= lax.broadcasted_iota(jnp.int32, (128, 256), 1)
    )
    counts = dot(stacked, jnp.where(upto, 1.0, 0.0).astype(BF16))
    earlier = jnp.zeros((PATCHES, 128), F32)
    found_ranks = []
    for b in range(pieces):
        mine = slice(b * PATCHES, (b + 1) * PATCHES)
        piece = hot[:, b * 128 : (b + 1) * 128]
        found_ranks.append(
            jnp.sum(piece * (counts[mine, :128] + earlier), axis=0, keepdims=True) - 1.0
        )
        earlier = earlier + counts[mine, 128:]
    rank = jnp.concatenate(found_ranks, axis=1).astype(jnp.int32)
    ranks[...] = rank

    rank_hot = one_hot(CAP, rank, BF16)
    table = jnp.concatenate(values + [jnp.zeros((2, FACES), F32)], axis=0)
    high, low = split(table)
    both = jnp.concatenate([high.astype(F32), low.astype(F32)], axis=0)
    spread = jnp.concatenate(
        [jnp.where(patches == p, both, 0.0).astype(BF16) for p in range(PATCHES)], axis=0
    )
    placed = dot_t(spread, rank_hot).reshape(PATCHES, 16, CAP)
    slots = placed[:, :8] + placed[:, 8:]
    own[...] = slots[:HALF]
    other[...] = slots[HALF:]


def stencil_kernel(
    adjoint, viscosity, jacobian, x_one, x_two, y_one, y_two, z_one, after, out
):
    def sides(axis, one, two):
        odd = parity(axis) == 1
        return jnp.where(odd, one, two), jnp.where(odd, two, one)

    gx, gy = lax.axis_index("gx"), lax.axis_index("gy")
    has_before_x = jnp.where(gx > 0, 1.0, 0.0)
    has_after_x = jnp.where(gx < lax.axis_size("gx") - 1, 1.0, 0.0)
    has_before_y = jnp.where(gy > 0, 1.0, 0.0)
    has_after_y = jnp.where(gy < lax.axis_size("gy") - 1, 1.0, 0.0)
    y_before, y_after = sides("gy", y_one[...], y_two[...])
    y_before, y_after = y_before * has_before_y, y_after * has_after_y
    z_side = jnp.transpose(z_one[4 * PROF :, :])
    odd_z = parity("gz")

    def x_side(f, side):
        before, after = sides("gx", x_one[f], x_two[f])
        return after * has_after_x if side else before * has_before_x

    rows = lax.broadcasted_iota(jnp.int32, (CY, CZ), 0)
    lanes = lax.broadcasted_iota(jnp.int32, (CY, CZ), 1)
    def field_at(f, x):
        return viscosity[x] if f == 5 else adjoint[f, x]

    def neighbours(f, x):
        center = field_at(f, x)
        yield field_at(f, x - 1) if x > 0 else x_side(f, 0)
        yield field_at(f, x + 1) if x < CX - 1 else x_side(f, 1)
        at = slice(f * CX + x, f * CX + x + 1)
        yield jnp.where(rows == 0, y_before[at, :], pltpu.roll(center, 1, 0))
        yield jnp.where(
            rows == CY - 1, y_after[at, :], pltpu.roll(center, CY - 1, 0)
        )
        part = slice(x * CY, (x + 1) * CY)
        low, high = pltpu.roll(center, 1, 1), pltpu.roll(center, CZ - 1, 1)
        edge = z_side[part, f : f + 1]
        low = jnp.where((lanes == 0) & (odd_z == 1), edge, low)
        high = jnp.where((lanes == CZ - 1) & (odd_z == 0), edge, high)
        yield jnp.where((lanes == 0) & (odd_z == 0), center, low)
        yield jnp.where((lanes == CZ - 1) & (odd_z == 1), center, high)

    for x in range(CX):
        visc = viscosity[x]
        weights = [0.5 * (visc + other) for other in neighbours(5, x)]
        for f in range(5):
            center = adjoint[f, x]
            total = jnp.zeros((CY, CZ), F32)
            for weight, other in zip(weights, neighbours(f, x)):
                total = total + weight * (other - center)
            for g in range(5):
                total = total + jacobian[f, g] * adjoint[g, x]
            out[f, x] = center + time_step * total


def wide(matrix):
    high, low = split(matrix)
    return jnp.concatenate([high, low, high], axis=1)


def product(left, right):
    high, low = split(right)
    return dot(left, jnp.concatenate([high, high, low], axis=0))


def join_kernel(first, second, third, fourth, edge, before, joined):
    for at, block in enumerate((first, second, third, fourth)):
        joined[at * PROF : (at + 1) * PROF, :] = block[0]
    joined[4 * PROF :, :] = edge[...]


def solve_kernel(mine, theirs, own, arrived, lift, readout, solved_own, solved_arrived):
    inverse = [
        ref[at * PROF : (at + 1) * PROF, :] for ref in (mine, theirs) for at in range(HALF // 2)
    ]
    read = wide(jnp.concatenate([readout[...], jnp.zeros((3, PROF), F32)], axis=0))
    spread = wide(lift[...])
    inverses = [wide(inverse[p]) for p in range(HALF)]
    folded = [wide(product(read, inverse[p])) for p in range(HALF)]
    rows = [jnp.concatenate([own[p], arrived[p]], axis=1) for p in range(HALF)]
    forcing = [product(spread, r[:6]) for r in rows]
    damping = [0.5 * r[5:6] for r in rows]
    right = forcing
    for sweep in range(ITERS - 1):
        profile = [product(w, r) for w, r in zip(inverses, right)]
        right = [g - d * jnp.tanh(q) for g, d, q in zip(forcing, damping, profile)]
    for p in range(HALF):
        result = product(folded[p], right[p])
        solved_own[p] = result[:, :CAP]
        solved_arrived[p] = result[:, CAP:]


def scatter_kernel(
    solved_own,
    returned,
    cell,
    patch,
    ranks,
    partial,
    adjoint,
    viscosity,
    z_two,
    updated,
    shear,
):
    result = jnp.concatenate([solved_own[...], returned[...]], axis=0).reshape(PATCHES * 8, CAP)
    rank_hot = one_hot(CAP, ranks[...], BF16)
    back = dot(
        jnp.concatenate(split(result), axis=1), jnp.concatenate([rank_hot, rank_hot], axis=0)
    )
    patches = slot_group(patch[...])
    wall = jnp.zeros((8, FACES), F32)
    for p in range(PATCHES):
        wall = wall + jnp.where(patches == p, back[p * 8 : (p + 1) * 8], 0.0)
    shear[...] = wall[:5]

    side = jnp.transpose(z_two[...])
    lane = parity("gz") * (CZ - 1)
    lanes = lax.broadcasted_iota(jnp.int32, (ROWS, CZ), 1)
    visc = viscosity[...].reshape(ROWS, CZ)
    at_edge = jnp.where(lanes == lane, 0.5 * (visc + side[:, 5:6]), 0.0)
    cells = cell[...]
    span_hot = one_hot(CZ, cells & (CZ - 1), BF16)
    row_hot = lax.broadcasted_iota(jnp.int32, (ROWS, FACES), 0) == (cells >> 8)
    high = wall.astype(BF16).astype(F32)
    low = wall - high
    for f in range(5):
        spread = [jnp.where(row_hot, part[f : f + 1], 0.0).astype(BF16) for part in (high, low)]
        both = dot_t(jnp.concatenate(spread, axis=0), span_hot)
        source = both[:ROWS] + both[ROWS:]
        value = adjoint[f].reshape(ROWS, CZ)
        edge = at_edge * (side[:, f : f + 1] - value)
        updated[f] = partial[f] + (time_step * (source + edge)).reshape(CX, CY, CZ)


def swapped(array, axis, partner):
    return lax.ppermute(array, axis, [(i, partner(i)) for i in range(lax.axis_size(axis))])


def first_side(array, axis):
    return swapped(array, axis, lambda i: i ^ 1)


def second_side(array, axis):
    size = lax.axis_size(axis)
    return swapped(array, axis, lambda i: (i + 1 if i % 2 else i - 1) % size)


def shape(*dims, dtype=F32):
    return jax.ShapeDtypeStruct(dims, dtype)


def body(
    adjoint, viscosity, flux_jacobian, face_cell, face_patch, wall_inverse, lift_matrix, readout
):
    cell = face_cell.reshape(1, FACES)
    patch = face_patch.reshape(1, FACES)
    face_x, face_y, face_z = shape(6, CY, CZ), shape(6 * CX, CZ), shape(8, ROWS)
    slots, numbers = shape(HALF, 8, CAP), shape(1, FACES, dtype=jnp.int32)
    arrays = [adjoint, viscosity, cell, patch, wall_inverse]
    adjoint, viscosity, cell, patch, inverse, x_one, x_two, y_one, y_two = pl.pallas_call(
        load_kernel,
        out_shape=tuple(shape(*a.shape, dtype=a.dtype) for a in arrays)
        + (face_x, face_x, face_y, face_y),
        in_specs=[HBM] * 5,
        out_specs=[VMEM] * 9,
        scratch_shapes=[pltpu.SemaphoreType.DMA((5,))],
        compiler_params=PARAMS,
        name="load",
    )(*[pltpu.with_memory_space_constraint(a, pltpu.HBM) for a in arrays])
    blocks = [inverse]
    for step in range(1, 4):
        blocks.append(swapped(inverse, "gz", lambda i: i ^ (4 * step)))
    y_two = second_side(y_two, "gy")
    z_one, z_two, own, other, ranks = pl.pallas_call(
        gather_kernel,
        out_shape=(face_z, face_z, slots, slots, numbers),
        in_specs=[VMEM] * 4,
        out_specs=[VMEM] * 5,
        compiler_params=PARAMS,
        name="gather",
    )(adjoint, viscosity, cell, patch)
    arrived = swapped(other, "gz", lambda i: i ^ 2)
    mine = pl.pallas_call(
        join_kernel,
        out_shape=shape(4 * PROF + 8, PROF),
        in_specs=[VMEM] * 5 + [ANY],
        out_specs=VMEM,
        compiler_params=PARAMS,
        name="join",
    )(*blocks, z_one, y_two)
    theirs = swapped(mine, "gz", lambda i: i ^ 1)
    solved_own, solved_arrived = pl.pallas_call(
        solve_kernel,
        out_shape=(slots, slots),
        in_specs=[VMEM] * 6,
        out_specs=[VMEM] * 2,
        compiler_params=PARAMS,
        cost_estimate=LONG,
        name="solve",
    )(mine, theirs, own, arrived, lift_matrix, readout)
    returned = swapped(solved_arrived, "gz", lambda i: i ^ 2)
    partial = pl.pallas_call(
        stencil_kernel,
        out_shape=shape(5, CX, CY, CZ),
        in_specs=[VMEM, VMEM, SMEM] + [VMEM] * 5 + [ANY],
        out_specs=VMEM,
        compiler_params=PARAMS,
        cost_estimate=LONG,
        name="stencil",
    )(
        adjoint,
        viscosity,
        flux_jacobian,
        first_side(x_one, "gx"),
        second_side(x_two, "gx"),
        first_side(y_one, "gy"),
        y_two,
        theirs,
        solved_own,
    )
    return pl.pallas_call(
        scatter_kernel,
        out_shape=(shape(5, CX, CY, CZ), shape(5, FACES)),
        in_specs=[VMEM] * 9,
        out_specs=[VMEM] * 2,
        compiler_params=PARAMS,
        name="scatter",
    )(
        solved_own,
        returned,
        cell,
        patch,
        ranks,
        partial,
        adjoint,
        viscosity,
        second_side(z_two, "gz"),
    )


def solution(mesh):
    in_specs = (
        P(None, "gx", "gy", "gz"),
        P("gx", "gy", "gz"),
        P(),
        P(("gx", "gy", "gz")),
        P(("gx", "gy", "gz"), None),
        P(("gx", "gy", "gz"), None, None),
        P(),
        P(),
    )
    out_specs = (P(None, "gx", "gy", "gz"), P(None, ("gx", "gy", "gz")))
    return jax.shard_map(body, mesh=mesh, in_specs=in_specs, out_specs=out_specs, check_vma=False)
```

time: 51 us -> 35.8 us (0.70)
  the two profiles are of different devices: /device:TPU:4 before, /device:TPU:40 now
where the time goes in v2:
time: 35.8 us; the launch traced here: 35.7 us
  starting transfers between devices  17.3 us (48%)
  waiting for transfers between devices  8.99 us (25%)
  Pallas kernels  8.61 us (24%)
  between operations  0.71 us (2%)
    ppermute x11, starting transfers between devices, swapped(): lax.ppermute(array, axis, [(i, partner(i)) for i in range(lax.axis_size(a...  17.3 us
    ppermute x11, waiting for transfers between devices, swapped(): lax.ppermute(array, axis, [(i, partner(i)) for i in range(lax.axis_size(a...  8.99 us
    pallas_call x1, Pallas kernels, body(): pl.pallas_call(solve_kernel, out_shape=(slots, slots), in_specs=[VMEM] *...  2.05 us
    pallas_call x1, Pallas kernels, body(): pl.pallas_call(scatter_kernel, out_shape=(shape(5, CX, CY, CZ), shape(5,...  1.93 us
    pallas_call x1, Pallas kernels, body(): pl.pallas_call(stencil_kernel, out_shape=shape(5, CX, CY, CZ), in_specs=[...  1.85 us
    pallas_call x1, Pallas kernels, body(): pl.pallas_call(gather_kernel, out_shape=(face_z, face_z, slots, slots, nu...  1.49 us
    pallas_call x1, Pallas kernels, body(): pl.pallas_call(load_kernel, out_shape=tuple((shape(*a.shape, dtype=a.dtyp...  1.26 us
  transfers between devices with their start and end apart: 11, of which 4 were waited for; matrix products, arithmetic and copies ran while one was open for 0% of the time, Pallas kernels for 15%

profile of v2, /device:TPU:40, one launch (start us, length us, event | category | flops | bytes accessed | tf_op | source)
XLA Modules:
  0.0 35.7 jit_solution(2403621028270316829)
XLA Ops:
  0.6 1.3 %load.1 = (f32[5,4,32,256]{3,2,1,0:T(8,128)S(1)}, f32[4,32,256]{2,1,0:T(8,128)S(1)}, s32[1,1024]{1,0:T(1,128)S(1)}, s32[1,1024]{1,0:T(1,128)S(1)}, f32[1,128,128...) custom-call(f32[5,4,32,256]{3,2,1,0:T(8,128)} %adjoint_hbm.1, ...), custom_call_target="tpu_custom_call" | custom-call | tf_op jit(solution)/shard_map/load/pallas_call | solution.py:327
  1.9 1.7 %collective-permute-start.2 = (f32[1,128,128]{2,1,0:T(8,128)S(1)}, f32[1,128,128]{2,1,0:T(8,128)S(1)}, u32[]{:S(2)}, u32[]{:S(2)}) collective-permute-start(f32[1,128,128]{2,1,0:T(8,128)S(1)} %get-tuple-element.18.first), channel_id=1, source_target_pairs={{0,12},{1,13},{2,14},{3,15},{4,8},{5,9},{6,10},{7,11},{8,4},{9,5},... | collective-permute-start | bytes 196616 | tf_op jit(solution)/shard_map/ppermute | solution.py:303
  3.6 0.9 %collective-permute-start.1 = (f32[1,128,128]{2,1,0:T(8,128)S(1)}, f32[1,128,128]{2,1,0:T(8,128)S(1)}, u32[]{:S(2)}, u32[]{:S(2)}) collective-permute-start(f32[1,128,128]{2,1,0:T(8,128)S(1)} %get-tuple-element.18.first), channel_id=1, source_target_pairs={{0,8},{1,9},{2,10},{3,11},{4,12},{5,13},{6,14},{7,15},{8,0},{9,1},... | collective-permute-start | bytes 196616 | tf_op jit(solution)/shard_map/ppermute | solution.py:303
  4.5 1.6 %collective-permute-start = (f32[1,128,128]{2,1,0:T(8,128)S(1)}, f32[1,128,128]{2,1,0:T(8,128)S(1)}, u32[]{:S(2)}, u32[]{:S(2)}) collective-permute-start(f32[1,128,128]{2,1,0:T(8,128)S(1)} %get-tuple-element.18.first), channel_id=1, source_target_pairs={{0,4},{1,5},{2,6},{3,7},{4,0},{5,1},{6,2},{7,3},{8,12},{9,13},{10,... | collective-permute-start | bytes 196616 | tf_op jit(solution)/shard_map/ppermute | solution.py:303
  6.1 4.9 %collective-permute-start.3 = (f32[24,256]{1,0:T(8,128)S(1)}, f32[24,256]{1,0:T(8,128)S(1)}, u32[]{:S(2)}, u32[]{:S(2)}) collective-permute-start(f32[24,256]{1,0:T(8,128)S(1)} %get-tuple-element.24), channel_id=1, source_target_pairs={{0,48},{16,32},{32,16},{48,0},{1,49},{17,33},{33,17},{49,1},{2,50}... | collective-permute-start | bytes 73736 | tf_op jit(solution)/shard_map/ppermute | solution.py:303
  11.0 1.5 %gather.1 = (f32[8,128]{1,0:T(8,128)S(1)}, f32[8,128]{1,0:T(8,128)S(1)}, f32[8,8,128]{2,1,0:T(8,128)S(1)}, f32[8,8,128]{2,1,0:T(8,128)S(1)}, s32[1,1024]{1,0:T(1,128)S(1)}) custom-call(f32[5,4,32,256]{3,2,1,0:T(8,128)S(1)} %get-tuple-element.19.adjoint, f32[4,32,256]{2,1,0:T(8,128)S(1)} %get-tuple-element.20.viscosity, ...), custom_call_target="tpu_custom_call" | custom-call | tf_op jit(solution)/shard_map/gather/pallas_call | solution.py:341
  12.5 0.8 %collective-permute-done.3.before.y_two = f32[24,256]{1,0:T(8,128)S(1)} collective-permute-done((f32[24,256]{1,0:T(8,128)S(1)}, f32[24,256]{1,0:T(8,128)S(1)}, u32[]{:S(2)}, u32[]{:S(2)}) %collective-permute-start.3) | collective-permute-done | bytes 24608 | tf_op jit(solution)/shard_map/ppermute | solution.py:303
  13.2 0.0 collective-permute-done.2.fourth
  13.2 0.0 collective-permute-done.1.third
  13.2 0.0 collective-permute-done.second
  13.3 0.0 copy-start.2
  13.3 0.6 %collective-permute-start.4 = (f32[520,128]{1,0:T(8,128)S(1)}, f32[520,128]{1,0:T(8,128)S(1)}, u32[]{:S(2)}, u32[]{:S(2)}) collective-permute-start(f32[520,128]{1,0:T(8,128)S(1)} %join.1.mine), channel_id=1, source_target_pairs={{0,1},{1,0},{2,3},{3,2},{4,5},{5,4},{6,7},{7,6},{8,9},{9,8},{10,11... | collective-permute-start | bytes 798728 | tf_op jit(solution)/shard_map/ppermute | solution.py:303
  13.9 3.1 %collective-permute-start.5 = (f32[8,8,128]{2,1,0:T(8,128)S(1)}, f32[8,8,128]{2,1,0:T(8,128)S(1)}, u32[]{:S(2)}, u32[]{:S(2)}) collective-permute-start(f32[8,8,128]{2,1,0:T(8,128)S(1)} %get-tuple-element.26), channel_id=1, source_target_pairs={{0,2},{1,3},{2,0},{3,1},{4,6},{5,7},{6,4},{7,5},{8,10},{9,11},{10,... | collective-permute-start | bytes 98312 | tf_op jit(solution)/shard_map/ppermute | solution.py:303
  17.0 0.0 collective-permute-start.9
  17.0 0.2 collective-permute-start.10
  17.2 1.5 %collective-permute-start.7 = (f32[6,32,256]{2,1,0:T(8,128)S(1)}, f32[6,32,256]{2,1,0:T(8,128)S(1)}, u32[]{:S(2)}, u32[]{:S(2)}) collective-permute-start(f32[6,32,256]{2,1,0:T(8,128)S(1)} %get-tuple-element.30), channel_id=1, source_target_pairs={{0,64},{64,0},{128,192},{192,128},{1,65},{65,1},{129,193},{193,129... | collective-permute-start | bytes 589832 | tf_op jit(solution)/shard_map/ppermute | solution.py:303
  18.7 0.0 copy-done.2
  18.7 0.1 copy.10.lift
  18.8 5.3 %collective-permute-done.5.arrived = f32[8,8,128]{2,1,0:T(8,128)S(1)} collective-permute-done((f32[8,8,128]{2,1,0:T(8,128)S(1)}, f32[8,8,128]{2,1,0:T(8,128)S(1)}, u32[]{:S(2)}, u32[]{:S(2)}) %collective-permute-start.5) | collective-permute-done | bytes 32800 | tf_op jit(solution)/shard_map/ppermute | solution.py:303
  24.1 2.8 %collective-permute-start.8 = (f32[6,32,256]{2,1,0:T(8,128)S(1)}, f32[6,32,256]{2,1,0:T(8,128)S(1)}, u32[]{:S(2)}, u32[]{:S(2)}) collective-permute-start(f32[6,32,256]{2,1,0:T(8,128)S(1)} %get-tuple-element.31), channel_id=1, source_target_pairs={{0,192},{64,128},{128,64},{192,0},{1,193},{65,129},{129,65},{193,1... | collective-permute-start | bytes 589832 | tf_op jit(solution)/shard_map/ppermute | solution.py:303
  26.9 0.0 collective-permute-done.4.theirs.z_one
  26.9 0.0 copy-done
  26.9 2.1 %solve.1 = (f32[8,8,128]{2,1,0:T(8,128)S(1)}, f32[8,8,128]{2,1,0:T(8,128)S(1)}) custom-call(f32[520,128]{1,0:T(8,128)S(1)} %join.1.mine, f32[520,128]{1,0:T(8,128)S(1)} %collective-permute-done.4.theirs.z_one, f32[8,8,128]{2,1,0:T(8,128)S(1)} %get-tuple-element.25.own, f32[8,8,128]{2,1,0:T(8,128)S(1)} %collective-permute-done.5.arrived, ...), custom_call_target="tpu_custom_call" | custom-call | flops 20000000000 | bytes 60000000 | tf_op jit(solution)/shard_map/solve/pallas_call | solution.py:359
  28.9 0.0 collective-permute-start.6
  29.0 0.0 collective-permute-done.9.y_one
  29.0 0.0 collective-permute-done.7.x_one
  29.0 2.0 %collective-permute-done.8.x_two = f32[6,32,256]{2,1,0:T(8,128)S(1)} collective-permute-done((f32[6,32,256]{2,1,0:T(8,128)S(1)}, f32[6,32,256]{2,1,0:T(8,128)S(1)}, u32[]{:S(2)}, u32[]{:S(2)}) %collective-permute-start.8) | collective-permute-done | bytes 196640 | tf_op jit(solution)/shard_map/ppermute | solution.py:303
  31.0 0.0 copy-done.1
  31.0 1.8 %stencil.1.partial = f32[5,4,32,256]{3,2,1,0:T(8,128)S(1)} custom-call(f32[5,4,32,256]{3,2,1,0:T(8,128)S(1)} %get-tuple-element.19.adjoint, f32[4,32,256]{2,1,0:T(8,128)S(1)} %get-tuple-element.20.viscosity, f32[5,5]{1,0:T(8,128)S(1)} %copy-done.1, f32[6,32,256]{2,1,0:T(8,128)S(1)} %collective-permute-done.7.x_one, ...), custom_call_target="tpu_custom_call" | custom-call | flops 20000000000 | bytes 60000000 | tf_op jit(solution)/shard_map/stencil/pallas_call | solution.py:369
  32.9 0.0 collective-permute-done.10.z_two
  32.9 0.9 %collective-permute-done.6.returned = f32[8,8,128]{2,1,0:T(8,128)S(1)} collective-permute-done((f32[8,8,128]{2,1,0:T(8,128)S(1)}, f32[8,8,128]{2,1,0:T(8,128)S(1)}, u32[]{:S(2)}, u32[]{:S(2)}) %collective-permute-start.6) | collective-permute-done | bytes 32800 | tf_op jit(solution)/shard_map/ppermute | solution.py:303
  33.8 1.9 %scatter.1 = (f32[5,4,32,256]{3,2,1,0:T(8,128)}, f32[5,1024]{1,0:T(8,128)}) custom-call(f32[8,8,128]{2,1,0:T(8,128)S(1)} %get-tuple-element.27.after.solved_own, f32[8,8,128]{2,1,0:T(8,128)S(1)} %collective-permute-done.6.returned, s32[1,1024]{1,0:T(1,128)S(1)} %get-tuple-element.21.cell, s32[1,1024]{1,0:T(1,128)S(1)} %get-tuple-element.22.patch, ...), custom_call_target="tpu_custom_call" | custom-call | tf_op jit(solution)/shard_map/scatter/pallas_call | solution.py:388
  (3 shorter events, 0.0 us)
Async XLA Ops:
  1.9 11.3 %collective-permute-start.2 = (f32[1,128,128]{2,1,0:T(8,128)S(1)}, f32[1,128,128]{2,1,0:T(8,128)S(1)}, u32[]{:S(2)}, u32[]{:S(2)}) collective-permute-start(f32[1,128,128]{2,1,0:T(8,128)S(1)} %get-tuple-element.18.first), channel_id=1, source_target_pairs={{0,12},{1,13},{2,14},{3,15},{4,8},{5,9},{6,10},{7,11},{8,4},{9,5},... | collective-permute-start | bytes 196616 | tf_op jit(solution)/shard_map/ppermute | solution.py:303
  3.6 9.7 %collective-permute-start.1 = (f32[1,128,128]{2,1,0:T(8,128)S(1)}, f32[1,128,128]{2,1,0:T(8,128)S(1)}, u32[]{:S(2)}, u32[]{:S(2)}) collective-permute-start(f32[1,128,128]{2,1,0:T(8,128)S(1)} %get-tuple-element.18.first), channel_id=1, source_target_pairs={{0,8},{1,9},{2,10},{3,11},{4,12},{5,13},{6,14},{7,15},{8,0},{9,1},... | collective-permute-start | bytes 196616 | tf_op jit(solution)/shard_map/ppermute | solution.py:303
  4.5 8.7 %collective-permute-start = (f32[1,128,128]{2,1,0:T(8,128)S(1)}, f32[1,128,128]{2,1,0:T(8,128)S(1)}, u32[]{:S(2)}, u32[]{:S(2)}) collective-permute-start(f32[1,128,128]{2,1,0:T(8,128)S(1)} %get-tuple-element.18.first), channel_id=1, source_target_pairs={{0,4},{1,5},{2,6},{3,7},{4,0},{5,1},{6,2},{7,3},{8,12},{9,13},{10,... | collective-permute-start | bytes 196616 | tf_op jit(solution)/shard_map/ppermute | solution.py:303
  6.1 7.2 %collective-permute-start.3 = (f32[24,256]{1,0:T(8,128)S(1)}, f32[24,256]{1,0:T(8,128)S(1)}, u32[]{:S(2)}, u32[]{:S(2)}) collective-permute-start(f32[24,256]{1,0:T(8,128)S(1)} %get-tuple-element.24), channel_id=1, source_target_pairs={{0,48},{16,32},{32,16},{48,0},{1,49},{17,33},{33,17},{49,1},{2,50}... | collective-permute-start | bytes 73736 | tf_op jit(solution)/shard_map/ppermute | solution.py:303
  13.3 5.4 %copy-start.2 = (f32[128,6]{0,1:T(8,128)S(1)}, f32[128,6]{0,1:T(8,128)}, u32[]{:S(2)}) copy-start(f32[128,6]{0,1:T(8,128)} %param.14) | copy-start | bytes 9220
  13.3 13.6 %collective-permute-start.4 = (f32[520,128]{1,0:T(8,128)S(1)}, f32[520,128]{1,0:T(8,128)S(1)}, u32[]{:S(2)}, u32[]{:S(2)}) collective-permute-start(f32[520,128]{1,0:T(8,128)S(1)} %join.1.mine), channel_id=1, source_target_pairs={{0,1},{1,0},{2,3},{3,2},{4,5},{5,4},{6,7},{7,6},{8,9},{9,8},{10,11... | collective-permute-start | bytes 798728 | tf_op jit(solution)/shard_map/ppermute | solution.py:303
  13.9 10.2 %collective-permute-start.5 = (f32[8,8,128]{2,1,0:T(8,128)S(1)}, f32[8,8,128]{2,1,0:T(8,128)S(1)}, u32[]{:S(2)}, u32[]{:S(2)}) collective-permute-start(f32[8,8,128]{2,1,0:T(8,128)S(1)} %get-tuple-element.26), channel_id=1, source_target_pairs={{0,2},{1,3},{2,0},{3,1},{4,6},{5,7},{6,4},{7,5},{8,10},{9,11},{10,... | collective-permute-start | bytes 98312 | tf_op jit(solution)/shard_map/ppermute | solution.py:303
  17.0 12.0 %collective-permute-start.9 = (f32[24,256]{1,0:T(8,128)S(1)}, f32[24,256]{1,0:T(8,128)S(1)}, u32[]{:S(2)}, u32[]{:S(2)}) collective-permute-start(f32[24,256]{1,0:T(8,128)S(1)} %get-tuple-element.32), channel_id=1, source_target_pairs={{0,16},{16,0},{32,48},{48,32},{1,17},{17,1},{33,49},{49,33},{2,18}... | collective-permute-start | bytes 73736 | tf_op jit(solution)/shard_map/ppermute | solution.py:303
  17.0 15.9 %collective-permute-start.10 = (f32[8,128]{1,0:T(8,128)S(1)}, f32[8,128]{1,0:T(8,128)S(1)}, u32[]{:S(2)}, u32[]{:S(2)}) collective-permute-start(f32[8,128]{1,0:T(8,128)S(1)} %get-tuple-element.33), channel_id=1, source_target_pairs={{0,15},{1,2},{2,1},{3,4},{4,3},{5,6},{6,5},{7,8},{8,7},{9,10},{10,... | collective-permute-start | bytes 12296 | tf_op jit(solution)/shard_map/ppermute | solution.py:303
  17.2 9.7 %copy-start = (f32[5,128]{1,0:T(8,128)S(1)}, f32[5,128]{1,0:T(8,128)}, u32[]{:S(2)}) copy-start(f32[5,128]{1,0:T(8,128)} %readout.1) | copy-start | bytes 7684
  17.2 11.8 %collective-permute-start.7 = (f32[6,32,256]{2,1,0:T(8,128)S(1)}, f32[6,32,256]{2,1,0:T(8,128)S(1)}, u32[]{:S(2)}, u32[]{:S(2)}) collective-permute-start(f32[6,32,256]{2,1,0:T(8,128)S(1)} %get-tuple-element.30), channel_id=1, source_target_pairs={{0,64},{64,0},{128,192},{192,128},{1,65},{65,1},{129,193},{193,129... | collective-permute-start | bytes 589832 | tf_op jit(solution)/shard_map/ppermute | solution.py:303
  24.1 6.9 %collective-permute-start.8 = (f32[6,32,256]{2,1,0:T(8,128)S(1)}, f32[6,32,256]{2,1,0:T(8,128)S(1)}, u32[]{:S(2)}, u32[]{:S(2)}) collective-permute-start(f32[6,32,256]{2,1,0:T(8,128)S(1)} %get-tuple-element.31), channel_id=1, source_target_pairs={{0,192},{64,128},{128,64},{192,0},{1,193},{65,129},{129,65},{193,1... | collective-permute-start | bytes 589832 | tf_op jit(solution)/shard_map/ppermute | solution.py:303
  26.9 4.2 %copy-start.1 = (f32[5,5]{1,0:T(8,128)S(1)}, f32[5,5]{1,0:T(8,128)}, u32[]{:S(2)}) copy-start(f32[5,5]{1,0:T(8,128)} %jacobian.1) | copy-start | bytes 304
  28.9 4.8 %collective-permute-start.6 = (f32[8,8,128]{2,1,0:T(8,128)S(1)}, f32[8,8,128]{2,1,0:T(8,128)S(1)}, u32[]{:S(2)}, u32[]{:S(2)}) collective-permute-start(f32[8,8,128]{2,1,0:T(8,128)S(1)} %get-tuple-element.28), channel_id=1, source_target_pairs={{0,2},{1,3},{2,0},{3,1},{4,6},{5,7},{6,4},{7,5},{8,10},{9,11},{10,... | collective-permute-start | bytes 98312 | tf_op jit(solution)/shard_map/ppermute | solution.py:303

commit v3 on v2

--- a/solution.py
+++ b/solution.py
@@ -68,11 +68,9 @@
     viscosity,
     cell,
     patch,
-    inverse,
-    x_one,
-    x_two,
+    package,
     y_one,
-    y_two,
+    z_one,
     arrivals,
 ):
     pairs = (
@@ -80,7 +78,7 @@
         (adjoint_hbm, adjoint),
         (cell_hbm, cell),
         (patch_hbm, patch),
-        (inverse_hbm, inverse),
+        (inverse_hbm, package.at[:, :PROF]),
     )
     copies = [
         pltpu.make_async_copy(source, target, arrivals.at[at])
@@ -88,46 +86,88 @@
     ]
     for copy in copies:
         copy.start()
-    odd_x, odd_y = parity("gx"), parity("gy")
-    x_first, x_second = (1 - odd_x) * (CX - 1), odd_x * (CX - 1)
     copies[0].wait()
     copies[1].wait()
+    odd_y = parity("gy")
+    for f in range(6):
+        field = viscosity if f == 5 else adjoint.at[f]
+        for x in range(CX):
+            low, high = field[x, 0:1, :], field[x, CY - 1 : CY, :]
+            at = slice(f * CX + x, f * CX + x + 1)
+            y_one[at, :] = jnp.where(odd_y == 1, low, high)
+    columns = lax.broadcasted_iota(jnp.int32, (ROWS, 128), 1)
+    z_low = z_high = jnp.zeros((ROWS, 128), F32)
+    for f in range(6):
+        field = (viscosity[...] if f == 5 else adjoint[f]).reshape(ROWS, CZ)
+        z_low = jnp.where(columns == f, field[:, 0:1], z_low)
+        z_high = jnp.where(columns == f, field[:, CZ - 1 : CZ], z_high)
+    z_low, z_high = jnp.transpose(z_low)[:8], jnp.transpose(z_high)[:8]
+    odd_z = parity("gz") == 1
+    z_one[...] = jnp.where(odd_z, z_low, z_high)
+    package[0, PROF:, :] = jnp.where(odd_z, z_high, z_low)
+    for copy in copies[2:]:
+        copy.wait()
+
+
+def early_kernel(
+    adjoint, viscosity, cell, patch, before, joined, y_two, own, other, ranks
+):
+    odd_y = parity("gy")
+    for f in range(6):
+        field = viscosity if f == 5 else adjoint.at[f]
+        for x in range(CX):
+            low, high = field[x, 0:1, :], field[x, CY - 1 : CY, :]
+            at = slice(f * CX + x, f * CX + x + 1)
+            y_two[at, :] = jnp.where(odd_y == 1, high, low)
+    results = (own, other, ranks)
+    near = lax.axis_index("gy") < lax.axis_size("gy") // 2
+
+    @pl.when(near)
+    def _():
+        gather(adjoint, viscosity, cell, patch, *results)
+
+    @pl.when(jnp.logical_not(near))
+    def _():
+        for ref in results:
+            ref[...] = jnp.zeros(ref.shape, ref.dtype)
+
+
+def late_kernel(adjoint, viscosity, cell, patch, *refs):
+    near = lax.axis_index("gy") < lax.axis_size("gy") // 2
+
+    @pl.when(near)
+    def _():
+        for found, result in zip(refs[:3], refs[3:]):
+            result[...] = found[...]
+
+    @pl.when(jnp.logical_not(near))
+    def _():
+        gather(adjoint, viscosity, cell, patch, *refs[3:])
+
+
+def faces_kernel(adjoint, viscosity, rows, before, x_one, x_two, sent):
+    sent[...] = rows[...]
+    odd_x = parity("gx")
+    x_first, x_second = (1 - odd_x) * (CX - 1), odd_x * (CX - 1)
     for f in range(6):
         field = viscosity if f == 5 else adjoint.at[f]
         x_one[f] = field[x_first]
         x_two[f] = field[x_second]
-        for x in range(CX):
-            low, high = field[x, 0:1, :], field[x, CY - 1 : CY, :]
-            at = slice(f * CX + x, f * CX + x + 1)
-            y_one[at, :] = jnp.where(odd_y == 1, low, high)
-            y_two[at, :] = jnp.where(odd_y == 1, high, low)
-    for copy in copies[2:]:
-        copy.wait()
-
-
-def gather_kernel(
-    adjoint, viscosity, cell, patch, z_one, z_two, own, other, ranks
-):
-    odd_z = parity("gz")
+
+
+def gather(adjoint, viscosity, cell, patch, own, other, ranks):
     cells = cell[...]
     patches = slot_group(patch[...])
     row = cells >> 8
     span = cells & (CZ - 1)
     span_hot = one_hot(CZ, span, BF16)
     row_hot = lax.broadcasted_iota(jnp.int32, (ROWS, FACES), 0) == row
-    columns = lax.broadcasted_iota(jnp.int32, (ROWS, 128), 1)
-    z_low = z_high = jnp.zeros((ROWS, 128), F32)
     values = []
     for f in range(6):
         field = (viscosity[...] if f == 5 else adjoint[f]).reshape(ROWS, CZ)
         both = dot(jnp.concatenate(split(field), axis=0), span_hot)
         found = both[:ROWS] + both[ROWS:]
         values.append(jnp.sum(jnp.where(row_hot, found, 0.0), axis=0, keepdims=True))
-        z_low = jnp.where(columns == f, field[:, 0:1], z_low)
-        z_high = jnp.where(columns == f, field[:, CZ - 1 : CZ], z_high)
-    z_low, z_high = jnp.transpose(z_low)[:8], jnp.transpose(z_high)[:8]
-    z_one[...] = jnp.where(odd_z == 1, z_low, z_high)
-    z_two[...] = jnp.where(odd_z == 1, z_high, z_low)
 
     hot = one_hot(PATCHES, patches, F32)
     pieces = FACES // 128
@@ -159,8 +199,9 @@
     )
     placed = dot_t(spread, rank_hot).reshape(PATCHES, 16, CAP)
     slots = placed[:, :8] + placed[:, 8:]
-    own[...] = slots[:HALF]
-    other[...] = slots[HALF:]
+    for p in range(HALF):
+        own[p * 6 : (p + 1) * 6, :] = slots[p, :6]
+        other[p * 6 : (p + 1) * 6, :] = slots[HALF + p, :6]
 
 
 def stencil_kernel(
@@ -177,7 +218,7 @@
     has_after_y = jnp.where(gy < lax.axis_size("gy") - 1, 1.0, 0.0)
     y_before, y_after = sides("gy", y_one[...], y_two[...])
     y_before, y_after = y_before * has_before_y, y_after * has_after_y
-    z_side = jnp.transpose(z_one[4 * PROF :, :])
+    z_side = jnp.transpose(z_one[4 * PROF : 4 * PROF + 8, :])
     odd_z = parity("gz")
 
     def x_side(f, side):
@@ -229,13 +270,19 @@
     return dot(left, jnp.concatenate([high, high, low], axis=0))
 
 
-def join_kernel(first, second, third, fourth, edge, before, joined):
+def join_kernel(first, second, third, fourth, edge, joined):
     for at, block in enumerate((first, second, third, fourth)):
-        joined[at * PROF : (at + 1) * PROF, :] = block[0]
-    joined[4 * PROF :, :] = edge[...]
-
-
-def solve_kernel(mine, theirs, own, arrived, lift, readout, solved_own, solved_arrived):
+        joined[at * PROF : (at + 1) * PROF, :] = block[0, :PROF, :]
+    place = lax.axis_index("gz")
+    inner = (place ^ (place >> 1)) & 1 == 1
+    nearer = (place >> 2) & 1 == (place >> 1) & 1
+    passed = jnp.where(nearer, second[0, PROF:, :], fourth[0, PROF:, :])
+    joined[4 * PROF : 4 * PROF + 8, :] = edge[...]
+    joined[4 * PROF + 8 :, :] = jnp.where(inner, first[0, PROF:, :], passed)
+
+
+def solve_kernel(mine, theirs, rows, lift, readout, *refs):
+    solved = refs[-1]
     inverse = [
         ref[at * PROF : (at + 1) * PROF, :] for ref in (mine, theirs) for at in range(HALF // 2)
     ]
@@ -243,8 +290,8 @@
     spread = wide(lift[...])
     inverses = [wide(inverse[p]) for p in range(HALF)]
     folded = [wide(product(read, inverse[p])) for p in range(HALF)]
-    rows = [jnp.concatenate([own[p], arrived[p]], axis=1) for p in range(HALF)]
-    forcing = [product(spread, r[:6]) for r in rows]
+    rows = [rows[p * 6 : (p + 1) * 6, :] for p in range(HALF)]
+    forcing = [product(spread, r) for r in rows]
     damping = [0.5 * r[5:6] for r in rows]
     right = forcing
     for sweep in range(ITERS - 1):
@@ -252,8 +299,9 @@
         right = [g - d * jnp.tanh(q) for g, d, q in zip(forcing, damping, profile)]
     for p in range(HALF):
         result = product(folded[p], right[p])
-        solved_own[p] = result[:, :CAP]
-        solved_arrived[p] = result[:, CAP:]
+        for f in range(5):
+            solved[f * HALF + p : f * HALF + p + 1, :] = result[f : f + 1]
+    solved[5 * HALF :, :] = theirs[4 * PROF + 8 :, :]
 
 
 def scatter_kernel(
@@ -265,22 +313,27 @@
     partial,
     adjoint,
     viscosity,
-    z_two,
     updated,
     shear,
 ):
-    result = jnp.concatenate([solved_own[...], returned[...]], axis=0).reshape(PATCHES * 8, CAP)
+    parts = (solved_own[: 5 * HALF, :], returned[: 5 * HALF, :])
+    result = jnp.concatenate(parts, axis=0)
     rank_hot = one_hot(CAP, ranks[...], BF16)
     back = dot(
         jnp.concatenate(split(result), axis=1), jnp.concatenate([rank_hot, rank_hot], axis=0)
     )
     patches = slot_group(patch[...])
-    wall = jnp.zeros((8, FACES), F32)
-    for p in range(PATCHES):
-        wall = wall + jnp.where(patches == p, back[p * 8 : (p + 1) * 8], 0.0)
+    numbers = lax.broadcasted_iota(jnp.int32, (HALF, FACES), 0)
+    kept = [numbers == patches, numbers + HALF == patches]
+    walls = []
+    for f in range(5):
+        parts = [back[at + f * HALF : at + (f + 1) * HALF] for at in (0, 5 * HALF)]
+        both = jnp.where(kept[0], parts[0], 0.0) + jnp.where(kept[1], parts[1], 0.0)
+        walls.append(jnp.sum(both, axis=0, keepdims=True))
+    wall = jnp.concatenate(walls + [jnp.zeros((3, FACES), F32)], axis=0)
     shear[...] = wall[:5]
 
-    side = jnp.transpose(z_two[...])
+    side = jnp.transpose(returned[5 * HALF :, :])
     lane = parity("gz") * (CZ - 1)
     lanes = lax.broadcasted_iota(jnp.int32, (ROWS, CZ), 1)
     visc = viscosity[...].reshape(ROWS, CZ)
@@ -322,50 +375,76 @@
     cell = face_cell.reshape(1, FACES)
     patch = face_patch.reshape(1, FACES)
     face_x, face_y, face_z = shape(6, CY, CZ), shape(6 * CX, CZ), shape(8, ROWS)
-    slots, numbers = shape(HALF, 8, CAP), shape(1, FACES, dtype=jnp.int32)
+    slots, numbers = shape(HALF * 6, CAP), shape(1, FACES, dtype=jnp.int32)
     arrays = [adjoint, viscosity, cell, patch, wall_inverse]
-    adjoint, viscosity, cell, patch, inverse, x_one, x_two, y_one, y_two = pl.pallas_call(
+    package = shape(1, PROF + 8, PROF)
+    adjoint, viscosity, cell, patch, package, y_one, z_one = pl.pallas_call(
         load_kernel,
-        out_shape=tuple(shape(*a.shape, dtype=a.dtype) for a in arrays)
-        + (face_x, face_x, face_y, face_y),
+        out_shape=tuple(shape(*a.shape, dtype=a.dtype) for a in arrays[:4])
+        + (package, face_y, face_z),
         in_specs=[HBM] * 5,
-        out_specs=[VMEM] * 9,
+        out_specs=[VMEM] * 7,
         scratch_shapes=[pltpu.SemaphoreType.DMA((5,))],
         compiler_params=PARAMS,
         name="load",
     )(*[pltpu.with_memory_space_constraint(a, pltpu.HBM) for a in arrays])
-    blocks = [inverse]
+    blocks = [package]
     for step in range(1, 4):
-        blocks.append(swapped(inverse, "gz", lambda i: i ^ (4 * step)))
-    y_two = second_side(y_two, "gy")
-    z_one, z_two, own, other, ranks = pl.pallas_call(
-        gather_kernel,
-        out_shape=(face_z, face_z, slots, slots, numbers),
-        in_specs=[VMEM] * 4,
-        out_specs=[VMEM] * 5,
-        compiler_params=PARAMS,
-        name="gather",
-    )(adjoint, viscosity, cell, patch)
-    arrived = swapped(other, "gz", lambda i: i ^ 2)
+        blocks.append(swapped(package, "gz", lambda i: i ^ (4 * step)))
     mine = pl.pallas_call(
         join_kernel,
-        out_shape=shape(4 * PROF + 8, PROF),
-        in_specs=[VMEM] * 5 + [ANY],
+        out_shape=shape(4 * PROF + 16, PROF),
+        in_specs=[VMEM] * 5,
         out_specs=VMEM,
         compiler_params=PARAMS,
         name="join",
-    )(*blocks, z_one, y_two)
+    )(*blocks, z_one)
     theirs = swapped(mine, "gz", lambda i: i ^ 1)
-    solved_own, solved_arrived = pl.pallas_call(
-        solve_kernel,
-        out_shape=(slots, slots),
-        in_specs=[VMEM] * 6,
-        out_specs=[VMEM] * 2,
+    fields = (adjoint, viscosity, cell, patch)
+    gathered = (slots, slots, numbers)
+    y_one = first_side(y_one, "gy")
+    y_two, *found = pl.pallas_call(
+        early_kernel,
+        out_shape=(face_y,) + gathered,
+        in_specs=[VMEM] * 4 + [ANY] * 2,
+        out_specs=[VMEM] * 4,
+        compiler_params=PARAMS,
+        name="early_gather",
+    )(*fields, y_one, y_one)
+    y_two = second_side(y_two, "gy")
+    own, other, ranks = pl.pallas_call(
+        late_kernel,
+        out_shape=gathered,
+        in_specs=[VMEM] * 7,
+        out_specs=[VMEM] * 3,
         compiler_params=PARAMS,
         cost_estimate=LONG,
-        name="solve",
-    )(mine, theirs, own, arrived, lift_matrix, readout)
+        name="late_gather",
+    )(*fields, *found)
+    x_one, x_two, other = pl.pallas_call(
+        faces_kernel,
+        out_shape=(face_x, face_x, slots),
+        in_specs=[VMEM, VMEM, VMEM, ANY],
+        out_specs=[VMEM] * 3,
+        compiler_params=PARAMS,
+        cost_estimate=LONG,
+        name="faces",
+    )(adjoint, viscosity, other, y_two)
+    arrived = swapped(other, "gz", lambda i: i ^ 2)
+    def solve(rows, *after):
+        return pl.pallas_call(
+            solve_kernel,
+            out_shape=shape(5 * HALF + 8, CAP),
+            in_specs=[VMEM] * 5 + [ANY] * len(after),
+            out_specs=VMEM,
+            compiler_params=PARAMS,
+            cost_estimate=LONG,
+            name="solve",
+        )(mine, theirs, rows, lift_matrix, readout, *after)
+
+    solved_arrived = solve(arrived)
     returned = swapped(solved_arrived, "gz", lambda i: i ^ 2)
+    solved_own = solve(own, solved_arrived)
     partial = pl.pallas_call(
         stencil_kernel,
         out_shape=shape(5, CX, CY, CZ),
@@ -380,7 +459,7 @@
         flux_jacobian,
         first_side(x_one, "gx"),
         second_side(x_two, "gx"),
-        first_side(y_one, "gy"),
+        y_one,
         y_two,
         theirs,
         solved_own,
@@ -388,7 +467,7 @@
     return pl.pallas_call(
         scatter_kernel,
         out_shape=(shape(5, CX, CY, CZ), shape(5, FACES)),
-        in_specs=[VMEM] * 9,
+        in_specs=[VMEM] * 8,
         out_specs=[VMEM] * 2,
         compiler_params=PARAMS,
         name="scatter",
@@ -401,7 +480,6 @@
         partial,
         adjoint,
         viscosity,
-        second_side(z_two, "gz"),
     )
 
 

time: 35.8 us -> 33 us (0.922)
  the two profiles are of different devices: /device:TPU:40 before, /device:TPU:1 now
where the time goes in v3:
time: 33 us; the launch traced here: 32.9 us
  starting transfers between devices  18 us (55%)
  Pallas kernels  10 us (30%)
  waiting for transfers between devices  4.06 us (12%)
  between operations  0.74 us (2%)
    ppermute x10, starting transfers between devices, swapped(): lax.ppermute(array, axis, [(i, partner(i)) for i in range(lax.axis_size(a...  18 us
    ppermute x10, waiting for transfers between devices, swapped(): lax.ppermute(array, axis, [(i, partner(i)) for i in range(lax.axis_size(a...  4.06 us
    pallas_call x2, Pallas kernels, solve(): pl.pallas_call(solve_kernel, out_shape=shape(5 * HALF + 8, CAP), in_specs...  3.12 us
    pallas_call x1, Pallas kernels, body(): pl.pallas_call(scatter_kernel, out_shape=(shape(5, CX, CY, CZ), shape(5,...  1.92 us
    pallas_call x1, Pallas kernels, body(): pl.pallas_call(stencil_kernel, out_shape=shape(5, CX, CY, CZ), in_specs=[...  1.86 us
    pallas_call x1, Pallas kernels, body(): pl.pallas_call(load_kernel, out_shape=tuple((shape(*a.shape, dtype=a.dtyp...  1.55 us
    pallas_call x1, Pallas kernels, body(): pl.pallas_call(early_kernel, out_shape=(face_y,) + gathered, in_specs=[VM...  1.52 us
  transfers between devices with their start and end apart: 10, of which 2 were waited for; matrix products, arithmetic and copies ran while one was open for 0% of the time, Pallas kernels for 20%

profile of v3, /device:TPU:1, one launch (start us, length us, event | category | flops | bytes accessed | tf_op | source)
XLA Modules:
  0.0 32.9 jit_solution(10555921741593498202)
XLA Ops:
  0.6 1.6 %load.1 = (f32[5,4,32,256]{3,2,1,0:T(8,128)S(1)}, f32[4,32,256]{2,1,0:T(8,128)S(1)}, s32[1,1024]{1,0:T(1,128)S(1)}, s32[1,1024]{1,0:T(1,128)S(1)}, f32[1,136,128...) custom-call(f32[5,4,32,256]{3,2,1,0:T(8,128)} %adjoint_hbm.1, f32[4,32,256]{2,1,0:T(8,128)} %viscosity_hbm.1, ...), custom_call_target="tpu_custom_call" | custom-call | tf_op jit(solution)/shard_map/load/pallas_call | solution.py:381
  2.2 3.3 %collective-permute-start.4 = (f32[24,256]{1,0:T(8,128)S(1)}, f32[24,256]{1,0:T(8,128)S(1)}, u32[]{:S(2)}, u32[]{:S(2)}) collective-permute-start(f32[24,256]{1,0:T(8,128)S(1)} %get-tuple-element.25), channel_id=1, source_target_pairs={{0,16},{16,0},{32,48},{48,32},{1,17},{17,1},{33,49},{49,33},{2,18}... | collective-permute-start | bytes 73736 | tf_op jit(solution)/shard_map/ppermute | solution.py:356
  5.5 1.0 %collective-permute-start.2 = (f32[1,136,128]{2,1,0:T(8,128)S(1)}, f32[1,136,128]{2,1,0:T(8,128)S(1)}, u32[]{:S(2)}, u32[]{:S(2)}) collective-permute-start(f32[1,136,128]{2,1,0:T(8,128)S(1)} %get-tuple-element.19.first), channel_id=1, source_target_pairs={{0,12},{1,13},{2,14},{3,15},{4,8},{5,9},{6,10},{7,11},{8,4},{9,5},... | collective-permute-start | bytes 208904 | tf_op jit(solution)/shard_map/ppermute | solution.py:356
  6.5 0.3 %collective-permute-start.1 = (f32[1,136,128]{2,1,0:T(8,128)S(1)}, f32[1,136,128]{2,1,0:T(8,128)S(1)}, u32[]{:S(2)}, u32[]{:S(2)}) collective-permute-start(f32[1,136,128]{2,1,0:T(8,128)S(1)} %get-tuple-element.19.first), channel_id=1, source_target_pairs={{0,8},{1,9},{2,10},{3,11},{4,12},{5,13},{6,14},{7,15},{8,0},{9,1},... | collective-permute-start | bytes 208904 | tf_op jit(solution)/shard_map/ppermute | solution.py:356
  6.9 1.9 %collective-permute-start = (f32[1,136,128]{2,1,0:T(8,128)S(1)}, f32[1,136,128]{2,1,0:T(8,128)S(1)}, u32[]{:S(2)}, u32[]{:S(2)}) collective-permute-start(f32[1,136,128]{2,1,0:T(8,128)S(1)} %get-tuple-element.19.first), channel_id=1, source_target_pairs={{0,4},{1,5},{2,6},{3,7},{4,0},{5,1},{6,2},{7,3},{8,12},{9,13},{10,... | collective-permute-start | bytes 208904 | tf_op jit(solution)/shard_map/ppermute | solution.py:356
  8.8 0.0 collective-permute-done.4.before.joined.y_one
  8.8 1.5 %early_gather.1 = (f32[24,256]{1,0:T(8,128)S(1)}, f32[48,128]{1,0:T(8,128)S(1)}, f32[48,128]{1,0:T(8,128)S(1)}, s32[1,1024]{1,0:T(1,128)S(1)}) custom-call(f32[5,4,32,256]{3,2,1,0:T(8,128)S(1)} %get-tuple-element.21.adjoint, f32[4,32,256]{2,1,0:T(8,128)S(1)} %get-tuple-element.22.viscosity, s32[1,1024]{1,0:T(1,128)S(1)} %get-tuple-element.23.cell, ...), custom_call_target="tpu_custom_call" | custom-call | tf_op jit(solution)/shard_map/early_gather/pallas_call | solution.py:406
  10.3 4.6 %collective-permute-start.5 = (f32[24,256]{1,0:T(8,128)S(1)}, f32[24,256]{1,0:T(8,128)S(1)}, u32[]{:S(2)}, u32[]{:S(2)}) collective-permute-start(f32[24,256]{1,0:T(8,128)S(1)} %get-tuple-element.31), channel_id=1, source_target_pairs={{0,48},{16,32},{32,16},{48,0},{1,49},{17,33},{33,17},{49,1},{2,50}... | collective-permute-start | bytes 73736 | tf_op jit(solution)/shard_map/ppermute | solution.py:356
  14.9 0.0 collective-permute-done.2.fourth
  14.9 0.0 collective-permute-done.1.third
  14.9 0.0 collective-permute-done.second
  15.0 0.8 %collective-permute-start.3 = (f32[528,128]{1,0:T(8,128)S(1)}, f32[528,128]{1,0:T(8,128)S(1)}, u32[]{:S(2)}, u32[]{:S(2)}) collective-permute-start(f32[528,128]{1,0:T(8,128)S(1)} %join.1.mine), channel_id=1, source_target_pairs={{0,1},{1,0},{2,3},{3,2},{4,5},{5,4},{6,7},{7,6},{8,9},{9,8},{10,11... | collective-permute-start | bytes 811016 | tf_op jit(solution)/shard_map/ppermute | solution.py:356
  15.8 2.1 %collective-permute-done.5.before.y_two = f32[24,256]{1,0:T(8,128)S(1)} collective-permute-done((f32[24,256]{1,0:T(8,128)S(1)}, f32[24,256]{1,0:T(8,128)S(1)}, u32[]{:S(2)}, u32[]{:S(2)}) %collective-permute-start.5) | collective-permute-done | bytes 24608 | tf_op jit(solution)/shard_map/ppermute | solution.py:356
  17.9 0.0 copy-start.2
  17.9 0.0 copy-start
  17.9 1.4 %collective-permute-start.6 = (f32[48,128]{1,0:T(8,128)S(1)}, f32[48,128]{1,0:T(8,128)S(1)}, u32[]{:S(2)}, u32[]{:S(2)}) collective-permute-start(f32[48,128]{1,0:T(8,128)S(1)} %get-tuple-element.32), channel_id=1, source_target_pairs={{0,2},{1,3},{2,0},{3,1},{4,6},{5,7},{6,4},{7,5},{8,10},{9,11},{10,... | collective-permute-start | bytes 73736 | tf_op jit(solution)/shard_map/ppermute | solution.py:356
  19.4 0.0 copy-done.2
  19.4 0.1 copy.11.lift
  19.5 1.3 %collective-permute-start.8 = (f32[6,32,256]{2,1,0:T(8,128)S(1)}, f32[6,32,256]{2,1,0:T(8,128)S(1)}, u32[]{:S(2)}, u32[]{:S(2)}) collective-permute-start(f32[6,32,256]{2,1,0:T(8,128)S(1)} %get-tuple-element.34), channel_id=1, source_target_pairs={{0,64},{64,0},{128,192},{192,128},{1,65},{65,1},{129,193},{193,129... | collective-permute-start | bytes 589832 | tf_op jit(solution)/shard_map/ppermute | solution.py:356
  20.8 1.8 %collective-permute-start.9 = (f32[6,32,256]{2,1,0:T(8,128)S(1)}, f32[6,32,256]{2,1,0:T(8,128)S(1)}, u32[]{:S(2)}, u32[]{:S(2)}) collective-permute-start(f32[6,32,256]{2,1,0:T(8,128)S(1)} %get-tuple-element.35), channel_id=1, source_target_pairs={{0,192},{64,128},{128,64},{192,0},{1,193},{65,129},{129,65},{193,1... | collective-permute-start | bytes 589832 | tf_op jit(solution)/shard_map/ppermute | solution.py:356
  22.6 0.0 collective-permute-done.6.rows
  22.6 1.9 %collective-permute-done.3.theirs.z_one = f32[528,128]{1,0:T(8,128)S(1)} collective-permute-done((f32[528,128]{1,0:T(8,128)S(1)}, f32[528,128]{1,0:T(8,128)S(1)}, u32[]{:S(2)}, u32[]{:S(2)}) %collective-permute-start.3) | collective-permute-done | bytes 270368 | tf_op jit(solution)/shard_map/ppermute | solution.py:356
  24.5 0.0 copy-done
  24.5 1.6 %solve.2.refs_0_ = f32[48,128]{1,0:T(8,128)S(1)} custom-call(f32[528,128]{1,0:T(8,128)S(1)} %join.1.mine, f32[528,128]{1,0:T(8,128)S(1)} %collective-permute-done.3.theirs.z_one, f32[48,128]{1,0:T(8,128)S(1)} %collective-permute-done.6.rows, f32[128,6]{1,0:T(8,128)S(1)} %copy.11.lift, f32[5,128]{1,0:T(8,128)S(1)} %copy-done), custom_call_target="tpu_custom_call" | custom-call | flops 20000000000 | bytes 60000000 | tf_op jit(solution)/shard_map/solve/pallas_call | solution.py:435
  26.1 1.4 %collective-permute-start.7 = (f32[48,128]{1,0:T(8,128)S(1)}, f32[48,128]{1,0:T(8,128)S(1)}, u32[]{:S(2)}, u32[]{:S(2)}) collective-permute-start(f32[48,128]{1,0:T(8,128)S(1)} %solve.2.refs_0_), channel_id=1, source_target_pairs={{0,2},{1,3},{2,0},{3,1},{4,6},{5,7},{6,4},{7,5},{8,10},{9,11},{10,... | collective-permute-start | bytes 73736 | tf_op jit(solution)/shard_map/ppermute | solution.py:356
  27.5 1.6 %solve.3.after.solved_own = f32[48,128]{1,0:T(8,128)S(1)} custom-call(f32[528,128]{1,0:T(8,128)S(1)} %join.1.mine, f32[528,128]{1,0:T(8,128)S(1)} %collective-permute-done.3.theirs.z_one, f32[48,128]{1,0:T(8,128)S(1)} %get-tuple-element.29.rows, f32[128,6]{1,0:T(8,128)S(1)} %copy.11.lift, f32[5,128]{1,0:T(8,128)S(1)} %copy-done, f32[48,128]{1,0:T(8,128)S(1)} %solve.2.refs_0_), custom_call_target="tpu_custom_call" | custom-call | flops 20000000000 | bytes 60000000 | tf_op jit(solution)/shard_map/solve/pallas_call | solution.py:435
  29.1 0.0 collective-permute-done.8.x_one
  29.1 0.0 collective-permute-done.9.x_two
  29.1 0.0 copy-done.1
  29.1 1.9 %stencil.1.partial = f32[5,4,32,256]{3,2,1,0:T(8,128)S(1)} custom-call(f32[5,4,32,256]{3,2,1,0:T(8,128)S(1)} %get-tuple-element.21.adjoint, f32[4,32,256]{2,1,0:T(8,128)S(1)} %get-tuple-element.22.viscosity, f32[5,5]{1,0:T(8,128)S(1)} %copy-done.1, f32[6,32,256]{2,1,0:T(8,128)S(1)} %collective-permute-done.8.x_one, ...), custom_call_target="tpu_custom_call" | custom-call | flops 20000000000 | bytes 60000000 | tf_op jit(solution)/shard_map/stencil/pallas_call | solution.py:448
  31.0 0.0 collective-permute-done.7.returned
  31.0 1.9 %scatter.1 = (f32[5,4,32,256]{3,2,1,0:T(8,128)}, f32[5,1024]{1,0:T(8,128)}) custom-call(f32[48,128]{1,0:T(8,128)S(1)} %solve.3.after.solved_own, f32[48,128]{1,0:T(8,128)S(1)} %collective-permute-done.7.returned, s32[1,1024]{1,0:T(1,128)S(1)} %get-tuple-element.23.cell, s32[1,1024]{1,0:T(1,128)S(1)} %get-tuple-element.24.patch, ...), custom_call_target="tpu_custom_call" | custom-call | tf_op jit(solution)/shard_map/scatter/pallas_call | solution.py:467
  (4 shorter events, 0.1 us)
Async XLA Ops:
  2.2 6.6 %collective-permute-start.4 = (f32[24,256]{1,0:T(8,128)S(1)}, f32[24,256]{1,0:T(8,128)S(1)}, u32[]{:S(2)}, u32[]{:S(2)}) collective-permute-start(f32[24,256]{1,0:T(8,128)S(1)} %get-tuple-element.25), channel_id=1, source_target_pairs={{0,16},{16,0},{32,48},{48,32},{1,17},{17,1},{33,49},{49,33},{2,18}... | collective-permute-start | bytes 73736 | tf_op jit(solution)/shard_map/ppermute | solution.py:356
  5.5 9.4 %collective-permute-start.2 = (f32[1,136,128]{2,1,0:T(8,128)S(1)}, f32[1,136,128]{2,1,0:T(8,128)S(1)}, u32[]{:S(2)}, u32[]{:S(2)}) collective-permute-start(f32[1,136,128]{2,1,0:T(8,128)S(1)} %get-tuple-element.19.first), channel_id=1, source_target_pairs={{0,12},{1,13},{2,14},{3,15},{4,8},{5,9},{6,10},{7,11},{8,4},{9,5},... | collective-permute-start | bytes 208904 | tf_op jit(solution)/shard_map/ppermute | solution.py:356
  6.5 8.4 %collective-permute-start.1 = (f32[1,136,128]{2,1,0:T(8,128)S(1)}, f32[1,136,128]{2,1,0:T(8,128)S(1)}, u32[]{:S(2)}, u32[]{:S(2)}) collective-permute-start(f32[1,136,128]{2,1,0:T(8,128)S(1)} %get-tuple-element.19.first), channel_id=1, source_target_pairs={{0,8},{1,9},{2,10},{3,11},{4,12},{5,13},{6,14},{7,15},{8,0},{9,1},... | collective-permute-start | bytes 208904 | tf_op jit(solution)/shard_map/ppermute | solution.py:356
  6.9 8.0 %collective-permute-start = (f32[1,136,128]{2,1,0:T(8,128)S(1)}, f32[1,136,128]{2,1,0:T(8,128)S(1)}, u32[]{:S(2)}, u32[]{:S(2)}) collective-permute-start(f32[1,136,128]{2,1,0:T(8,128)S(1)} %get-tuple-element.19.first), channel_id=1, source_target_pairs={{0,4},{1,5},{2,6},{3,7},{4,0},{5,1},{6,2},{7,3},{8,12},{9,13},{10,... | collective-permute-start | bytes 208904 | tf_op jit(solution)/shard_map/ppermute | solution.py:356
  10.3 7.6 %collective-permute-start.5 = (f32[24,256]{1,0:T(8,128)S(1)}, f32[24,256]{1,0:T(8,128)S(1)}, u32[]{:S(2)}, u32[]{:S(2)}) collective-permute-start(f32[24,256]{1,0:T(8,128)S(1)} %get-tuple-element.31), channel_id=1, source_target_pairs={{0,48},{16,32},{32,16},{48,0},{1,49},{17,33},{33,17},{49,1},{2,50}... | collective-permute-start | bytes 73736 | tf_op jit(solution)/shard_map/ppermute | solution.py:356
  15.0 9.6 %collective-permute-start.3 = (f32[528,128]{1,0:T(8,128)S(1)}, f32[528,128]{1,0:T(8,128)S(1)}, u32[]{:S(2)}, u32[]{:S(2)}) collective-permute-start(f32[528,128]{1,0:T(8,128)S(1)} %join.1.mine), channel_id=1, source_target_pairs={{0,1},{1,0},{2,3},{3,2},{4,5},{5,4},{6,7},{7,6},{8,9},{9,8},{10,11... | collective-permute-start | bytes 811016 | tf_op jit(solution)/shard_map/ppermute | solution.py:356
  17.9 1.5 %copy-start.2 = (f32[128,6]{0,1:T(8,128)S(1)}, f32[128,6]{0,1:T(8,128)}, u32[]{:S(2)}) copy-start(f32[128,6]{0,1:T(8,128)} %param.14) | copy-start | bytes 9220
  17.9 6.6 %copy-start = (f32[5,128]{1,0:T(8,128)S(1)}, f32[5,128]{1,0:T(8,128)}, u32[]{:S(2)}) copy-start(f32[5,128]{1,0:T(8,128)} %readout.3) | copy-start | bytes 7684
  17.9 4.7 %collective-permute-start.6 = (f32[48,128]{1,0:T(8,128)S(1)}, f32[48,128]{1,0:T(8,128)S(1)}, u32[]{:S(2)}, u32[]{:S(2)}) collective-permute-start(f32[48,128]{1,0:T(8,128)S(1)} %get-tuple-element.32), channel_id=1, source_target_pairs={{0,2},{1,3},{2,0},{3,1},{4,6},{5,7},{6,4},{7,5},{8,10},{9,11},{10,... | collective-permute-start | bytes 73736 | tf_op jit(solution)/shard_map/ppermute | solution.py:356
  19.5 9.6 %collective-permute-start.8 = (f32[6,32,256]{2,1,0:T(8,128)S(1)}, f32[6,32,256]{2,1,0:T(8,128)S(1)}, u32[]{:S(2)}, u32[]{:S(2)}) collective-permute-start(f32[6,32,256]{2,1,0:T(8,128)S(1)} %get-tuple-element.34), channel_id=1, source_target_pairs={{0,64},{64,0},{128,192},{192,128},{1,65},{65,1},{129,193},{193,129... | collective-permute-start | bytes 589832 | tf_op jit(solution)/shard_map/ppermute | solution.py:356
  20.8 8.3 %collective-permute-start.9 = (f32[6,32,256]{2,1,0:T(8,128)S(1)}, f32[6,32,256]{2,1,0:T(8,128)S(1)}, u32[]{:S(2)}, u32[]{:S(2)}) collective-permute-start(f32[6,32,256]{2,1,0:T(8,128)S(1)} %get-tuple-element.35), channel_id=1, source_target_pairs={{0,192},{64,128},{128,64},{192,0},{1,193},{65,129},{129,65},{193,1... | collective-permute-start | bytes 589832 | tf_op jit(solution)/shard_map/ppermute | solution.py:356
  26.1 4.9 %collective-permute-start.7 = (f32[48,128]{1,0:T(8,128)S(1)}, f32[48,128]{1,0:T(8,128)S(1)}, u32[]{:S(2)}, u32[]{:S(2)}) collective-permute-start(f32[48,128]{1,0:T(8,128)S(1)} %solve.2.refs_0_), channel_id=1, source_target_pairs={{0,2},{1,3},{2,0},{3,1},{4,6},{5,7},{6,4},{7,5},{8,10},{9,11},{10,... | collective-permute-start | bytes 73736 | tf_op jit(solution)/shard_map/ppermute | solution.py:356
  27.5 1.6 %copy-start.1 = (f32[5,5]{1,0:T(8,128)S(1)}, f32[5,5]{1,0:T(8,128)}, u32[]{:S(2)}) copy-start(f32[5,5]{1,0:T(8,128)} %jacobian.1) | copy-start | bytes 304

commit v4 on v3

--- a/solution.py
+++ b/solution.py
@@ -27,6 +27,7 @@
 ANY = pl.BlockSpec(memory_space=pl.ANY)
 SMEM = pl.BlockSpec(memory_space=pltpu.SMEM)
 LONG = pl.CostEstimate(flops=20_000_000_000, bytes_accessed=60_000_000, transcendentals=0)
+SHORT = pl.CostEstimate(flops=1000, bytes_accessed=1000, transcendentals=0)
 PARAMS = pltpu.CompilerParams(vmem_limit_bytes=48 * 1024 * 1024)
 
 
@@ -204,48 +205,21 @@
         other[p * 6 : (p + 1) * 6, :] = slots[HALF + p, :6]
 
 
-def stencil_kernel(
-    adjoint, viscosity, jacobian, x_one, x_two, y_one, y_two, z_one, after, out
-):
-    def sides(axis, one, two):
-        odd = parity(axis) == 1
-        return jnp.where(odd, one, two), jnp.where(odd, two, one)
-
-    gx, gy = lax.axis_index("gx"), lax.axis_index("gy")
-    has_before_x = jnp.where(gx > 0, 1.0, 0.0)
-    has_after_x = jnp.where(gx < lax.axis_size("gx") - 1, 1.0, 0.0)
-    has_before_y = jnp.where(gy > 0, 1.0, 0.0)
-    has_after_y = jnp.where(gy < lax.axis_size("gy") - 1, 1.0, 0.0)
-    y_before, y_after = sides("gy", y_one[...], y_two[...])
-    y_before, y_after = y_before * has_before_y, y_after * has_after_y
-    z_side = jnp.transpose(z_one[4 * PROF : 4 * PROF + 8, :])
-    odd_z = parity("gz")
-
-    def x_side(f, side):
-        before, after = sides("gx", x_one[f], x_two[f])
-        return after * has_after_x if side else before * has_before_x
-
+def interior(adjoint, viscosity, jacobian, faces, out):
     rows = lax.broadcasted_iota(jnp.int32, (CY, CZ), 0)
     lanes = lax.broadcasted_iota(jnp.int32, (CY, CZ), 1)
+
     def field_at(f, x):
         return viscosity[x] if f == 5 else adjoint[f, x]
 
     def neighbours(f, x):
         center = field_at(f, x)
-        yield field_at(f, x - 1) if x > 0 else x_side(f, 0)
-        yield field_at(f, x + 1) if x < CX - 1 else x_side(f, 1)
-        at = slice(f * CX + x, f * CX + x + 1)
-        yield jnp.where(rows == 0, y_before[at, :], pltpu.roll(center, 1, 0))
-        yield jnp.where(
-            rows == CY - 1, y_after[at, :], pltpu.roll(center, CY - 1, 0)
-        )
-        part = slice(x * CY, (x + 1) * CY)
-        low, high = pltpu.roll(center, 1, 1), pltpu.roll(center, CZ - 1, 1)
-        edge = z_side[part, f : f + 1]
-        low = jnp.where((lanes == 0) & (odd_z == 1), edge, low)
-        high = jnp.where((lanes == CZ - 1) & (odd_z == 0), edge, high)
-        yield jnp.where((lanes == 0) & (odd_z == 0), center, low)
-        yield jnp.where((lanes == CZ - 1) & (odd_z == 1), center, high)
+        yield field_at(f, max(x - 1, 0))
+        yield field_at(f, min(x + 1, CX - 1))
+        yield jnp.where(rows == 0, center, pltpu.roll(center, 1, 0))
+        yield jnp.where(rows == CY - 1, center, pltpu.roll(center, CY - 1, 0))
+        yield jnp.where(lanes == 0, center, pltpu.roll(center, 1, 1))
+        yield jnp.where(lanes == CZ - 1, center, pltpu.roll(center, CZ - 1, 1))
 
     for x in range(CX):
         visc = viscosity[x]
@@ -258,6 +232,38 @@
             for g in range(5):
                 total = total + jacobian[f, g] * adjoint[g, x]
             out[f, x] = center + time_step * total
+
+
+def stencil_kernel(
+    adjoint, viscosity, base, x_one, x_two, y_one, y_two, z_one, after, out
+):
+    def sides(axis, one, two):
+        odd, place = parity(axis) == 1, lax.axis_index(axis)
+        has_before = jnp.where(place > 0, 1.0, 0.0)
+        has_after = jnp.where(place < lax.axis_size(axis) - 1, 1.0, 0.0)
+        return jnp.where(odd, one, two) * has_before, jnp.where(odd, two, one) * has_after
+
+    y_sides = sides("gy", y_one[...], y_two[...])
+    x_visc = sides("gx", x_one[5], x_two[5])
+    side = jnp.transpose(z_one[4 * PROF : 4 * PROF + 8, :])
+    lane = (1 - parity("gz")) * (CZ - 1)
+    lanes = lax.broadcasted_iota(jnp.int32, (ROWS, CZ), 1)
+    visc = viscosity[...].reshape(ROWS, CZ)
+    at_edge = jnp.where(lanes == lane, 0.5 * (visc + side[:, 5:6]), 0.0)
+    for f in range(5):
+        value = adjoint[f].reshape(ROWS, CZ)
+        edge = time_step * (at_edge * (side[:, f : f + 1] - value))
+        out[f] = base[f] + edge.reshape(CX, CY, CZ)
+        for x, beside, other in zip((0, CX - 1), sides("gx", x_one[f], x_two[f]), x_visc):
+            weight = 0.5 * (viscosity[x] + other)
+            out[f, x] = out[f, x] + time_step * (weight * (beside - adjoint[f, x]))
+        for x in range(CX):
+            for row, beside in zip((0, CY - 1), y_sides):
+                at = slice(row, row + 1)
+                other = beside[5 * CX + x : 5 * CX + x + 1]
+                weight = 0.5 * (viscosity[x, at, :] + other)
+                here = beside[f * CX + x : f * CX + x + 1] - adjoint[f, x, at, :]
+                out[f, x, at, :] = out[f, x, at, :] + time_step * (weight * here)
 
 
 def wide(matrix):
@@ -442,13 +448,22 @@
             name="solve",
         )(mine, theirs, rows, lift_matrix, readout, *after)
 
-    solved_arrived = solve(arrived)
+    base = pl.pallas_call(
+        interior,
+        out_shape=shape(5, CX, CY, CZ),
+        in_specs=[VMEM, VMEM, SMEM, ANY],
+        out_specs=VMEM,
+        compiler_params=PARAMS,
+        cost_estimate=SHORT,
+        name="interior",
+    )(adjoint, viscosity, flux_jacobian, x_one)
+    solved_arrived = solve(arrived, base)
     returned = swapped(solved_arrived, "gz", lambda i: i ^ 2)
     solved_own = solve(own, solved_arrived)
     partial = pl.pallas_call(
         stencil_kernel,
         out_shape=shape(5, CX, CY, CZ),
-        in_specs=[VMEM, VMEM, SMEM] + [VMEM] * 5 + [ANY],
+        in_specs=[VMEM] * 8 + [ANY],
         out_specs=VMEM,
         compiler_params=PARAMS,
         cost_estimate=LONG,
@@ -456,7 +471,7 @@
     )(
         adjoint,
         viscosity,
-        flux_jacobian,
+        base,
         first_side(x_one, "gx"),
         second_side(x_two, "gx"),
         y_one,

time: 33 us -> 32.5 us (0.985)
  the two profiles are of different devices: /device:TPU:1 before, /device:TPU:4 now
where the time goes in v4:
time: 32.5 us; the launch traced here: 32 us
  starting transfers between devices  17.3 us (53%)
  Pallas kernels  10.2 us (31%)
  waiting for transfers between devices  3.62 us (11%)
  between operations  0.74 us (2%)
    ppermute x10, starting transfers between devices, swapped(): lax.ppermute(array, axis, [(i, partner(i)) for i in range(lax.axis_size(a...  17.3 us
    ppermute x10, waiting for transfers between devices, swapped(): lax.ppermute(array, axis, [(i, partner(i)) for i in range(lax.axis_size(a...  3.62 us
    pallas_call x2, Pallas kernels, solve(): pl.pallas_call(solve_kernel, out_shape=shape(5 * HALF + 8, CAP), in_specs...  3.11 us
    pallas_call x1, Pallas kernels, body(): pl.pallas_call(scatter_kernel, out_shape=(shape(5, CX, CY, CZ), shape(5,...  1.92 us
    pallas_call x1, Pallas kernels, body(): pl.pallas_call(interior, out_shape=shape(5, CX, CY, CZ), in_specs=[VMEM,...  1.64 us
    pallas_call x1, Pallas kernels, body(): pl.pallas_call(load_kernel, out_shape=tuple((shape(*a.shape, dtype=a.dtyp...  1.55 us
    pallas_call x1, Pallas kernels, body(): pl.pallas_call(early_kernel, out_shape=(face_y,) + gathered, in_specs=[VM...  1.52 us
  transfers between devices with their start and end apart: 10, of which 3 were waited for; matrix products, arithmetic and copies ran while one was open for 0% of the time, Pallas kernels for 21%

profile of v4, /device:TPU:4, one launch (start us, length us, event | category | flops | bytes accessed | tf_op | source)
XLA Modules:
  0.0 32.0 jit_solution(10542110055365601553)
XLA Ops:
  0.6 1.6 %load.1 = (f32[5,4,32,256]{3,2,1,0:T(8,128)S(1)}, f32[4,32,256]{2,1,0:T(8,128)S(1)}, s32[1,1024]{1,0:T(1,128)S(1)}, s32[1,1024]{1,0:T(1,128)S(1)}, f32[1,136,128...) custom-call(f32[5,4,32,256]{3,2,1,0:T(8,128)} %adjoint_hbm.1, f32[4,32,256]{2,1,0:T(8,128)} %viscosity_hbm.1, ...), custom_call_target="tpu_custom_call" | custom-call | tf_op jit(solution)/shard_map/load/pallas_call | solution.py:387
  2.2 0.1 collective-permute-start.4
  2.3 3.1 %collective-permute-start.2 = (f32[1,136,128]{2,1,0:T(8,128)S(1)}, f32[1,136,128]{2,1,0:T(8,128)S(1)}, u32[]{:S(2)}, u32[]{:S(2)}) collective-permute-start(f32[1,136,128]{2,1,0:T(8,128)S(1)} %get-tuple-element.19.first), channel_id=1, source_target_pairs={{0,12},{1,13},{2,14},{3,15},{4,8},{5,9},{6,10},{7,11},{8,4},{9,5},... | collective-permute-start | bytes 208904 | tf_op jit(solution)/shard_map/ppermute | solution.py:362
  5.4 0.6 %collective-permute-start.1 = (f32[1,136,128]{2,1,0:T(8,128)S(1)}, f32[1,136,128]{2,1,0:T(8,128)S(1)}, u32[]{:S(2)}, u32[]{:S(2)}) collective-permute-start(f32[1,136,128]{2,1,0:T(8,128)S(1)} %get-tuple-element.19.first), channel_id=1, source_target_pairs={{0,8},{1,9},{2,10},{3,11},{4,12},{5,13},{6,14},{7,15},{8,0},{9,1},... | collective-permute-start | bytes 208904 | tf_op jit(solution)/shard_map/ppermute | solution.py:362
  6.0 0.5 %collective-permute-start = (f32[1,136,128]{2,1,0:T(8,128)S(1)}, f32[1,136,128]{2,1,0:T(8,128)S(1)}, u32[]{:S(2)}, u32[]{:S(2)}) collective-permute-start(f32[1,136,128]{2,1,0:T(8,128)S(1)} %get-tuple-element.19.first), channel_id=1, source_target_pairs={{0,4},{1,5},{2,6},{3,7},{4,0},{5,1},{6,2},{7,3},{8,12},{9,13},{10,... | collective-permute-start | bytes 208904 | tf_op jit(solution)/shard_map/ppermute | solution.py:362
  6.5 0.0 collective-permute-done.4.before.joined.y_one
  6.5 1.5 %early_gather.1 = (f32[24,256]{1,0:T(8,128)S(1)}, f32[48,128]{1,0:T(8,128)S(1)}, f32[48,128]{1,0:T(8,128)S(1)}, s32[1,1024]{1,0:T(1,128)S(1)}) custom-call(f32[5,4,32,256]{3,2,1,0:T(8,128)S(1)} %get-tuple-element.21.adjoint, f32[4,32,256]{2,1,0:T(8,128)S(1)} %get-tuple-element.22.viscosity, s32[1,1024]{1,0:T(1,128)S(1)} %get-tuple-element.23.cell, ...), custom_call_target="tpu_custom_call" | custom-call | tf_op jit(solution)/shard_map/early_gather/pallas_call | solution.py:412
  8.0 5.0 %collective-permute-start.5 = (f32[24,256]{1,0:T(8,128)S(1)}, f32[24,256]{1,0:T(8,128)S(1)}, u32[]{:S(2)}, u32[]{:S(2)}) collective-permute-start(f32[24,256]{1,0:T(8,128)S(1)} %get-tuple-element.31), channel_id=1, source_target_pairs={{0,48},{16,32},{32,16},{48,0},{1,49},{17,33},{33,17},{49,1},{2,50}... | collective-permute-start | bytes 73736 | tf_op jit(solution)/shard_map/ppermute | solution.py:362
  13.0 0.0 collective-permute-done.2.fourth
  13.0 0.0 collective-permute-done.1.third
  13.0 0.0 collective-permute-done.second
  13.1 1.1 %collective-permute-start.3 = (f32[528,128]{1,0:T(8,128)S(1)}, f32[528,128]{1,0:T(8,128)S(1)}, u32[]{:S(2)}, u32[]{:S(2)}) collective-permute-start(f32[528,128]{1,0:T(8,128)S(1)} %join.1.mine), channel_id=1, source_target_pairs={{0,1},{1,0},{2,3},{3,2},{4,5},{5,4},{6,7},{7,6},{8,9},{9,8},{10,11... | collective-permute-start | bytes 811016 | tf_op jit(solution)/shard_map/ppermute | solution.py:362
  14.2 1.1 %collective-permute-done.5.before.y_two = f32[24,256]{1,0:T(8,128)S(1)} collective-permute-done((f32[24,256]{1,0:T(8,128)S(1)}, f32[24,256]{1,0:T(8,128)S(1)}, u32[]{:S(2)}, u32[]{:S(2)}) %collective-permute-start.5) | collective-permute-done | bytes 24608 | tf_op jit(solution)/shard_map/ppermute | solution.py:362
  15.3 0.0 copy-start.2
  15.3 3.4 %collective-permute-start.6 = (f32[48,128]{1,0:T(8,128)S(1)}, f32[48,128]{1,0:T(8,128)S(1)}, u32[]{:S(2)}, u32[]{:S(2)}) collective-permute-start(f32[48,128]{1,0:T(8,128)S(1)} %get-tuple-element.32), channel_id=1, source_target_pairs={{0,2},{1,3},{2,0},{3,1},{4,6},{5,7},{6,4},{7,5},{8,10},{9,11},{10,... | collective-permute-start | bytes 73736 | tf_op jit(solution)/shard_map/ppermute | solution.py:362
  18.7 0.0 copy-done.2
  18.7 0.1 copy.11.lift
  18.8 0.6 %collective-permute-start.9 = (f32[6,32,256]{2,1,0:T(8,128)S(1)}, f32[6,32,256]{2,1,0:T(8,128)S(1)}, u32[]{:S(2)}, u32[]{:S(2)}) collective-permute-start(f32[6,32,256]{2,1,0:T(8,128)S(1)} %get-tuple-element.35), channel_id=1, source_target_pairs={{0,192},{64,128},{128,64},{192,0},{1,193},{65,129},{129,65},{193,1... | collective-permute-start | bytes 589832 | tf_op jit(solution)/shard_map/ppermute | solution.py:362
  19.5 1.1 %collective-permute-start.8 = (f32[6,32,256]{2,1,0:T(8,128)S(1)}, f32[6,32,256]{2,1,0:T(8,128)S(1)}, u32[]{:S(2)}, u32[]{:S(2)}) collective-permute-start(f32[6,32,256]{2,1,0:T(8,128)S(1)} %get-tuple-element.33.faces), channel_id=1, source_target_pairs={{0,64},{64,0},{128,192},{192,128},{1,65},{65,1},{129,193},{193,129... | collective-permute-start | bytes 589832 | tf_op jit(solution)/shard_map/ppermute | solution.py:362
  20.6 0.0 copy-done
  20.6 1.6 %interior.1.refs_0_.base = f32[5,4,32,256]{3,2,1,0:T(8,128)S(1)} custom-call(f32[5,4,32,256]{3,2,1,0:T(8,128)S(1)} %get-tuple-element.21.adjoint, f32[4,32,256]{2,1,0:T(8,128)S(1)} %get-tuple-element.22.viscosity, f32[5,5]{1,0:T(8,128)S(1)} %copy-done, f32[6,32,256]{2,1,0:T(8,128)S(1)} %get-tuple-element.33.faces), custom_call_target="tpu_custom_call" | custom-call | flops 1000 | bytes 1000 | tf_op jit(solution)/shard_map/interior/pallas_call | solution.py:451
  22.2 0.0 collective-permute-done.6.rows
  22.2 1.2 %collective-permute-done.3.theirs.z_one = f32[528,128]{1,0:T(8,128)S(1)} collective-permute-done((f32[528,128]{1,0:T(8,128)S(1)}, f32[528,128]{1,0:T(8,128)S(1)}, u32[]{:S(2)}, u32[]{:S(2)}) %collective-permute-start.3) | collective-permute-done | bytes 270368 | tf_op jit(solution)/shard_map/ppermute | solution.py:362
  23.5 0.0 copy-done.1
  23.5 1.6 %solve.2.refs_0_ = f32[48,128]{1,0:T(8,128)S(1)} custom-call(f32[528,128]{1,0:T(8,128)S(1)} %join.1.mine, f32[528,128]{1,0:T(8,128)S(1)} %collective-permute-done.3.theirs.z_one, f32[48,128]{1,0:T(8,128)S(1)} %collective-permute-done.6.rows, f32[128,6]{1,0:T(8,128)S(1)} %copy.11.lift, f32[5,128]{1,0:T(8,128)S(1)} %copy-done.1, ...), custom_call_target="tpu_custom_call" | custom-call | flops 20000000000 | bytes 60000000 | tf_op jit(solution)/shard_map/solve/pallas_call | solution.py:441
  25.0 1.7 %collective-permute-start.7 = (f32[48,128]{1,0:T(8,128)S(1)}, f32[48,128]{1,0:T(8,128)S(1)}, u32[]{:S(2)}, u32[]{:S(2)}) collective-permute-start(f32[48,128]{1,0:T(8,128)S(1)} %solve.2.refs_0_), channel_id=1, source_target_pairs={{0,2},{1,3},{2,0},{3,1},{4,6},{5,7},{6,4},{7,5},{8,10},{9,11},{10,... | collective-permute-start | bytes 73736 | tf_op jit(solution)/shard_map/ppermute | solution.py:362
  26.7 1.6 %solve.3.after.solved_own = f32[48,128]{1,0:T(8,128)S(1)} custom-call(f32[528,128]{1,0:T(8,128)S(1)} %join.1.mine, f32[528,128]{1,0:T(8,128)S(1)} %collective-permute-done.3.theirs.z_one, f32[48,128]{1,0:T(8,128)S(1)} %get-tuple-element.29.rows, f32[128,6]{1,0:T(8,128)S(1)} %copy.11.lift, f32[5,128]{1,0:T(8,128)S(1)} %copy-done.1, f32[48,128]{1,0:T(8,128)S(1)} %solve.2.refs_0_), custom_call_target="tpu_custom_call" | custom-call | flops 20000000000 | bytes 60000000 | tf_op jit(solution)/shard_map/solve/pallas_call | solution.py:441
  28.3 0.0 collective-permute-done.9.x_two
  28.3 0.0 collective-permute-done.8.x_one
  28.3 0.4 %stencil.1.partial = f32[5,4,32,256]{3,2,1,0:T(8,128)S(1)} custom-call(f32[5,4,32,256]{3,2,1,0:T(8,128)S(1)} %get-tuple-element.21.adjoint, f32[4,32,256]{2,1,0:T(8,128)S(1)} %get-tuple-element.22.viscosity, f32[5,4,32,256]{3,2,1,0:T(8,128)S(1)} %interior.1.refs_0_.base, f32[6,32,256]{2,1,0:T(8,128)S(1)} %collective-permute-done.8.x_one, ...), custom_call_target="tpu_custom_call" | custom-call | flops 20000000000 | bytes 60000000 | tf_op jit(solution)/shard_map/stencil/pallas_call | solution.py:463
  28.7 1.3 %collective-permute-done.7.returned = f32[48,128]{1,0:T(8,128)S(1)} collective-permute-done((f32[48,128]{1,0:T(8,128)S(1)}, f32[48,128]{1,0:T(8,128)S(1)}, u32[]{:S(2)}, u32[]{:S(2)}) %collective-permute-start.7) | collective-permute-done | bytes 24608 | tf_op jit(solution)/shard_map/ppermute | solution.py:362
  30.0 1.9 %scatter.1 = (f32[5,4,32,256]{3,2,1,0:T(8,128)}, f32[5,1024]{1,0:T(8,128)}) custom-call(f32[48,128]{1,0:T(8,128)S(1)} %solve.3.after.solved_own, f32[48,128]{1,0:T(8,128)S(1)} %collective-permute-done.7.returned, s32[1,1024]{1,0:T(1,128)S(1)} %get-tuple-element.23.cell, s32[1,1024]{1,0:T(1,128)S(1)} %get-tuple-element.24.patch, ...), custom_call_target="tpu_custom_call" | custom-call | tf_op jit(solution)/shard_map/scatter/pallas_call | solution.py:482
  (5 shorter events, 0.1 us)
Async XLA Ops:
  2.2 4.3 %collective-permute-start.4 = (f32[24,256]{1,0:T(8,128)S(1)}, f32[24,256]{1,0:T(8,128)S(1)}, u32[]{:S(2)}, u32[]{:S(2)}) collective-permute-start(f32[24,256]{1,0:T(8,128)S(1)} %get-tuple-element.25), channel_id=1, source_target_pairs={{0,16},{16,0},{32,48},{48,32},{1,17},{17,1},{33,49},{49,33},{2,18}... | collective-permute-start | bytes 73736 | tf_op jit(solution)/shard_map/ppermute | solution.py:362
  2.3 10.7 %collective-permute-start.2 = (f32[1,136,128]{2,1,0:T(8,128)S(1)}, f32[1,136,128]{2,1,0:T(8,128)S(1)}, u32[]{:S(2)}, u32[]{:S(2)}) collective-permute-start(f32[1,136,128]{2,1,0:T(8,128)S(1)} %get-tuple-element.19.first), channel_id=1, source_target_pairs={{0,12},{1,13},{2,14},{3,15},{4,8},{5,9},{6,10},{7,11},{8,4},{9,5},... | collective-permute-start | bytes 208904 | tf_op jit(solution)/shard_map/ppermute | solution.py:362
  5.4 7.6 %collective-permute-start.1 = (f32[1,136,128]{2,1,0:T(8,128)S(1)}, f32[1,136,128]{2,1,0:T(8,128)S(1)}, u32[]{:S(2)}, u32[]{:S(2)}) collective-permute-start(f32[1,136,128]{2,1,0:T(8,128)S(1)} %get-tuple-element.19.first), channel_id=1, source_target_pairs={{0,8},{1,9},{2,10},{3,11},{4,12},{5,13},{6,14},{7,15},{8,0},{9,1},... | collective-permute-start | bytes 208904 | tf_op jit(solution)/shard_map/ppermute | solution.py:362
  6.0 7.0 %collective-permute-start = (f32[1,136,128]{2,1,0:T(8,128)S(1)}, f32[1,136,128]{2,1,0:T(8,128)S(1)}, u32[]{:S(2)}, u32[]{:S(2)}) collective-permute-start(f32[1,136,128]{2,1,0:T(8,128)S(1)} %get-tuple-element.19.first), channel_id=1, source_target_pairs={{0,4},{1,5},{2,6},{3,7},{4,0},{5,1},{6,2},{7,3},{8,12},{9,13},{10,... | collective-permute-start | bytes 208904 | tf_op jit(solution)/shard_map/ppermute | solution.py:362
  8.0 7.2 %collective-permute-start.5 = (f32[24,256]{1,0:T(8,128)S(1)}, f32[24,256]{1,0:T(8,128)S(1)}, u32[]{:S(2)}, u32[]{:S(2)}) collective-permute-start(f32[24,256]{1,0:T(8,128)S(1)} %get-tuple-element.31), channel_id=1, source_target_pairs={{0,48},{16,32},{32,16},{48,0},{1,49},{17,33},{33,17},{49,1},{2,50}... | collective-permute-start | bytes 73736 | tf_op jit(solution)/shard_map/ppermute | solution.py:362
  13.1 10.4 %collective-permute-start.3 = (f32[528,128]{1,0:T(8,128)S(1)}, f32[528,128]{1,0:T(8,128)S(1)}, u32[]{:S(2)}, u32[]{:S(2)}) collective-permute-start(f32[528,128]{1,0:T(8,128)S(1)} %join.1.mine), channel_id=1, source_target_pairs={{0,1},{1,0},{2,3},{3,2},{4,5},{5,4},{6,7},{7,6},{8,9},{9,8},{10,11... | collective-permute-start | bytes 811016 | tf_op jit(solution)/shard_map/ppermute | solution.py:362
  15.3 3.5 %copy-start.2 = (f32[128,6]{0,1:T(8,128)S(1)}, f32[128,6]{0,1:T(8,128)}, u32[]{:S(2)}) copy-start(f32[128,6]{0,1:T(8,128)} %param.14) | copy-start | bytes 9220
  15.3 7.0 %collective-permute-start.6 = (f32[48,128]{1,0:T(8,128)S(1)}, f32[48,128]{1,0:T(8,128)S(1)}, u32[]{:S(2)}, u32[]{:S(2)}) collective-permute-start(f32[48,128]{1,0:T(8,128)S(1)} %get-tuple-element.32), channel_id=1, source_target_pairs={{0,2},{1,3},{2,0},{3,1},{4,6},{5,7},{6,4},{7,5},{8,10},{9,11},{10,... | collective-permute-start | bytes 73736 | tf_op jit(solution)/shard_map/ppermute | solution.py:362
  18.7 1.9 %copy-start = (f32[5,5]{1,0:T(8,128)S(1)}, f32[5,5]{1,0:T(8,128)}, u32[]{:S(2)}) copy-start(f32[5,5]{1,0:T(8,128)} %jacobian.1) | copy-start | bytes 304
  18.8 9.5 %collective-permute-start.9 = (f32[6,32,256]{2,1,0:T(8,128)S(1)}, f32[6,32,256]{2,1,0:T(8,128)S(1)}, u32[]{:S(2)}, u32[]{:S(2)}) collective-permute-start(f32[6,32,256]{2,1,0:T(8,128)S(1)} %get-tuple-element.35), channel_id=1, source_target_pairs={{0,192},{64,128},{128,64},{192,0},{1,193},{65,129},{129,65},{193,1... | collective-permute-start | bytes 589832 | tf_op jit(solution)/shard_map/ppermute | solution.py:362
  19.4 4.0 %copy-start.1 = (f32[5,128]{1,0:T(8,128)S(1)}, f32[5,128]{1,0:T(8,128)}, u32[]{:S(2)}) copy-start(f32[5,128]{1,0:T(8,128)} %readout.3) | copy-start | bytes 7684
  19.5 8.9 %collective-permute-start.8 = (f32[6,32,256]{2,1,0:T(8,128)S(1)}, f32[6,32,256]{2,1,0:T(8,128)S(1)}, u32[]{:S(2)}, u32[]{:S(2)}) collective-permute-start(f32[6,32,256]{2,1,0:T(8,128)S(1)} %get-tuple-element.33.faces), channel_id=1, source_target_pairs={{0,64},{64,0},{128,192},{192,128},{1,65},{65,1},{129,193},{193,129... | collective-permute-start | bytes 589832 | tf_op jit(solution)/shard_map/ppermute | solution.py:362
  25.0 5.0 %collective-permute-start.7 = (f32[48,128]{1,0:T(8,128)S(1)}, f32[48,128]{1,0:T(8,128)S(1)}, u32[]{:S(2)}, u32[]{:S(2)}) collective-permute-start(f32[48,128]{1,0:T(8,128)S(1)} %solve.2.refs_0_), channel_id=1, source_target_pairs={{0,2},{1,3},{2,0},{3,1},{4,6},{5,7},{6,4},{7,5},{8,10},{9,11},{10,... | collective-permute-start | bytes 73736 | tf_op jit(solution)/shard_map/ppermute | solution.py:362

commit v5 on v4

--- a/solution.py
+++ b/solution.py
@@ -146,7 +146,7 @@
         gather(adjoint, viscosity, cell, patch, *refs[3:])
 
 
-def faces_kernel(adjoint, viscosity, rows, before, x_one, x_two, sent):
+def faces_kernel(adjoint, viscosity, rows, before, base, x_one, x_two, sent):
     sent[...] = rows[...]
     odd_x = parity("gx")
     x_first, x_second = (1 - odd_x) * (CX - 1), odd_x * (CX - 1)
@@ -427,15 +427,24 @@
         cost_estimate=LONG,
         name="late_gather",
     )(*fields, *found)
+    base = pl.pallas_call(
+        interior,
+        out_shape=shape(5, CX, CY, CZ),
+        in_specs=[VMEM, VMEM, SMEM, ANY],
+        out_specs=VMEM,
+        compiler_params=PARAMS,
+        cost_estimate=SHORT,
+        name="interior",
+    )(adjoint, viscosity, flux_jacobian, mine)
     x_one, x_two, other = pl.pallas_call(
         faces_kernel,
         out_shape=(face_x, face_x, slots),
-        in_specs=[VMEM, VMEM, VMEM, ANY],
+        in_specs=[VMEM, VMEM, VMEM, ANY, ANY],
         out_specs=[VMEM] * 3,
         compiler_params=PARAMS,
         cost_estimate=LONG,
         name="faces",
-    )(adjoint, viscosity, other, y_two)
+    )(adjoint, viscosity, other, y_two, base)
     arrived = swapped(other, "gz", lambda i: i ^ 2)
     def solve(rows, *after):
         return pl.pallas_call(
@@ -448,16 +457,7 @@
             name="solve",
         )(mine, theirs, rows, lift_matrix, readout, *after)
 
-    base = pl.pallas_call(
-        interior,
-        out_shape=shape(5, CX, CY, CZ),
-        in_specs=[VMEM, VMEM, SMEM, ANY],
-        out_specs=VMEM,
-        compiler_params=PARAMS,
-        cost_estimate=SHORT,
-        name="interior",
-    )(adjoint, viscosity, flux_jacobian, x_one)
-    solved_arrived = solve(arrived, base)
+    solved_arrived = solve(arrived)
     returned = swapped(solved_arrived, "gz", lambda i: i ^ 2)
     solved_own = solve(own, solved_arrived)
     partial = pl.pallas_call(

time: 32.5 us -> 32.1 us (0.988); the launches traced: 32 us -> 32 us
  starting transfers between devices: 17.3 us -> 16.4 us
  waiting for transfers between devices: 3.62 us -> 4.41 us
    ppermute x10, starting transfers between devices: 17.3 us -> 16.4 us  [swapped(): lax.ppermute(array, axis, [(i, partner(i)) for i in range(lax.axis_size(a...]
    ppermute x10, waiting for transfers between devices: 3.62 us -> 4.41 us  [swapped(): lax.ppermute(array, axis, [(i, partner(i)) for i in range(lax.axis_size(a...]
where the time goes in v5:
time: 32.1 us; the launch traced here: 32 us
  starting transfers between devices  16.4 us (51%)
  Pallas kernels  10.2 us (32%)
  waiting for transfers between devices  4.41 us (14%)
  between operations  0.76 us (2%)
    ppermute x10, starting transfers between devices, swapped(): lax.ppermute(array, axis, [(i, partner(i)) for i in range(lax.axis_size(a...  16.4 us
    ppermute x10, waiting for transfers between devices, swapped(): lax.ppermute(array, axis, [(i, partner(i)) for i in range(lax.axis_size(a...  4.41 us
    pallas_call x2, Pallas kernels, solve(): pl.pallas_call(solve_kernel, out_shape=shape(5 * HALF + 8, CAP), in_specs...  3.12 us
    pallas_call x1, Pallas kernels, body(): pl.pallas_call(scatter_kernel, out_shape=(shape(5, CX, CY, CZ), shape(5,...  1.92 us
    pallas_call x1, Pallas kernels, body(): pl.pallas_call(interior, out_shape=shape(5, CX, CY, CZ), in_specs=[VMEM,...  1.64 us
    pallas_call x1, Pallas kernels, body(): pl.pallas_call(load_kernel, out_shape=tuple((shape(*a.shape, dtype=a.dtyp...  1.55 us
    pallas_call x1, Pallas kernels, body(): pl.pallas_call(early_kernel, out_shape=(face_y,) + gathered, in_specs=[VM...  1.52 us
  transfers between devices with their start and end apart: 10, of which 3 were waited for; matrix products, arithmetic and copies ran while one was open for 0% of the time, Pallas kernels for 21%

profile of v5, /device:TPU:4, one launch (start us, length us, event | category | flops | bytes accessed | tf_op | source)
XLA Modules:
  0.0 32.0 jit_solution(5995483934807206382)
XLA Ops:
  0.6 1.6 %load.1 = (f32[5,4,32,256]{3,2,1,0:T(8,128)S(1)}, f32[4,32,256]{2,1,0:T(8,128)S(1)}, s32[1,1024]{1,0:T(1,128)S(1)}, s32[1,1024]{1,0:T(1,128)S(1)}, f32[1,136,128...) custom-call(f32[5,4,32,256]{3,2,1,0:T(8,128)} %adjoint_hbm.1, f32[4,32,256]{2,1,0:T(8,128)} %viscosity_hbm.1, ...), custom_call_target="tpu_custom_call" | custom-call | tf_op jit(solution)/shard_map/load/pallas_call | solution.py:387
  2.2 0.1 collective-permute-start.4
  2.3 3.1 %collective-permute-start.2 = (f32[1,136,128]{2,1,0:T(8,128)S(1)}, f32[1,136,128]{2,1,0:T(8,128)S(1)}, u32[]{:S(2)}, u32[]{:S(2)}) collective-permute-start(f32[1,136,128]{2,1,0:T(8,128)S(1)} %get-tuple-element.19.first), channel_id=1, source_target_pairs={{0,12},{1,13},{2,14},{3,15},{4,8},{5,9},{6,10},{7,11},{8,4},{9,5},... | collective-permute-start | bytes 208904 | tf_op jit(solution)/shard_map/ppermute | solution.py:362
  5.4 0.6 %collective-permute-start.1 = (f32[1,136,128]{2,1,0:T(8,128)S(1)}, f32[1,136,128]{2,1,0:T(8,128)S(1)}, u32[]{:S(2)}, u32[]{:S(2)}) collective-permute-start(f32[1,136,128]{2,1,0:T(8,128)S(1)} %get-tuple-element.19.first), channel_id=1, source_target_pairs={{0,8},{1,9},{2,10},{3,11},{4,12},{5,13},{6,14},{7,15},{8,0},{9,1},... | collective-permute-start | bytes 208904 | tf_op jit(solution)/shard_map/ppermute | solution.py:362
  6.0 0.5 %collective-permute-start = (f32[1,136,128]{2,1,0:T(8,128)S(1)}, f32[1,136,128]{2,1,0:T(8,128)S(1)}, u32[]{:S(2)}, u32[]{:S(2)}) collective-permute-start(f32[1,136,128]{2,1,0:T(8,128)S(1)} %get-tuple-element.19.first), channel_id=1, source_target_pairs={{0,4},{1,5},{2,6},{3,7},{4,0},{5,1},{6,2},{7,3},{8,12},{9,13},{10,... | collective-permute-start | bytes 208904 | tf_op jit(solution)/shard_map/ppermute | solution.py:362
  6.5 0.0 collective-permute-done.4.before.joined.y_one
  6.5 1.5 %early_gather.1 = (f32[24,256]{1,0:T(8,128)S(1)}, f32[48,128]{1,0:T(8,128)S(1)}, f32[48,128]{1,0:T(8,128)S(1)}, s32[1,1024]{1,0:T(1,128)S(1)}) custom-call(f32[5,4,32,256]{3,2,1,0:T(8,128)S(1)} %get-tuple-element.21.adjoint, f32[4,32,256]{2,1,0:T(8,128)S(1)} %get-tuple-element.22.viscosity, s32[1,1024]{1,0:T(1,128)S(1)} %get-tuple-element.23.cell, ...), custom_call_target="tpu_custom_call" | custom-call | tf_op jit(solution)/shard_map/early_gather/pallas_call | solution.py:412
  8.0 5.0 %collective-permute-start.5 = (f32[24,256]{1,0:T(8,128)S(1)}, f32[24,256]{1,0:T(8,128)S(1)}, u32[]{:S(2)}, u32[]{:S(2)}) collective-permute-start(f32[24,256]{1,0:T(8,128)S(1)} %get-tuple-element.31), channel_id=1, source_target_pairs={{0,48},{16,32},{32,16},{48,0},{1,49},{17,33},{33,17},{49,1},{2,50}... | collective-permute-start | bytes 73736 | tf_op jit(solution)/shard_map/ppermute | solution.py:362
  13.0 0.0 collective-permute-done.2.fourth
  13.0 0.0 collective-permute-done.1.third
  13.0 0.0 collective-permute-done.second
  13.1 0.0 copy-start
  13.1 1.1 %collective-permute-start.3 = (f32[528,128]{1,0:T(8,128)S(1)}, f32[528,128]{1,0:T(8,128)S(1)}, u32[]{:S(2)}, u32[]{:S(2)}) collective-permute-start(f32[528,128]{1,0:T(8,128)S(1)} %join.1.faces.mine), channel_id=1, source_target_pairs={{0,1},{1,0},{2,3},{3,2},{4,5},{5,4},{6,7},{7,6},{8,9},{9,8},{10,11... | collective-permute-start | bytes 811016 | tf_op jit(solution)/shard_map/ppermute | solution.py:362
  14.2 0.0 copy-done
  14.2 1.6 %interior.1.base = f32[5,4,32,256]{3,2,1,0:T(8,128)S(1)} custom-call(f32[5,4,32,256]{3,2,1,0:T(8,128)S(1)} %get-tuple-element.21.adjoint, f32[4,32,256]{2,1,0:T(8,128)S(1)} %get-tuple-element.22.viscosity, f32[5,5]{1,0:T(8,128)S(1)} %copy-done, f32[528,128]{1,0:T(8,128)S(1)} %join.1.faces.mine), custom_call_target="tpu_custom_call" | custom-call | flops 1000 | bytes 1000 | tf_op jit(solution)/shard_map/interior/pallas_call | solution.py:430
  15.8 0.0 collective-permute-done.5.before.y_two
  15.9 0.0 copy-start.2
  15.9 0.0 copy-start.1
  15.9 3.1 %collective-permute-start.6 = (f32[48,128]{1,0:T(8,128)S(1)}, f32[48,128]{1,0:T(8,128)S(1)}, u32[]{:S(2)}, u32[]{:S(2)}) collective-permute-start(f32[48,128]{1,0:T(8,128)S(1)} %get-tuple-element.32), channel_id=1, source_target_pairs={{0,2},{1,3},{2,0},{3,1},{4,6},{5,7},{6,4},{7,5},{8,10},{9,11},{10,... | collective-permute-start | bytes 73736 | tf_op jit(solution)/shard_map/ppermute | solution.py:362
  19.0 0.1 copy.11.lift
  19.1 1.3 %collective-permute-start.8 = (f32[6,32,256]{2,1,0:T(8,128)S(1)}, f32[6,32,256]{2,1,0:T(8,128)S(1)}, u32[]{:S(2)}, u32[]{:S(2)}) collective-permute-start(f32[6,32,256]{2,1,0:T(8,128)S(1)} %get-tuple-element.34), channel_id=1, source_target_pairs={{0,64},{64,0},{128,192},{192,128},{1,65},{65,1},{129,193},{193,129... | collective-permute-start | bytes 589832 | tf_op jit(solution)/shard_map/ppermute | solution.py:362
  20.4 0.0 collective-permute-start.9
  20.4 1.1 %collective-permute-done.6.rows = f32[48,128]{1,0:T(8,128)S(1)} collective-permute-done((f32[48,128]{1,0:T(8,128)S(1)}, f32[48,128]{1,0:T(8,128)S(1)}, u32[]{:S(2)}, u32[]{:S(2)}) %collective-permute-start.6) | collective-permute-done | bytes 24608 | tf_op jit(solution)/shard_map/ppermute | solution.py:362
  21.5 2.0 %collective-permute-done.3.theirs.z_one = f32[528,128]{1,0:T(8,128)S(1)} collective-permute-done((f32[528,128]{1,0:T(8,128)S(1)}, f32[528,128]{1,0:T(8,128)S(1)}, u32[]{:S(2)}, u32[]{:S(2)}) %collective-permute-start.3) | collective-permute-done | bytes 270368 | tf_op jit(solution)/shard_map/ppermute | solution.py:362
  23.5 1.6 %solve.2.refs_0_ = f32[48,128]{1,0:T(8,128)S(1)} custom-call(f32[528,128]{1,0:T(8,128)S(1)} %join.1.faces.mine, f32[528,128]{1,0:T(8,128)S(1)} %collective-permute-done.3.theirs.z_one, f32[48,128]{1,0:T(8,128)S(1)} %collective-permute-done.6.rows, f32[128,6]{1,0:T(8,128)S(1)} %copy.11.lift, f32[5,128]{1,0:T(8,128)S(1)} %copy-done.1), custom_call_target="tpu_custom_call" | custom-call | flops 20000000000 | bytes 60000000 | tf_op jit(solution)/shard_map/solve/pallas_call | solution.py:450
  25.1 1.7 %collective-permute-start.7 = (f32[48,128]{1,0:T(8,128)S(1)}, f32[48,128]{1,0:T(8,128)S(1)}, u32[]{:S(2)}, u32[]{:S(2)}) collective-permute-start(f32[48,128]{1,0:T(8,128)S(1)} %solve.2.refs_0_), channel_id=1, source_target_pairs={{0,2},{1,3},{2,0},{3,1},{4,6},{5,7},{6,4},{7,5},{8,10},{9,11},{10,... | collective-permute-start | bytes 73736 | tf_op jit(solution)/shard_map/ppermute | solution.py:362
  26.7 1.6 %solve.3.after.solved_own = f32[48,128]{1,0:T(8,128)S(1)} custom-call(f32[528,128]{1,0:T(8,128)S(1)} %join.1.faces.mine, f32[528,128]{1,0:T(8,128)S(1)} %collective-permute-done.3.theirs.z_one, f32[48,128]{1,0:T(8,128)S(1)} %get-tuple-element.29.rows, f32[128,6]{1,0:T(8,128)S(1)} %copy.11.lift, f32[5,128]{1,0:T(8,128)S(1)} %copy-done.1, ...), custom_call_target="tpu_custom_call" | custom-call | flops 20000000000 | bytes 60000000 | tf_op jit(solution)/shard_map/solve/pallas_call | solution.py:450
  28.3 0.0 collective-permute-done.8.x_one
  28.3 0.0 collective-permute-done.9.x_two
  28.3 0.4 %stencil.1.partial = f32[5,4,32,256]{3,2,1,0:T(8,128)S(1)} custom-call(f32[5,4,32,256]{3,2,1,0:T(8,128)S(1)} %get-tuple-element.21.adjoint, f32[4,32,256]{2,1,0:T(8,128)S(1)} %get-tuple-element.22.viscosity, f32[5,4,32,256]{3,2,1,0:T(8,128)S(1)} %interior.1.base, f32[6,32,256]{2,1,0:T(8,128)S(1)} %collective-permute-done.8.x_one, ...), custom_call_target="tpu_custom_call" | custom-call | flops 20000000000 | bytes 60000000 | tf_op jit(solution)/shard_map/stencil/pallas_call | solution.py:463
  28.8 1.3 %collective-permute-done.7.returned = f32[48,128]{1,0:T(8,128)S(1)} collective-permute-done((f32[48,128]{1,0:T(8,128)S(1)}, f32[48,128]{1,0:T(8,128)S(1)}, u32[]{:S(2)}, u32[]{:S(2)}) %collective-permute-start.7) | collective-permute-done | bytes 24608 | tf_op jit(solution)/shard_map/ppermute | solution.py:362
  30.0 1.9 %scatter.1 = (f32[5,4,32,256]{3,2,1,0:T(8,128)}, f32[5,1024]{1,0:T(8,128)}) custom-call(f32[48,128]{1,0:T(8,128)S(1)} %solve.3.after.solved_own, f32[48,128]{1,0:T(8,128)S(1)} %collective-permute-done.7.returned, s32[1,1024]{1,0:T(1,128)S(1)} %get-tuple-element.23.cell, s32[1,1024]{1,0:T(1,128)S(1)} %get-tuple-element.24.patch, ...), custom_call_target="tpu_custom_call" | custom-call | tf_op jit(solution)/shard_map/scatter/pallas_call | solution.py:482
  (5 shorter events, 0.1 us)
Async XLA Ops:
  2.2 4.3 %collective-permute-start.4 = (f32[24,256]{1,0:T(8,128)S(1)}, f32[24,256]{1,0:T(8,128)S(1)}, u32[]{:S(2)}, u32[]{:S(2)}) collective-permute-start(f32[24,256]{1,0:T(8,128)S(1)} %get-tuple-element.25), channel_id=1, source_target_pairs={{0,16},{16,0},{32,48},{48,32},{1,17},{17,1},{33,49},{49,33},{2,18}... | collective-permute-start | bytes 73736 | tf_op jit(solution)/shard_map/ppermute | solution.py:362
  2.3 10.7 %collective-permute-start.2 = (f32[1,136,128]{2,1,0:T(8,128)S(1)}, f32[1,136,128]{2,1,0:T(8,128)S(1)}, u32[]{:S(2)}, u32[]{:S(2)}) collective-permute-start(f32[1,136,128]{2,1,0:T(8,128)S(1)} %get-tuple-element.19.first), channel_id=1, source_target_pairs={{0,12},{1,13},{2,14},{3,15},{4,8},{5,9},{6,10},{7,11},{8,4},{9,5},... | collective-permute-start | bytes 208904 | tf_op jit(solution)/shard_map/ppermute | solution.py:362
  5.4 7.6 %collective-permute-start.1 = (f32[1,136,128]{2,1,0:T(8,128)S(1)}, f32[1,136,128]{2,1,0:T(8,128)S(1)}, u32[]{:S(2)}, u32[]{:S(2)}) collective-permute-start(f32[1,136,128]{2,1,0:T(8,128)S(1)} %get-tuple-element.19.first), channel_id=1, source_target_pairs={{0,8},{1,9},{2,10},{3,11},{4,12},{5,13},{6,14},{7,15},{8,0},{9,1},... | collective-permute-start | bytes 208904 | tf_op jit(solution)/shard_map/ppermute | solution.py:362
  6.0 7.0 %collective-permute-start = (f32[1,136,128]{2,1,0:T(8,128)S(1)}, f32[1,136,128]{2,1,0:T(8,128)S(1)}, u32[]{:S(2)}, u32[]{:S(2)}) collective-permute-start(f32[1,136,128]{2,1,0:T(8,128)S(1)} %get-tuple-element.19.first), channel_id=1, source_target_pairs={{0,4},{1,5},{2,6},{3,7},{4,0},{5,1},{6,2},{7,3},{8,12},{9,13},{10,... | collective-permute-start | bytes 208904 | tf_op jit(solution)/shard_map/ppermute | solution.py:362
  8.0 7.8 %collective-permute-start.5 = (f32[24,256]{1,0:T(8,128)S(1)}, f32[24,256]{1,0:T(8,128)S(1)}, u32[]{:S(2)}, u32[]{:S(2)}) collective-permute-start(f32[24,256]{1,0:T(8,128)S(1)} %get-tuple-element.31), channel_id=1, source_target_pairs={{0,48},{16,32},{32,16},{48,0},{1,49},{17,33},{33,17},{49,1},{2,50}... | collective-permute-start | bytes 73736 | tf_op jit(solution)/shard_map/ppermute | solution.py:362
  13.1 1.1 %copy-start = (f32[5,5]{1,0:T(8,128)S(1)}, f32[5,5]{1,0:T(8,128)}, u32[]{:S(2)}) copy-start(f32[5,5]{1,0:T(8,128)} %jacobian.1) | copy-start | bytes 304
  13.1 10.4 %collective-permute-start.3 = (f32[528,128]{1,0:T(8,128)S(1)}, f32[528,128]{1,0:T(8,128)S(1)}, u32[]{:S(2)}, u32[]{:S(2)}) collective-permute-start(f32[528,128]{1,0:T(8,128)S(1)} %join.1.faces.mine), channel_id=1, source_target_pairs={{0,1},{1,0},{2,3},{3,2},{4,5},{5,4},{6,7},{7,6},{8,9},{9,8},{10,11... | collective-permute-start | bytes 811016 | tf_op jit(solution)/shard_map/ppermute | solution.py:362
  15.9 3.1 %copy-start.2 = (f32[128,6]{0,1:T(8,128)S(1)}, f32[128,6]{0,1:T(8,128)}, u32[]{:S(2)}) copy-start(f32[128,6]{0,1:T(8,128)} %param.14) | copy-start | bytes 9220
  15.9 7.6 %copy-start.1 = (f32[5,128]{1,0:T(8,128)S(1)}, f32[5,128]{1,0:T(8,128)}, u32[]{:S(2)}) copy-start(f32[5,128]{1,0:T(8,128)} %readout.3) | copy-start | bytes 7684
  15.9 5.6 %collective-permute-start.6 = (f32[48,128]{1,0:T(8,128)S(1)}, f32[48,128]{1,0:T(8,128)S(1)}, u32[]{:S(2)}, u32[]{:S(2)}) collective-permute-start(f32[48,128]{1,0:T(8,128)S(1)} %get-tuple-element.32), channel_id=1, source_target_pairs={{0,2},{1,3},{2,0},{3,1},{4,6},{5,7},{6,4},{7,5},{8,10},{9,11},{10,... | collective-permute-start | bytes 73736 | tf_op jit(solution)/shard_map/ppermute | solution.py:362
  19.1 9.2 %collective-permute-start.8 = (f32[6,32,256]{2,1,0:T(8,128)S(1)}, f32[6,32,256]{2,1,0:T(8,128)S(1)}, u32[]{:S(2)}, u32[]{:S(2)}) collective-permute-start(f32[6,32,256]{2,1,0:T(8,128)S(1)} %get-tuple-element.34), channel_id=1, source_target_pairs={{0,64},{64,0},{128,192},{192,128},{1,65},{65,1},{129,193},{193,129... | collective-permute-start | bytes 589832 | tf_op jit(solution)/shard_map/ppermute | solution.py:362
  20.4 7.9 %collective-permute-start.9 = (f32[6,32,256]{2,1,0:T(8,128)S(1)}, f32[6,32,256]{2,1,0:T(8,128)S(1)}, u32[]{:S(2)}, u32[]{:S(2)}) collective-permute-start(f32[6,32,256]{2,1,0:T(8,128)S(1)} %get-tuple-element.35), channel_id=1, source_target_pairs={{0,192},{64,128},{128,64},{192,0},{1,193},{65,129},{129,65},{193,1... | collective-permute-start | bytes 589832 | tf_op jit(solution)/shard_map/ppermute | solution.py:362
  25.1 5.0 %collective-permute-start.7 = (f32[48,128]{1,0:T(8,128)S(1)}, f32[48,128]{1,0:T(8,128)S(1)}, u32[]{:S(2)}, u32[]{:S(2)}) collective-permute-start(f32[48,128]{1,0:T(8,128)S(1)} %solve.2.refs_0_), channel_id=1, source_target_pairs={{0,2},{1,3},{2,0},{3,1},{4,6},{5,7},{6,4},{7,5},{8,10},{9,11},{10,... | collective-permute-start | bytes 73736 | tf_op jit(solution)/shard_map/ppermute | solution.py:362

commit v6 on v5

--- a/solution.py
+++ b/solution.py
@@ -57,6 +57,16 @@
 def slot_group(patches):
     apart = patches ^ lax.axis_index("gz")
     return ((apart >> 1) & 1) * HALF + (apart & 1) * (HALF // 2) + (apart >> 2)
+
+
+def z_face(adjoint, viscosity, far):
+    columns = lax.broadcasted_iota(jnp.int32, (ROWS, 128), 1)
+    face = jnp.zeros((ROWS, 128), F32)
+    for f in range(6):
+        field = (viscosity[...] if f == 5 else adjoint[f]).reshape(ROWS, CZ)
+        edge = jnp.where(far == 1, field[:, CZ - 1 : CZ], field[:, 0:1])
+        face = jnp.where(columns == f, edge, face)
+    return jnp.transpose(face)[:8]
 
 
 def load_kernel(
@@ -71,7 +81,6 @@
     patch,
     package,
     y_one,
-    z_one,
     arrivals,
 ):
     pairs = (
@@ -96,22 +105,13 @@
             low, high = field[x, 0:1, :], field[x, CY - 1 : CY, :]
             at = slice(f * CX + x, f * CX + x + 1)
             y_one[at, :] = jnp.where(odd_y == 1, low, high)
-    columns = lax.broadcasted_iota(jnp.int32, (ROWS, 128), 1)
-    z_low = z_high = jnp.zeros((ROWS, 128), F32)
-    for f in range(6):
-        field = (viscosity[...] if f == 5 else adjoint[f]).reshape(ROWS, CZ)
-        z_low = jnp.where(columns == f, field[:, 0:1], z_low)
-        z_high = jnp.where(columns == f, field[:, CZ - 1 : CZ], z_high)
-    z_low, z_high = jnp.transpose(z_low)[:8], jnp.transpose(z_high)[:8]
-    odd_z = parity("gz") == 1
-    z_one[...] = jnp.where(odd_z, z_low, z_high)
-    package[0, PROF:, :] = jnp.where(odd_z, z_high, z_low)
+    package[0, PROF:, :] = z_face(adjoint, viscosity, parity("gz"))
     for copy in copies[2:]:
         copy.wait()
 
 
 def early_kernel(
-    adjoint, viscosity, cell, patch, before, joined, y_two, own, other, ranks
+    adjoint, viscosity, cell, patch, before, joined, y_two, own, other, ranks, z_one
 ):
     odd_y = parity("gy")
     for f in range(6):
@@ -120,7 +120,7 @@
             low, high = field[x, 0:1, :], field[x, CY - 1 : CY, :]
             at = slice(f * CX + x, f * CX + x + 1)
             y_two[at, :] = jnp.where(odd_y == 1, high, low)
-    results = (own, other, ranks)
+    results = (own, other, ranks, z_one)
     near = lax.axis_index("gy") < lax.axis_size("gy") // 2
 
     @pl.when(near)
@@ -138,12 +138,12 @@
 
     @pl.when(near)
     def _():
-        for found, result in zip(refs[:3], refs[3:]):
+        for found, result in zip(refs[:4], refs[4:]):
             result[...] = found[...]
 
     @pl.when(jnp.logical_not(near))
     def _():
-        gather(adjoint, viscosity, cell, patch, *refs[3:])
+        gather(adjoint, viscosity, cell, patch, *refs[4:])
 
 
 def faces_kernel(adjoint, viscosity, rows, before, base, x_one, x_two, sent):
@@ -156,7 +156,8 @@
         x_two[f] = field[x_second]
 
 
-def gather(adjoint, viscosity, cell, patch, own, other, ranks):
+def gather(adjoint, viscosity, cell, patch, own, other, ranks, z_one):
+    z_one[...] = z_face(adjoint, viscosity, 1 - parity("gz"))
     cells = cell[...]
     patches = slot_group(patch[...])
     row = cells >> 8
@@ -384,12 +385,12 @@
     slots, numbers = shape(HALF * 6, CAP), shape(1, FACES, dtype=jnp.int32)
     arrays = [adjoint, viscosity, cell, patch, wall_inverse]
     package = shape(1, PROF + 8, PROF)
-    adjoint, viscosity, cell, patch, package, y_one, z_one = pl.pallas_call(
+    adjoint, viscosity, cell, patch, package, y_one = pl.pallas_call(
         load_kernel,
         out_shape=tuple(shape(*a.shape, dtype=a.dtype) for a in arrays[:4])
-        + (package, face_y, face_z),
+        + (package, face_y),
         in_specs=[HBM] * 5,
-        out_specs=[VMEM] * 7,
+        out_specs=[VMEM] * 6,
         scratch_shapes=[pltpu.SemaphoreType.DMA((5,))],
         compiler_params=PARAMS,
         name="load",
@@ -397,6 +398,27 @@
     blocks = [package]
     for step in range(1, 4):
         blocks.append(swapped(package, "gz", lambda i: i ^ (4 * step)))
+    fields = (adjoint, viscosity, cell, patch)
+    gathered = (slots, slots, numbers, face_z)
+    y_one = first_side(y_one, "gy")
+    y_two, *found = pl.pallas_call(
+        early_kernel,
+        out_shape=(face_y,) + gathered,
+        in_specs=[VMEM] * 4 + [ANY] * 2,
+        out_specs=[VMEM] * 5,
+        compiler_params=PARAMS,
+        name="early_gather",
+    )(*fields, y_one, y_one)
+    y_two = second_side(y_two, "gy")
+    own, other, ranks, z_one = pl.pallas_call(
+        late_kernel,
+        out_shape=gathered,
+        in_specs=[VMEM] * 8,
+        out_specs=[VMEM] * 4,
+        compiler_params=PARAMS,
+        cost_estimate=LONG,
+        name="late_gather",
+    )(*fields, *found)
     mine = pl.pallas_call(
         join_kernel,
         out_shape=shape(4 * PROF + 16, PROF),
@@ -406,27 +428,6 @@
         name="join",
     )(*blocks, z_one)
     theirs = swapped(mine, "gz", lambda i: i ^ 1)
-    fields = (adjoint, viscosity, cell, patch)
-    gathered = (slots, slots, numbers)
-    y_one = first_side(y_one, "gy")
-    y_two, *found = pl.pallas_call(
-        early_kernel,
-        out_shape=(face_y,) + gathered,
-        in_specs=[VMEM] * 4 + [ANY] * 2,
-        out_specs=[VMEM] * 4,
-        compiler_params=PARAMS,
-        name="early_gather",
-    )(*fields, y_one, y_one)
-    y_two = second_side(y_two, "gy")
-    own, other, ranks = pl.pallas_call(
-        late_kernel,
-        out_shape=gathered,
-        in_specs=[VMEM] * 7,
-        out_specs=[VMEM] * 3,
-        compiler_params=PARAMS,
-        cost_estimate=LONG,
-        name="late_gather",
-    )(*fields, *found)
     base = pl.pallas_call(
         interior,
         out_shape=shape(5, CX, CY, CZ),

time: 32.1 us -> 32.3 us (level)
  no operation moved by 1% of the time
where the time goes in v6:
time: 32.3 us; the launch traced here: 32.2 us
  starting transfers between devices  16.4 us (51%)
  Pallas kernels  10.4 us (32%)
  waiting for transfers between devices  4.41 us (14%)
  between operations  0.76 us (2%)
    ppermute x10, starting transfers between devices, swapped(): lax.ppermute(array, axis, [(i, partner(i)) for i in range(lax.axis_size(a...  16.4 us
    ppermute x10, waiting for transfers between devices, swapped(): lax.ppermute(array, axis, [(i, partner(i)) for i in range(lax.axis_size(a...  4.41 us
    pallas_call x2, Pallas kernels, solve(): pl.pallas_call(solve_kernel, out_shape=shape(5 * HALF + 8, CAP), in_specs...  3.12 us
    pallas_call x1, Pallas kernels, body(): pl.pallas_call(scatter_kernel, out_shape=(shape(5, CX, CY, CZ), shape(5,...  1.92 us
    pallas_call x1, Pallas kernels, body(): pl.pallas_call(load_kernel, out_shape=tuple((shape(*a.shape, dtype=a.dtyp...  1.76 us
    pallas_call x1, Pallas kernels, body(): pl.pallas_call(interior, out_shape=shape(5, CX, CY, CZ), in_specs=[VMEM,...  1.64 us
    pallas_call x1, Pallas kernels, body(): pl.pallas_call(early_kernel, out_shape=(face_y,) + gathered, in_specs=[VM...  1.53 us
  transfers between devices with their start and end apart: 10, of which 3 were waited for; matrix products, arithmetic and copies ran while one was open for 0% of the time, Pallas kernels for 21%

profile of v6, /device:TPU:4, one launch (start us, length us, event | category | flops | bytes accessed | tf_op | source)
XLA Modules:
  0.0 32.2 jit_solution(15353148518989828261)
XLA Ops:
  0.6 1.8 %load.1 = (f32[5,4,32,256]{3,2,1,0:T(8,128)S(1)}, f32[4,32,256]{2,1,0:T(8,128)S(1)}, s32[1,1024]{1,0:T(1,128)S(1)}, s32[1,1024]{1,0:T(1,128)S(1)}, f32[1,136,128]{2,1,0:T(8,128)S(1)}, /*index=5*/f32[24,256]{1,0:T(8,128)S(1)}) custom-call(f32[5,4,32,256]{3,2,1,0:T(8,128)} %adjoint_hbm.1, f32[4,32,256]{2,1,0:T(8,128)} %viscosity_hbm.1, s32[1,1024]{1,0:T(1,128)} %bitcast.2, ...), custom_call_target="tpu_custom_call" | custom-call | tf_op jit(solution)/shard_map/load/pallas_call | solution.py:388
  2.4 0.1 collective-permute-start.3
  2.5 3.1 %collective-permute-start.2 = (f32[1,136,128]{2,1,0:T(8,128)S(1)}, f32[1,136,128]{2,1,0:T(8,128)S(1)}, u32[]{:S(2)}, u32[]{:S(2)}) collective-permute-start(f32[1,136,128]{2,1,0:T(8,128)S(1)} %get-tuple-element.20.first), channel_id=1, source_target_pairs={{0,12},{1,13},{2,14},{3,15},{4,8},{5,9},{6,10},{7,11},{8,4},{9,5},... | collective-permute-start | bytes 208904 | tf_op jit(solution)/shard_map/ppermute | solution.py:363
  5.6 0.6 %collective-permute-start.1 = (f32[1,136,128]{2,1,0:T(8,128)S(1)}, f32[1,136,128]{2,1,0:T(8,128)S(1)}, u32[]{:S(2)}, u32[]{:S(2)}) collective-permute-start(f32[1,136,128]{2,1,0:T(8,128)S(1)} %get-tuple-element.20.first), channel_id=1, source_target_pairs={{0,8},{1,9},{2,10},{3,11},{4,12},{5,13},{6,14},{7,15},{8,0},{9,1},... | collective-permute-start | bytes 208904 | tf_op jit(solution)/shard_map/ppermute | solution.py:363
  6.2 0.5 %collective-permute-start = (f32[1,136,128]{2,1,0:T(8,128)S(1)}, f32[1,136,128]{2,1,0:T(8,128)S(1)}, u32[]{:S(2)}, u32[]{:S(2)}) collective-permute-start(f32[1,136,128]{2,1,0:T(8,128)S(1)} %get-tuple-element.20.first), channel_id=1, source_target_pairs={{0,4},{1,5},{2,6},{3,7},{4,0},{5,1},{6,2},{7,3},{8,12},{9,13},{10,... | collective-permute-start | bytes 208904 | tf_op jit(solution)/shard_map/ppermute | solution.py:363
  6.7 0.0 collective-permute-done.3.before.joined.y_one
  6.7 1.5 %early_gather.1 = (f32[24,256]{1,0:T(8,128)S(1)}, f32[48,128]{1,0:T(8,128)S(1)}, f32[48,128]{1,0:T(8,128)S(1)}, s32[1,1024]{1,0:T(1,128)S(1)}, f32[8,128]{1,0:T(8,128)S(1)}) custom-call(f32[5,4,32,256]{3,2,1,0:T(8,128)S(1)} %get-tuple-element.21.adjoint, f32[4,32,256]{2,1,0:T(8,128)S(1)} %get-tuple-element.22.viscosity, ...), custom_call_target="tpu_custom_call" | custom-call | tf_op jit(solution)/shard_map/early_gather/pallas_call | solution.py:404
  8.2 5.0 %collective-permute-start.5 = (f32[24,256]{1,0:T(8,128)S(1)}, f32[24,256]{1,0:T(8,128)S(1)}, u32[]{:S(2)}, u32[]{:S(2)}) collective-permute-start(f32[24,256]{1,0:T(8,128)S(1)} %get-tuple-element.33), channel_id=1, source_target_pairs={{0,48},{16,32},{32,16},{48,0},{1,49},{17,33},{33,17},{49,1},{2,50}... | collective-permute-start | bytes 73736 | tf_op jit(solution)/shard_map/ppermute | solution.py:363
  13.2 0.0 collective-permute-done.2.fourth
  13.2 0.0 collective-permute-done.1.third
  13.2 0.0 collective-permute-done.second
  13.3 0.0 copy-start
  13.3 1.1 %collective-permute-start.4 = (f32[528,128]{1,0:T(8,128)S(1)}, f32[528,128]{1,0:T(8,128)S(1)}, u32[]{:S(2)}, u32[]{:S(2)}) collective-permute-start(f32[528,128]{1,0:T(8,128)S(1)} %join.1.faces.mine), channel_id=1, source_target_pairs={{0,1},{1,0},{2,3},{3,2},{4,5},{5,4},{6,7},{7,6},{8,9},{9,8},{10,11... | collective-permute-start | bytes 811016 | tf_op jit(solution)/shard_map/ppermute | solution.py:363
  14.4 1.6 %interior.1.base = f32[5,4,32,256]{3,2,1,0:T(8,128)S(1)} custom-call(f32[5,4,32,256]{3,2,1,0:T(8,128)S(1)} %get-tuple-element.21.adjoint, f32[4,32,256]{2,1,0:T(8,128)S(1)} %get-tuple-element.22.viscosity, f32[5,5]{1,0:T(8,128)S(1)} %copy-done, f32[528,128]{1,0:T(8,128)S(1)} %join.1.faces.mine), custom_call_target="tpu_custom_call" | custom-call | flops 1000 | bytes 1000 | tf_op jit(solution)/shard_map/interior/pallas_call | solution.py:431
  16.1 0.0 collective-permute-done.5.before.y_two
  16.1 0.0 copy-start.2
  16.1 0.0 copy-start.1
  16.1 3.1 %collective-permute-start.6 = (f32[48,128]{1,0:T(8,128)S(1)}, f32[48,128]{1,0:T(8,128)S(1)}, u32[]{:S(2)}, u32[]{:S(2)}) collective-permute-start(f32[48,128]{1,0:T(8,128)S(1)} %get-tuple-element.34), channel_id=1, source_target_pairs={{0,2},{1,3},{2,0},{3,1},{4,6},{5,7},{6,4},{7,5},{8,10},{9,11},{10,... | collective-permute-start | bytes 73736 | tf_op jit(solution)/shard_map/ppermute | solution.py:363
  19.2 0.0 copy-done.2
  19.2 0.1 copy.11.lift
  19.3 1.3 %collective-permute-start.8 = (f32[6,32,256]{2,1,0:T(8,128)S(1)}, f32[6,32,256]{2,1,0:T(8,128)S(1)}, u32[]{:S(2)}, u32[]{:S(2)}) collective-permute-start(f32[6,32,256]{2,1,0:T(8,128)S(1)} %get-tuple-element.36), channel_id=1, source_target_pairs={{0,64},{64,0},{128,192},{192,128},{1,65},{65,1},{129,193},{193,129... | collective-permute-start | bytes 589832 | tf_op jit(solution)/shard_map/ppermute | solution.py:363
  20.6 0.0 collective-permute-start.9
  20.6 1.1 %collective-permute-done.6.rows = f32[48,128]{1,0:T(8,128)S(1)} collective-permute-done((f32[48,128]{1,0:T(8,128)S(1)}, f32[48,128]{1,0:T(8,128)S(1)}, u32[]{:S(2)}, u32[]{:S(2)}) %collective-permute-start.6) | collective-permute-done | bytes 24608 | tf_op jit(solution)/shard_map/ppermute | solution.py:363
  21.7 2.0 %collective-permute-done.4.theirs.z_one = f32[528,128]{1,0:T(8,128)S(1)} collective-permute-done((f32[528,128]{1,0:T(8,128)S(1)}, f32[528,128]{1,0:T(8,128)S(1)}, u32[]{:S(2)}, u32[]{:S(2)}) %collective-permute-start.4) | collective-permute-done | bytes 270368 | tf_op jit(solution)/shard_map/ppermute | solution.py:363
  23.7 1.6 %solve.2.refs_0_ = f32[48,128]{1,0:T(8,128)S(1)} custom-call(f32[528,128]{1,0:T(8,128)S(1)} %join.1.faces.mine, f32[528,128]{1,0:T(8,128)S(1)} %collective-permute-done.4.theirs.z_one, f32[48,128]{1,0:T(8,128)S(1)} %collective-permute-done.6.rows, f32[128,6]{1,0:T(8,128)S(1)} %copy.11.lift, f32[5,128]{1,0:T(8,128)S(1)} %copy-done.1), custom_call_target="tpu_custom_call" | custom-call | flops 20000000000 | bytes 60000000 | tf_op jit(solution)/shard_map/solve/pallas_call | solution.py:451
  25.3 1.7 %collective-permute-start.7 = (f32[48,128]{1,0:T(8,128)S(1)}, f32[48,128]{1,0:T(8,128)S(1)}, u32[]{:S(2)}, u32[]{:S(2)}) collective-permute-start(f32[48,128]{1,0:T(8,128)S(1)} %solve.2.refs_0_), channel_id=1, source_target_pairs={{0,2},{1,3},{2,0},{3,1},{4,6},{5,7},{6,4},{7,5},{8,10},{9,11},{10,... | collective-permute-start | bytes 73736 | tf_op jit(solution)/shard_map/ppermute | solution.py:363
  27.0 1.6 %solve.3.after.solved_own = f32[48,128]{1,0:T(8,128)S(1)} custom-call(f32[528,128]{1,0:T(8,128)S(1)} %join.1.faces.mine, f32[528,128]{1,0:T(8,128)S(1)} %collective-permute-done.4.theirs.z_one, f32[48,128]{1,0:T(8,128)S(1)} %get-tuple-element.31.rows, f32[128,6]{1,0:T(8,128)S(1)} %copy.11.lift, f32[5,128]{1,0:T(8,128)S(1)} %copy-done.1, ...), custom_call_target="tpu_custom_call" | custom-call | flops 20000000000 | bytes 60000000 | tf_op jit(solution)/shard_map/solve/pallas_call | solution.py:451
  28.5 0.0 collective-permute-done.8.x_one
  28.5 0.0 collective-permute-done.9.x_two
  28.6 0.4 %stencil.1.partial = f32[5,4,32,256]{3,2,1,0:T(8,128)S(1)} custom-call(f32[5,4,32,256]{3,2,1,0:T(8,128)S(1)} %get-tuple-element.21.adjoint, f32[4,32,256]{2,1,0:T(8,128)S(1)} %get-tuple-element.22.viscosity, f32[5,4,32,256]{3,2,1,0:T(8,128)S(1)} %interior.1.base, f32[6,32,256]{2,1,0:T(8,128)S(1)} %collective-permute-done.8.x_one, ...), custom_call_target="tpu_custom_call" | custom-call | flops 20000000000 | bytes 60000000 | tf_op jit(solution)/shard_map/stencil/pallas_call | solution.py:464
  29.0 1.3 %collective-permute-done.7.returned = f32[48,128]{1,0:T(8,128)S(1)} collective-permute-done((f32[48,128]{1,0:T(8,128)S(1)}, f32[48,128]{1,0:T(8,128)S(1)}, u32[]{:S(2)}, u32[]{:S(2)}) %collective-permute-start.7) | collective-permute-done | bytes 24608 | tf_op jit(solution)/shard_map/ppermute | solution.py:363
  30.3 1.9 %scatter.1 = (f32[5,4,32,256]{3,2,1,0:T(8,128)}, f32[5,1024]{1,0:T(8,128)}) custom-call(f32[48,128]{1,0:T(8,128)S(1)} %solve.3.after.solved_own, f32[48,128]{1,0:T(8,128)S(1)} %collective-permute-done.7.returned, s32[1,1024]{1,0:T(1,128)S(1)} %get-tuple-element.23.cell, s32[1,1024]{1,0:T(1,128)S(1)} %get-tuple-element.24.patch, ...), custom_call_target="tpu_custom_call" | custom-call | tf_op jit(solution)/shard_map/scatter/pallas_call | solution.py:483
  (5 shorter events, 0.1 us)
Async XLA Ops:
  2.4 4.3 %collective-permute-start.3 = (f32[24,256]{1,0:T(8,128)S(1)}, f32[24,256]{1,0:T(8,128)S(1)}, u32[]{:S(2)}, u32[]{:S(2)}) collective-permute-start(f32[24,256]{1,0:T(8,128)S(1)} %get-tuple-element.25), channel_id=1, source_target_pairs={{0,16},{16,0},{32,48},{48,32},{1,17},{17,1},{33,49},{49,33},{2,18}... | collective-permute-start | bytes 73736 | tf_op jit(solution)/shard_map/ppermute | solution.py:363
  2.5 10.7 %collective-permute-start.2 = (f32[1,136,128]{2,1,0:T(8,128)S(1)}, f32[1,136,128]{2,1,0:T(8,128)S(1)}, u32[]{:S(2)}, u32[]{:S(2)}) collective-permute-start(f32[1,136,128]{2,1,0:T(8,128)S(1)} %get-tuple-element.20.first), channel_id=1, source_target_pairs={{0,12},{1,13},{2,14},{3,15},{4,8},{5,9},{6,10},{7,11},{8,4},{9,5},... | collective-permute-start | bytes 208904 | tf_op jit(solution)/shard_map/ppermute | solution.py:363
  5.6 7.6 %collective-permute-start.1 = (f32[1,136,128]{2,1,0:T(8,128)S(1)}, f32[1,136,128]{2,1,0:T(8,128)S(1)}, u32[]{:S(2)}, u32[]{:S(2)}) collective-permute-start(f32[1,136,128]{2,1,0:T(8,128)S(1)} %get-tuple-element.20.first), channel_id=1, source_target_pairs={{0,8},{1,9},{2,10},{3,11},{4,12},{5,13},{6,14},{7,15},{8,0},{9,1},... | collective-permute-start | bytes 208904 | tf_op jit(solution)/shard_map/ppermute | solution.py:363
  6.2 7.0 %collective-permute-start = (f32[1,136,128]{2,1,0:T(8,128)S(1)}, f32[1,136,128]{2,1,0:T(8,128)S(1)}, u32[]{:S(2)}, u32[]{:S(2)}) collective-permute-start(f32[1,136,128]{2,1,0:T(8,128)S(1)} %get-tuple-element.20.first), channel_id=1, source_target_pairs={{0,4},{1,5},{2,6},{3,7},{4,0},{5,1},{6,2},{7,3},{8,12},{9,13},{10,... | collective-permute-start | bytes 208904 | tf_op jit(solution)/shard_map/ppermute | solution.py:363
  8.2 7.8 %collective-permute-start.5 = (f32[24,256]{1,0:T(8,128)S(1)}, f32[24,256]{1,0:T(8,128)S(1)}, u32[]{:S(2)}, u32[]{:S(2)}) collective-permute-start(f32[24,256]{1,0:T(8,128)S(1)} %get-tuple-element.33), channel_id=1, source_target_pairs={{0,48},{16,32},{32,16},{48,0},{1,49},{17,33},{33,17},{49,1},{2,50}... | collective-permute-start | bytes 73736 | tf_op jit(solution)/shard_map/ppermute | solution.py:363
  13.3 1.1 %copy-start = (f32[5,5]{1,0:T(8,128)S(1)}, f32[5,5]{1,0:T(8,128)}, u32[]{:S(2)}) copy-start(f32[5,5]{1,0:T(8,128)} %jacobian.1) | copy-start | bytes 304
  13.3 10.4 %collective-permute-start.4 = (f32[528,128]{1,0:T(8,128)S(1)}, f32[528,128]{1,0:T(8,128)S(1)}, u32[]{:S(2)}, u32[]{:S(2)}) collective-permute-start(f32[528,128]{1,0:T(8,128)S(1)} %join.1.faces.mine), channel_id=1, source_target_pairs={{0,1},{1,0},{2,3},{3,2},{4,5},{5,4},{6,7},{7,6},{8,9},{9,8},{10,11... | collective-permute-start | bytes 811016 | tf_op jit(solution)/shard_map/ppermute | solution.py:363
  16.1 3.1 %copy-start.2 = (f32[128,6]{0,1:T(8,128)S(1)}, f32[128,6]{0,1:T(8,128)}, u32[]{:S(2)}) copy-start(f32[128,6]{0,1:T(8,128)} %param.14) | copy-start | bytes 9220
  16.1 7.6 %copy-start.1 = (f32[5,128]{1,0:T(8,128)S(1)}, f32[5,128]{1,0:T(8,128)}, u32[]{:S(2)}) copy-start(f32[5,128]{1,0:T(8,128)} %readout.3) | copy-start | bytes 7684
  16.1 5.6 %collective-permute-start.6 = (f32[48,128]{1,0:T(8,128)S(1)}, f32[48,128]{1,0:T(8,128)S(1)}, u32[]{:S(2)}, u32[]{:S(2)}) collective-permute-start(f32[48,128]{1,0:T(8,128)S(1)} %get-tuple-element.34), channel_id=1, source_target_pairs={{0,2},{1,3},{2,0},{3,1},{4,6},{5,7},{6,4},{7,5},{8,10},{9,11},{10,... | collective-permute-start | bytes 73736 | tf_op jit(solution)/shard_map/ppermute | solution.py:363
  19.3 9.2 %collective-permute-start.8 = (f32[6,32,256]{2,1,0:T(8,128)S(1)}, f32[6,32,256]{2,1,0:T(8,128)S(1)}, u32[]{:S(2)}, u32[]{:S(2)}) collective-permute-start(f32[6,32,256]{2,1,0:T(8,128)S(1)} %get-tuple-element.36), channel_id=1, source_target_pairs={{0,64},{64,0},{128,192},{192,128},{1,65},{65,1},{129,193},{193,129... | collective-permute-start | bytes 589832 | tf_op jit(solution)/shard_map/ppermute | solution.py:363
  20.6 7.9 %collective-permute-start.9 = (f32[6,32,256]{2,1,0:T(8,128)S(1)}, f32[6,32,256]{2,1,0:T(8,128)S(1)}, u32[]{:S(2)}, u32[]{:S(2)}) collective-permute-start(f32[6,32,256]{2,1,0:T(8,128)S(1)} %get-tuple-element.37), channel_id=1, source_target_pairs={{0,192},{64,128},{128,64},{192,0},{1,193},{65,129},{129,65},{193,1... | collective-permute-start | bytes 589832 | tf_op jit(solution)/shard_map/ppermute | solution.py:363
  25.3 5.0 %collective-permute-start.7 = (f32[48,128]{1,0:T(8,128)S(1)}, f32[48,128]{1,0:T(8,128)S(1)}, u32[]{:S(2)}, u32[]{:S(2)}) collective-permute-start(f32[48,128]{1,0:T(8,128)S(1)} %solve.2.refs_0_), channel_id=1, source_target_pairs={{0,2},{1,3},{2,0},{3,1},{4,6},{5,7},{6,4},{7,5},{8,10},{9,11},{10,... | collective-permute-start | bytes 73736 | tf_op jit(solution)/shard_map/ppermute | solution.py:363
